TPU v7x, 32 devices: a whole 2x2x4 slice. The times are simulated.
32 devices in a mesh: dp: 4 (over z), row: 4 (over y, core), col: 2 (over x).
Axes of the slice: x: 2, y: 2, z: 4, core: 2. Of those that a mesh axis runs over, the one named last changes fastest.
Arguments:
- layer_input: bfloat16 [8192, 2048], P(('dp', 'col'), 'row'), may hold values from -6 to 6
- lengths: int32 [16, 4], replicated, may hold values from 1 to 256, 512 in all within a row
- deal_table: int32 [4, 4], replicated, may hold values from 0 to 3, each once within a row
- ln1_gain: float32 [2048], P('row'), may hold values from 0.5 to 1.5
- ln1_bias: float32 [2048], P('row'), may hold values from -1.5 to 1.5
- qkv_weight: bfloat16 [2048, 6144], P('row', 'col'), may hold values from -1 to 1
- qkv_bias: float32 [6144], P('col'), may hold values from -1.5 to 1.5
- dense_weight: bfloat16 [2048, 2048], P('col', 'row'), may hold values from -1 to 1
- dense_bias: float32 [2048], P('row'), may hold values from -1.5 to 1.5
- ln2_gain: float32 [2048], P('row'), may hold values from 0.5 to 1.5
- ln2_bias: float32 [2048], P('row'), may hold values from -1.5 to 1.5
- fc1_weight: bfloat16 [2048, 8192], P('row', 'col'), may hold values from -1 to 1
- fc1_bias: float32 [8192], P('col'), may hold values from -1.5 to 1.5
- fc2_weight: bfloat16 [8192, 2048], P('col', 'row'), may hold values from -0.0625 to 0.0625
- fc2_bias: float32 [2048], P('row'), may hold values from -1.5 to 1.5
- cotangent: bfloat16 [8192, 2048], P(('dp', 'col'), 'row'), may hold values from -6 to 6
Outputs:
- output: bfloat16 [8192, 2048], P(('dp', 'col'), 'row')
- input_grad: float32 [8192, 2048], P(('dp', 'col'), 'row')
- ln1_gain_grad: float32 [2048], P('row')
- ln1_bias_grad: float32 [2048], P('row')
- qkv_weight_grad: float32 [2048, 6144], P('row', 'col')
- qkv_bias_grad: float32 [6144], P('col')
- dense_weight_grad: float32 [2048, 2048], P('col', 'row')
- dense_bias_grad: float32 [2048], P('row')
- ln2_gain_grad: float32 [2048], P('row')
- ln2_bias_grad: float32 [2048], P('row')
- fc1_weight_grad: float32 [2048, 8192], P('row', 'col')
- fc1_bias_grad: float32 [8192], P('col')
- fc2_weight_grad: float32 [8192, 2048], P('col', 'row')
- fc2_bias_grad: float32 [2048], P('row')
Inputs may be any that keep to these rules, and one draw needn't show every extreme that they name: Row i holds, in token order, the lengths of the 4 sequences packed in given slab i; each row sums to 512. `deal_table`: each row is a permutation of the 4 groups.
All inputs are finite; a program needn't handle non-finite values.
Results may differ from a plain program's by a relative error of at most 0.0091.
Values may be sent and summed in bfloat16 or wider, within the bound.
A program may use at most 384 MiB of HBM per device.

v0:
```python
from functools import partial
import math

import jax
import jax.numpy as jnp
from jax import lax
from jax.sharding import PartitionSpec as P

D = 2048
HD = 128
ROT = 32
QBLK = 512


norm_epsilon = 1e-05
masked_score = -1000000000.0


def rotary_tables(positions):
    frequency = 1.0 / 10000.0 ** (jnp.arange(0, ROT, 2, dtype=jnp.float32) / ROT)
    angles = positions.astype(jnp.float32)[:, None] * frequency[None, :]
    angles = jnp.concatenate([angles, angles], axis=1)
    return (jnp.cos(angles), jnp.sin(angles))


def rotate(values, cos_table, sin_table):
    half_rot = ROT // 2
    rotated = values[..., :ROT]
    turned = jnp.concatenate([-rotated[..., half_rot:], rotated[..., :half_rot]], axis=-1)
    rotated = rotated * cos_table[:, None, :] + turned * sin_table[:, None, :]
    return jnp.concatenate([rotated, values[..., ROT:]], axis=-1)


def segment_layout(seq_lengths, length):
    seq_ends = jnp.cumsum(seq_lengths)
    token_place = jnp.arange(length, dtype=jnp.int32)
    sequence_ids = jnp.sum((token_place[:, None] >= seq_ends[None, :]).astype(jnp.int32), axis=1)
    starts = seq_ends - seq_lengths
    seq_hits = sequence_ids[:, None] == jnp.arange(seq_lengths.shape[0], dtype=jnp.int32)[None, :]
    seq_begin = jnp.sum(jnp.where(seq_hits, starts[None, :], 0), axis=1)
    return (sequence_ids, token_place - seq_begin)


def contract_rows(left_side, right_side):
    return lax.dot_general(
        left_side, right_side, (((0,), (0,)), ((), ())), preferred_element_type=jnp.float32
    )


def contract_cols(left_side, right_side):
    return lax.dot_general(
        left_side, right_side, (((1,), (1,)), ((), ())), preferred_element_type=jnp.float32
    )


def pick_rows(pooled, chosen):
    row_hits = chosen[None, :] == jnp.arange(pooled.shape[0], dtype=jnp.int32)[:, None]
    return jnp.sum(jnp.where(row_hits[:, :, None], pooled.astype(jnp.float32), 0.0), axis=0)


def local(
    layer_input,
    lengths,
    deal_table,
    ln1_gain,
    ln1_bias,
    qkv_weight,
    qkv_bias,
    dense_weight,
    dense_bias,
    ln2_gain,
    ln2_bias,
    fc1_weight,
    fc1_bias,
    fc2_weight,
    fc2_bias,
    cotangent,
):
    dp_count = lax.axis_size("dp")
    row_count = lax.axis_size("row")
    col_count = lax.axis_size("col")
    group_id = lax.axis_index("dp")
    row_id = lax.axis_index("row")
    col_id = lax.axis_index("col")
    own_rows, own_feats = layer_input.shape
    group_rows = own_rows * col_count
    slab_rows = group_rows // row_count
    qkv_cols = qkv_weight.shape[1]
    attn_cols = dense_weight.shape[0]
    heads_here = qkv_cols // (3 * HD)
    score_scale = 1.0 / math.sqrt(HD)
    local_slab = (col_id * own_rows + jnp.arange(own_rows, dtype=jnp.int32)) // slab_rows
    slab_hits = local_slab[:, None] == jnp.arange(row_count, dtype=jnp.int32)[None, :]
    deal_here = lax.dynamic_index_in_dim(deal_table, group_id, 1, keepdims=False)
    source = jnp.sum(jnp.where(slab_hits, deal_here[None, :], 0), axis=1)
    pooled = lax.all_gather(layer_input, "dp", axis=0, tiled=True).reshape(
        dp_count, own_rows, own_feats
    )
    mine_rows = pick_rows(pooled, source).astype(jnp.bfloat16)
    input_all = lax.all_gather(mine_rows, "col", axis=0, tiled=True)
    input_wide = input_all.astype(jnp.float32)
    row_stats = lax.psum(
        (jnp.sum(input_wide, axis=1), jnp.sum(input_wide * input_wide, axis=1)), "row"
    )
    row_mean = row_stats[0] / D
    inv_std = lax.rsqrt(row_stats[1] / D - row_mean * row_mean + norm_epsilon)
    normed = (input_wide - row_mean[:, None]) * inv_std[:, None]
    own_start = col_id * own_rows
    normed_own = lax.dynamic_slice_in_dim(normed, own_start, own_rows, 0)
    inv_std_own = lax.dynamic_slice_in_dim(inv_std, own_start, own_rows, 0)
    ln1_all = (normed * ln1_gain + ln1_bias).astype(jnp.bfloat16)
    ln2_all = (normed * ln2_gain + ln2_bias).astype(jnp.bfloat16)
    part_one = ln1_all
    part_two = ln2_all
    first_sums = lax.psum_scatter(
        jnp.concatenate(
            [
                jnp.dot(part_one, qkv_weight, preferred_element_type=jnp.float32),
                jnp.dot(part_two, fc1_weight, preferred_element_type=jnp.float32),
            ],
            axis=1,
        ),
        "row",
        scatter_dimension=0,
        tiled=True,
    )
    qkv_out = first_sums[:, :qkv_cols] + qkv_bias
    hidden = first_sums[:, qkv_cols:] + fc1_bias
    slab_source = (
        lax.dynamic_index_in_dim(deal_here, row_id, 0, keepdims=False) * row_count + row_id
    )
    seq_lengths = lax.dynamic_index_in_dim(lengths, slab_source, 0, keepdims=False)
    sequence_ids, positions = segment_layout(seq_lengths, slab_rows)
    token_place = jnp.arange(slab_rows, dtype=jnp.int32)
    cos_table, sin_table = rotary_tables(positions)
    packed = qkv_out.reshape(slab_rows, heads_here, 3, HD)
    query_pre = packed[:, :, 0]
    key_pre = packed[:, :, 1]
    queries = rotate(query_pre, cos_table, sin_table).astype(jnp.bfloat16)
    keys_rot = rotate(key_pre, cos_table, sin_table).astype(jnp.bfloat16)
    values = packed[:, :, 2].astype(jnp.bfloat16)

    def block_scores(block_id):
        first_row = block_id * QBLK
        last_row = first_row + QBLK
        allowed = (sequence_ids[first_row:last_row, None] == sequence_ids[None, :last_row]) & (
            token_place[None, :last_row] <= token_place[first_row:last_row, None]
        )
        scores = (
            jnp.einsum("qhd,khd->hqk", queries, keys_rot, preferred_element_type=jnp.float32)
            * score_scale
        )
        return jnp.where(allowed[None], scores, masked_score)

    block_id = 0
    last_row = (block_id + 1) * QBLK
    scores = block_scores(block_id)
    row_top = jnp.max(scores, axis=-1, keepdims=True)
    exp_total = jnp.sum(jnp.exp(scores - row_top), axis=-1, keepdims=True)
    log_total = row_top + jnp.log(exp_total)
    probs_low = jnp.exp(scores - log_total).astype(jnp.bfloat16)
    mixtures = jnp.einsum("hqk,khd->qhd", probs_low, values, preferred_element_type=jnp.float32)
    log_totals = [log_total]
    attn_out = mixtures.reshape(slab_rows, attn_cols).astype(jnp.bfloat16)
    activated = jax.nn.gelu(hidden, approximate=False).astype(jnp.bfloat16)
    attn_all, act_all = (
        lax.all_gather(attn_out, "row", axis=0, tiled=True),
        lax.all_gather(activated, "row", axis=0, tiled=True),
    )
    part_one = attn_all
    part_two = act_all
    branch_sum = lax.psum_scatter(
        jnp.dot(part_one, dense_weight, preferred_element_type=jnp.float32)
        + jnp.dot(part_two, fc2_weight, preferred_element_type=jnp.float32),
        "col",
        scatter_dimension=0,
        tiled=True,
    )
    output = (mine_rows.astype(jnp.float32) + branch_sum + dense_bias + fc2_bias).astype(
        jnp.bfloat16
    )
    grad_all = lax.all_gather(cotangent, "col", axis=0, tiled=True)
    dense_grad = contract_rows(attn_all, grad_all)
    fc2_grad = contract_rows(act_all, grad_all)
    out_bias_grad = jnp.sum(grad_all, axis=0, dtype=jnp.float32)
    grad_block = grad_all
    grad_second = lax.psum_scatter(
        jnp.concatenate(
            [contract_cols(grad_block, dense_weight), contract_cols(grad_block, fc2_weight)], axis=1
        ),
        "row",
        scatter_dimension=0,
        tiled=True,
    )
    grad_mix = grad_second[:, :attn_cols].astype(jnp.bfloat16).reshape(slab_rows, heads_here, HD)
    gelu_back = jax.vjp(partial(jax.nn.gelu, approximate=False), hidden)[1]
    grad_hidden = gelu_back(grad_second[:, attn_cols:])[0]
    grad_key = jnp.zeros((slab_rows, heads_here, HD), jnp.float32)
    grad_value = jnp.zeros((slab_rows, heads_here, HD), jnp.float32)
    block_id = 0
    first_row = block_id * QBLK
    last_row = first_row + QBLK
    probs_full = jnp.exp(block_scores(block_id) - log_totals[block_id])
    probs_low = probs_full.astype(jnp.bfloat16)
    grad_block = grad_mix
    grad_value = grad_value.at[:last_row].add(
        jnp.einsum("hqk,qhd->khd", probs_low, grad_block, preferred_element_type=jnp.float32)
    )
    grad_probs = jnp.einsum("qhd,khd->hqk", grad_block, values, preferred_element_type=jnp.float32)
    centre = jnp.sum(probs_full * grad_probs, axis=-1, keepdims=True)
    grad_scores = (probs_full * (grad_probs - centre)).astype(jnp.bfloat16)
    grad_queries = (
        jnp.einsum("hqk,khd->qhd", grad_scores, keys_rot, preferred_element_type=jnp.float32)
        * score_scale
    )
    grad_key = grad_key.at[:last_row].add(
        jnp.einsum("hqk,qhd->khd", grad_scores, queries, preferred_element_type=jnp.float32)
        * score_scale
    )
    turn_back = jax.vjp(lambda values_in: rotate(values_in, cos_table, sin_table), query_pre)[1]
    grad_query_pre = turn_back(grad_queries)[0]
    grad_key_pre = turn_back(grad_key)[0]
    grad_qkv = jnp.stack([grad_query_pre, grad_key_pre, grad_value], axis=2).reshape(
        slab_rows, qkv_cols
    )
    grad_first = jnp.concatenate([grad_qkv, grad_hidden], axis=1).astype(jnp.bfloat16)
    grad_first_all = lax.all_gather(grad_first, "row", axis=0, tiled=True)
    grad_qkv_all = grad_first_all[:, :qkv_cols]
    grad_hidden_all = grad_first_all[:, qkv_cols:]
    qkv_weight_grad = contract_rows(ln1_all, grad_qkv_all)
    qkv_bias_grad = jnp.sum(grad_qkv_all, axis=0, dtype=jnp.float32)
    fc1_weight_grad = contract_rows(ln2_all, grad_hidden_all)
    fc1_bias_grad = jnp.sum(grad_hidden_all, axis=0, dtype=jnp.float32)
    grad_block = grad_first_all
    summed = lax.psum_scatter(
        jnp.concatenate(
            [
                contract_cols(grad_block[:, :qkv_cols], qkv_weight),
                contract_cols(grad_block[:, qkv_cols:], fc1_weight),
            ],
            axis=1,
        ),
        "col",
        scatter_dimension=0,
        tiled=True,
    )
    grad_ln_one = summed[:, :own_feats]
    grad_ln_two = summed[:, own_feats:]
    gain_terms = (
        jnp.sum(grad_ln_one * normed_own, axis=0),
        jnp.sum(grad_ln_one, axis=0),
        jnp.sum(grad_ln_two * normed_own, axis=0),
        jnp.sum(grad_ln_two, axis=0),
    )
    grad_normed = grad_ln_one * ln1_gain + grad_ln_two * ln2_gain
    row_sums = lax.psum(
        (jnp.sum(grad_normed, axis=1), jnp.sum(grad_normed * normed_own, axis=1)), "row"
    )
    grad_dealt = cotangent.astype(jnp.float32) + inv_std_own[:, None] * (
        grad_normed - row_sums[0][:, None] / D - normed_own * row_sums[1][:, None] / D
    )
    gain_sums = lax.psum(
        (gain_terms[0], gain_terms[1], gain_terms[2], gain_terms[3]), ("dp", "col")
    )
    weights_summed = lax.psum(
        (
            qkv_weight_grad,
            qkv_bias_grad,
            dense_grad,
            fc1_weight_grad,
            fc1_bias_grad,
            fc2_grad,
            out_bias_grad,
        ),
        "dp",
    )
    pool_back = lax.all_gather(grad_dealt, "dp", axis=0, tiled=True).reshape(
        dp_count, own_rows, own_feats
    )
    back_here = jnp.sum(
        jnp.where(deal_table == group_id, jnp.arange(dp_count, dtype=jnp.int32)[None, :], 0), axis=1
    )
    target = jnp.sum(jnp.where(slab_hits, back_here[None, :], 0), axis=1)
    input_grad = pick_rows(pool_back, target)
    return (
        output,
        input_grad,
        gain_sums[0],
        gain_sums[1],
        weights_summed[0],
        weights_summed[1],
        weights_summed[2],
        weights_summed[6],
        gain_sums[2],
        gain_sums[3],
        weights_summed[3],
        weights_summed[4],
        weights_summed[5],
        weights_summed[6],
    )


def solution(mesh):
    placed = (
        P(("dp", "col"), "row"),
        P(),
        P(),
        P("row"),
        P("row"),
        P("row", "col"),
        P("col"),
        P("col", "row"),
        P("row"),
        P("row"),
        P("row"),
        P("row", "col"),
        P("col"),
        P("col", "row"),
        P("row"),
        P(("dp", "col"), "row"),
    )
    return jax.shard_map(
        local,
        mesh=mesh,
        in_specs=placed,
        out_specs=(
            P(("dp", "col"), "row"),
            P(("dp", "col"), "row"),
            P("row"),
            P("row"),
            P("row", "col"),
            P("col"),
            P("col", "row"),
            P("row"),
            P("row"),
            P("row"),
            P("row", "col"),
            P("col"),
            P("col", "row"),
            P("row"),
        ),
        check_vma=False,
    )
```

profile of v0, /device:TPU:0, one launch (start us, length us, event | category | flops | bytes accessed | tf_op | source)
XLA Modules:
  0.0 2455.7 jit_solution(17101282455384753450)
XLA Ops:
  11.1 34.3 %all-gather.16.cloned.1.call-done = bf16[2048,512]{1,0:T(8,128)(2,1)} async-done(((bf16[1024,512]{1,0:T(8,128)(2,1)}), bf16[2048,512]{1,0:T(8,128)(2,1)}) %all-gather.16.cloned.1.call-update) | async-done | bytes 2097168 | tf_op jit(solution)/shard_map/all_gather | solution.py:182
  45.4 7.8 fusion.54
  53.2 17.1 fusion.55
  70.3 57.5 %all-gather.8.cloned.1.call-done = bf16[4096,512]{1,0:T(8,128)(2,1)} async-done(((bf16[1024,512]{1,0:T(8,128)(2,1)}), bf16[4096,512]{1,0:T(8,128)(2,1)}) %all-gather.8.cloned.1.call-update) | async-done | bytes 4194320 | tf_op jit(solution)/shard_map/all_gather | solution.py:96
  131.8 28.8 %pad_maximum_fusion.1 = f32[2048,5120]{1,0:T(8,128)} fusion(f32[2048,4096]{1,0:T(8,128)} %fusion.55, f32[2048,1024]{1,0:T(8,128)} %fusion.54), kind=kLoop, calls=%fused_computation.1 | loop fusion | flops 10485760 | bytes 83886080 | tf_op jit(solution)/shard_map/concatenate | solution.py:188
  165.8 11.6 all-reduce.10
  177.5 20.5 fusion.28
  198.0 21.4 fusion.29
  219.5 39.4 %pad_maximum_fusion = f32[2048,7168]{1,0:T(8,128)} fusion(f32[2048,4096]{1,0:T(8,128)} %fusion.29, f32[2048,3072]{1,0:T(8,128)} %fusion.28), kind=kLoop, calls=%fused_computation | loop fusion | flops 14680064 | bytes 117440512 | tf_op jit(solution)/shard_map/concatenate | solution.py:116
  263.5 191.3 %reduce-scatter.9.cloned.1.call-done = f32[512,5120]{1,0:T(8,128)} async-done(((f32[2048,5120]{1,0:T(8,128)}), f32[512,5120]{1,0:T(8,128)}) %reduce-scatter.9.cloned.1.call-update) | async-done | bytes 10485776 | tf_op jit(solution)/shard_map/reduce_scatter | solution.py:187
  460.3 394.9 %reduce-scatter.5.cloned.1.call-done = f32[512,7168]{1,0:T(8,128)} async-done(((f32[2048,7168]{1,0:T(8,128)}), f32[512,7168]{1,0:T(8,128)}) %reduce-scatter.5.cloned.1.call-update) | async-done | bytes 14680080 | tf_op jit(solution)/shard_map/reduce_scatter | solution.py:115
  928.1 23.0 add_convert_fusion
  956.8 7.2 convolution_convert_fusion.1
  964.1 13.0 multiply_convert_fusion.1
  977.2 157.7 %all-gather.18.cloned.1.call-done = bf16[2048,7168]{1,0:T(8,128)(2,1)} async-done(((bf16[512,7168]{1,0:T(8,128)(2,1)}), bf16[2048,7168]{1,0:T(8,128)(2,1)}) %all-gather.18.cloned.1.call-update) | async-done | bytes 29360144 | tf_op jit(solution)/shard_map/all_gather | solution.py:227
  1134.9 9.7 fusion.6
  1144.6 14.0 fusion.2
  1163.3 8.2 all-gather.12.cloned.1.call-done
  1171.5 6.9 fusion.53
  1178.4 100.6 %all-gather.14.cloned.1.call-done = bf16[2048,4096]{1,0:T(8,128)(2,1)} async-done(((bf16[512,4096]{1,0:T(8,128)(2,1)}), bf16[2048,4096]{1,0:T(8,128)(2,1)}) %all-gather.14.cloned.1.call-update) | async-done | bytes 16777232 | tf_op jit(solution)/shard_map/all_gather | solution.py:168
  1279.1 15.5 convolution_add_fusion
  1298.8 82.4 %reduce-scatter.11.cloned.1.call-done = f32[1024,1024]{1,0:T(8,128)} async-done(((f32[2048,1024]{1,0:T(8,128)}), f32[1024,1024]{1,0:T(8,128)}) %reduce-scatter.11.cloned.1.call-update) | async-done | bytes 4194320 | tf_op jit(solution)/shard_map/reduce_scatter | solution.py:235
  1386.3 7.0 all-reduce.9
  1404.7 14.8 fusion.57
  1419.5 11.9 fusion.4
  1431.5 15.4 fusion
  1459.8 6.9 convert_reduce_fusion
  1466.7 25.0 %all-reduce.11 = (f32[3072]{0:T(1024)}, f32[512]{0:T(512)S(1)}, f32[4096]{0:T(1024)}) all-reduce(f32[3072]{0:T(1024)S(1)} %convert_reduce_fusion.1, f32[512]{0:T(512)S(1)} %convert_reduce_fusion.3, f32[4096]{0:T(1024)S(1)} %convert_reduce_fusion), channel_id=1, replica_groups=mesh['dp'=4,'row'=4,'col'=2] {'dp'}, use_global_device_ids=true, to_apply=%region_29.30 | all-reduce | flops 7680 | bytes 61440 | tf_op jit(solution)/shard_map/psum | solution.py:265
  1491.7 20.8 all-reduce.8
  1512.4 78.7 %all-gather.20.cloned.1.call-done = f32[4096,512]{1,0:T(8,128)} async-done(((f32[1024,512]{1,0:T(8,128)}), f32[4096,512]{1,0:T(8,128)}) %all-gather.20.cloned.1.call-update) | async-done | bytes 8388624 | tf_op jit(solution)/shard_map/all_gather | solution.py:277
  1596.4 833.8 %all-reduce.15.cloned.1.call-done = (f32[512,3072]{1,0:T(8,128)}, f32[1024,512]{1,0:T(8,128)}, f32[512,4096]{1,0:T(8,128)}, f32[4096,512]{1,0:T(8,128)}) async-done(((f32[512,3072]{1,0:T(8,128)}, f32[1024,512]{1,0:T(8,128)}, f32[512,4096]{1,0:T(8,128)}, f32[4096,512]{1,0:T(8,128)}), (f32[512,3072]{1,0:T(8,128)}, f32[1024,512]{1,0:T(8,128)}, f32[512,4096]{1,0:T(8,128)}, ...) | async-done | bytes 25165840 | tf_op jit(solution)/shard_map/psum | solution.py:265
  2430.9 6.9 copy.157
  (176 shorter events, 156.1 us)
Async XLA Ops:
  7.2 170.3 %copy-start = (bf16[512,3072]{1,0:T(8,128)(2,1)S(1)}, bf16[512,3072]{1,0:T(8,128)(2,1)}, u32[]{:S(2)}) copy-start(bf16[512,3072]{1,0:T(8,128)(2,1)} %param.29) | copy-start | bytes 9437188
  7.2 38.2 %all-gather.16.cloned.1.call-start = ((), (), s32[]{:S(2)}) async-start(), calls=%async_computation.10 | async-start | bytes 3145728 | tf_op jit(solution)/shard_map/all_gather | solution.py:182
  7.9 119.9 %all-gather.8.cloned.1.call-start = ((), (), s32[]{:S(2)}) async-start(), calls=%async_computation.4 | async-start | bytes 5242880 | tf_op jit(solution)/shard_map/all_gather | solution.py:96
  8.7 154.9 %all-gather.10.cloned.1.call-start = ((), (), s32[]{:S(2)}) async-start(), calls=%async_computation.5 | async-start | bytes 3145728 | tf_op jit(solution)/shard_map/all_gather | solution.py:100
  45.4 7.8 copy-start.14
  131.8 323.0 %reduce-scatter.9.cloned.1.call-start = ((), (), s32[]{:S(2)}) async-start(), calls=%async_computation.11 | async-start | bytes 52428800 | tf_op jit(solution)/shard_map/reduce_scatter | solution.py:187
  160.7 16.8 copy-start.29
  160.7 16.8 copy-start.34
  160.7 694.5 %reduce-scatter.5.cloned.1.call-start = ((), (), s32[]{:S(2)}) async-start(), calls=%async_computation.6 | async-start | bytes 73400320 | tf_op jit(solution)/shard_map/reduce_scatter | solution.py:115
  177.4 20.6 copy-start.19
  177.4 20.6 copy-start.21
  177.5 20.6 copy-start.5
  177.5 20.6 copy-start.31
  177.5 20.5 copy-start.33
  177.5 20.5 copy-start.36
  258.8 596.3 %copy-start.24 = (f32[3072]{0:T(1024)S(1)}, f32[3072]{0:T(1024)}, u32[]{:S(2)}) copy-start(f32[3072]{0:T(1024)} %param.30) | copy-start | bytes 36868
  258.9 876.0 %all-gather.18.cloned.1.call-start = ((), (), s32[]{:S(2)}) async-start(), calls=%async_computation.12 | async-start | bytes 36700160 | tf_op jit(solution)/shard_map/all_gather | solution.py:227
  889.6 15.0 copy-start.1
  928.1 23.1 copy-start.4
  956.7 214.8 %all-gather.12.cloned.1.call-start = ((), (), s32[]{:S(2)}) async-start(), calls=%async_computation.7 | async-start | bytes 5242880 | tf_op jit(solution)/shard_map/all_gather | solution.py:167
  964.1 315.0 %all-gather.14.cloned.1.call-start = ((), (), s32[]{:S(2)}) async-start(), calls=%async_computation.8 | async-start | bytes 20971520 | tf_op jit(solution)/shard_map/all_gather | solution.py:168
  977.1 404.1 %reduce-scatter.11.cloned.1.call-start = ((), (), s32[]{:S(2)}) async-start(), calls=%async_computation.13 | async-start | bytes 12582912 | tf_op jit(solution)/shard_map/reduce_scatter | solution.py:235
  1163.3 286.6 %reduce-scatter.7.cloned.1.call-start = ((), (), s32[]{:S(2)}) async-start(), calls=%async_computation.9 | async-start | bytes 6291456 | tf_op jit(solution)/shard_map/reduce_scatter | solution.py:172
  1294.6 86.6 %copy-start.30 = (f32[512]{0:T(512)S(1)}, f32[512]{0:T(512)}, u32[]{:S(2)}) copy-start(f32[512]{0:T(512)} %param.27) | copy-start | bytes 6148
  1294.6 86.6 %copy-start.32 = (f32[512]{0:T(512)S(1)}, f32[512]{0:T(512)}, u32[]{:S(2)}) copy-start(f32[512]{0:T(512)} %param.33) | copy-start | bytes 6148
  1294.6 296.5 %all-gather.20.cloned.1.call-start = ((), (), s32[]{:S(2)}) async-start(), calls=%async_computation.14 | async-start | bytes 10485760 | tf_op jit(solution)/shard_map/all_gather | solution.py:277
  1397.8 1032.5 %all-reduce.15.cloned.1.call-start = ((), (), s32[]{:S(2)}) async-start(), calls=%async_computation.15 | async-start | bytes 50331648 | tf_op jit(solution)/shard_map/psum | solution.py:265
  1404.7 14.8 copy-start.6
  1404.7 14.8 copy-start.35
  1419.5 11.9 copy-start.37
  1491.7 938.6 %copy-start.28 = (f32[512]{0:T(512)}, f32[512]{0:T(512)S(1)}, u32[]{:S(2)}) copy-start(f32[512]{0:T(512)S(1)} %get-tuple-element.145) | copy-start | bytes 6148
  2430.8 8.6 copy-start.7
  (20 other events, 63.3 us)
Sparse Core Ops, SparseCore 0:
  9.6 35.7 all-gather.15
  47.0 80.7 all-gather.7
  131.9 31.6 all-gather.9
  166.0 288.7 reduce-scatter.8
  457.4 397.7 reduce-scatter.4
  956.9 177.9 all-gather.17
  1137.0 34.4 all-gather.11
  1173.1 105.9 all-gather.13
  1281.9 99.2 reduce-scatter.10
  1383.5 54.3 reduce-scatter.6
  1439.9 151.1 all-gather.19
  1595.0 835.2 all-reduce.14
where the time goes:
time: 2460 us
  waiting for transfers between devices  1940 us (79%)
  other arithmetic  187 us (8%)
  matrix products  183 us (7%)
  blocking collectives  64.3 us (3%)
  local copies, waits for them, and re-layouts  61 us (2%)
    psum x1, waiting for transfers between devices, local(): lax.psum((qkv_weight_grad, qkv_bias_grad, dense_grad, fc1_weight_grad, fc...  834 us
    reduce_scatter x1, waiting for transfers between devices, local(): lax.psum_scatter(jnp.concatenate([jnp.dot(part_one, qkv_weight, preferred...  395 us
    reduce_scatter x1, waiting for transfers between devices, local(): lax.psum_scatter(jnp.concatenate([contract_cols(grad_block, dense_weight)...  191 us
    all_gather x1, waiting for transfers between devices, local(): grad_first_all = lax.all_gather(grad_first, 'row', axis=0, tiled=True)  158 us
    all_gather x1, waiting for transfers between devices, local(): lax.all_gather(activated, 'row', axis=0, tiled=True)  101 us
    reduce_scatter x1, waiting for transfers between devices, local(): lax.psum_scatter(jnp.concatenate([contract_cols(grad_block[:, :qkv_cols],...  82.4 us
    all_gather x1, waiting for transfers between devices, local(): lax.all_gather(grad_dealt, 'dp', axis=0, tiled=True)  78.7 us
    all_gather x1, waiting for transfers between devices, local(): lax.all_gather(layer_input, 'dp', axis=0, tiled=True)  57.5 us
  transfers between devices with their start and end apart: 12, of which 11 were waited for; matrix products, arithmetic and copies ran while one was open for 12% of the time, Pallas kernels for 0%

commit v1 on v0

--- a/solution.py
+++ b/solution.py
@@ -4,12 +4,17 @@
 import jax
 import jax.numpy as jnp
 from jax import lax
+from jax.experimental import pallas as pl
+from jax.experimental.pallas import tpu as pltpu
 from jax.sharding import PartitionSpec as P
 
 D = 2048
 HD = 128
 ROT = 32
 QBLK = 512
+CHUNK = 256
+BF16 = jnp.bfloat16
+F32 = jnp.float32
 
 
 norm_epsilon = 1e-05
@@ -300,7 +305,357 @@
     )
 
 
+def row_swap(block, offset):
+    return lax.ppermute(block, "row", [(i, i ^ offset) for i in range(4)])
+
+
+def col_swap(block):
+    return lax.ppermute(block, "col", [(0, 1), (1, 0)])
+
+
+def line_route(item, sources):
+    plane = lax.axis_index("dp")
+    from_below = lax.ppermute(item, "dp", [(0, 1), (1, 2)])
+    from_above = lax.ppermute(item, "dp", [(3, 2), (2, 1)])
+    far = lax.ppermute(jnp.where(plane == 1, from_below, from_above), "dp", [(1, 2), (2, 1)])
+    beside = jnp.where(plane == 1, from_above, from_below)
+    edge_wants = jnp.where(plane == 1, sources[:, 0], sources[:, 3])[:, None, None]
+    outward = jnp.where(edge_wants == plane, item, jnp.where(edge_wants == 3 - plane, beside, far))
+    at_edge = lax.ppermute(outward, "dp", [(1, 0), (2, 3)])
+    wants = lax.dynamic_index_in_dim(sources, plane, 1, keepdims=True)[:, :, None]
+    near = jnp.where(wants == 3 - plane, beside, far)
+    inner = jnp.where((wants == 0) & (plane == 1), from_below, near)
+    inner = jnp.where((wants == 3) & (plane == 2), from_above, inner)
+    moved = jnp.where((plane == 0) | (plane == 3), at_edge, inner)
+    return jnp.where(wants == plane, item, moved)
+
+
+def line_sum(block):
+    plane = lax.axis_index("dp")
+    arrived = lax.ppermute(block, "dp", [(0, 1), (3, 2)])
+    half = (block.astype(F32) + arrived.astype(F32)).astype(BF16)
+    other = lax.ppermute(half, "dp", [(1, 2), (2, 1)])
+    full = (half.astype(F32) + other.astype(F32)).astype(BF16)
+    edge = lax.ppermute(full, "dp", [(1, 0), (2, 3)])
+    return jnp.where((plane == 0) | (plane == 3), edge, full)
+
+
+def attention_body(qkv_ref, back_ref, cos_ref, low_ref, high_ref, begin_ref, attn_ref, grad_ref):
+    scale = 1.0 / math.sqrt(HD)
+    cos, low, high = cos_ref[...], low_ref[...], high_ref[...]
+
+    def turn(values):
+        return values * cos + pltpu.roll(values, HD - 16, 1) * low + pltpu.roll(values, 16, 1) * high
+
+    def turn_back(values):
+        return (
+            values * cos
+            + pltpu.roll(values * high, HD - 16, 1)
+            + pltpu.roll(values * low, 16, 1)
+        )
+
+    def product(left, right, dims):
+        return lax.dot_general(left, right, (dims, ((), ())), preferred_element_type=F32)
+
+    query = turn(qkv_ref[:, :HD]).astype(BF16)
+    key = turn(qkv_ref[:, HD : 2 * HD]).astype(BF16)
+    value = qkv_ref[:, 2 * HD :].astype(BF16)
+    back = back_ref[...]
+    rows = query.shape[0]
+    scores = product(query, key, ((1,), (1,))) * scale
+    at = lax.broadcasted_iota(jnp.int32, (rows, rows), 0)
+    of = lax.broadcasted_iota(jnp.int32, (rows, rows), 1)
+    allowed = (of <= at) & (of >= begin_ref[:, :1])
+    scores = jnp.where(allowed, scores, masked_score)
+    weight = jnp.exp(scores - jnp.max(scores, axis=1, keepdims=True))
+    probs = weight * (1.0 / jnp.sum(weight, axis=1, keepdims=True))
+    probs_low = probs.astype(BF16)
+    attn_ref[...] = product(probs_low, value, ((1,), (0,))).astype(BF16)
+    grad_probs = product(back, value, ((1,), (1,)))
+    centre = jnp.sum(probs * grad_probs, axis=1, keepdims=True)
+    grad_scores = (probs * (grad_probs - centre)).astype(BF16)
+    grad_query = product(grad_scores, key, ((1,), (0,))) * scale
+    grad_key = product(grad_scores, query, ((0,), (0,))) * scale
+    grad_ref[:, :HD] = turn_back(grad_query).astype(BF16)
+    grad_ref[:, HD : 2 * HD] = turn_back(grad_key).astype(BF16)
+    grad_ref[:, 2 * HD :] = product(probs_low, back, ((0,), (0,))).astype(BF16)
+
+
+def attention_both(qkv, back, cos, low, high, begin):
+    rows = qkv.shape[0]
+    heads = qkv.shape[1] // (3 * HD)
+    slab = 512
+    per_slab = pl.BlockSpec((slab, HD), lambda s, h: (s, 0))
+    return pl.pallas_call(
+        attention_body,
+        grid=(rows // slab, heads),
+        in_specs=[
+            pl.BlockSpec((slab, 3 * HD), lambda s, h: (s, h)),
+            pl.BlockSpec((slab, HD), lambda s, h: (s, h)),
+            per_slab,
+            per_slab,
+            per_slab,
+            per_slab,
+        ],
+        out_specs=[
+            pl.BlockSpec((slab, HD), lambda s, h: (s, h)),
+            pl.BlockSpec((slab, 3 * HD), lambda s, h: (s, h)),
+        ],
+        out_shape=[
+            jax.ShapeDtypeStruct((rows, heads * HD), BF16),
+            jax.ShapeDtypeStruct((rows, heads * 3 * HD), BF16),
+        ],
+        compiler_params=pltpu.CompilerParams(vmem_limit_bytes=40 * 1024 * 1024),
+        cost_estimate=pl.CostEstimate(
+            flops=14 * rows * slab * HD * heads,
+            bytes_accessed=rows * heads * HD * 24,
+            transcendentals=rows * slab * heads,
+        ),
+    )(qkv, back, cos, low, high, begin)
+
+
+def dealt_layer(
+    layer_input,
+    lengths,
+    deal_table,
+    ln1_gain,
+    ln1_bias,
+    qkv_weight,
+    qkv_bias,
+    dense_weight,
+    dense_bias,
+    ln2_gain,
+    ln2_bias,
+    fc1_weight,
+    fc1_bias,
+    fc2_weight,
+    fc2_bias,
+    cotangent,
+):
+    plane = lax.axis_index("dp")
+    row = lax.axis_index("row")
+    col = lax.axis_index("col")
+    own_rows, own_feats = layer_input.shape
+    rows = 2 * own_rows
+    slab = own_rows // 2
+    qkv_cols = qkv_weight.shape[1]
+    qkv_here = qkv_cols // 4
+    attn_here = dense_weight.shape[0] // 4
+    hidden_cols = fc1_weight.shape[1]
+    hidden_here = hidden_cols // 4
+
+    slab_ids = 2 * col + jnp.arange(2, dtype=jnp.int32)
+    deal_here = lax.dynamic_slice_in_dim(deal_table, 2 * col, 2, 0)
+    undeal_here = jnp.argmax(
+        deal_here[:, None, :] == jnp.arange(4, dtype=jnp.int32)[None, :, None], axis=2
+    ).astype(jnp.int32)
+
+    def plane_gather(own):
+        across = row_swap(own, 2)
+        halves = [[own, across], [col_swap(own), col_swap(across)]]
+        return [
+            [pair[0], row_swap(pair[0], 1), pair[1], row_swap(pair[1], 1)] for pair in halves
+        ]
+
+    def swap_rows(pieces):
+        return [pieces(0)] + [row_swap(pieces(j), j) for j in (1, 2, 3)]
+
+    x_parts = plane_gather(layer_input)
+    norms = jnp.stack([ln1_gain, ln1_bias, ln2_gain, ln2_bias])
+    norms = jnp.concatenate(swap_rows(lambda j: norms), axis=1)
+
+    cot_own = line_route(cotangent.reshape(2, slab, own_feats), undeal_here).reshape(
+        own_rows, own_feats
+    )
+    cot_parts = plane_gather(cot_own)
+
+    def first_slice(weight, width, at, size):
+        parts = swap_rows(
+            lambda j: lax.dynamic_slice_in_dim(weight, (row ^ j) * width + at, size, 1)
+        )
+        return jnp.concatenate(parts, axis=0)
+
+    def second_slice(weight, width, at, size):
+        parts = swap_rows(
+            lambda j: lax.dynamic_slice_in_dim(weight, (row ^ j) * width + at, size, 0)
+        )
+        return jnp.concatenate(parts, axis=1)
+
+    chunks = range(0, hidden_here, CHUNK)
+    fc1_parts = [first_slice(fc1_weight, hidden_here, at, CHUNK) for at in chunks]
+    fc2_parts = [second_slice(fc2_weight, hidden_here, at, CHUNK) for at in chunks]
+    qkv_here_weight = first_slice(qkv_weight, qkv_here, 0, qkv_here)
+    dense_here = second_slice(dense_weight, attn_here, 0, attn_here)
+
+    x_all = jnp.concatenate([jnp.concatenate(half, axis=1) for half in x_parts], axis=0)
+    wide = x_all.astype(F32)
+    mean = jnp.sum(wide, axis=1, keepdims=True) / D
+    inv_std = lax.rsqrt(jnp.sum(wide * wide, axis=1, keepdims=True) / D - mean * mean + norm_epsilon)
+    normed = (wide - mean) * inv_std
+    ln1_all = (normed * norms[0] + norms[1]).astype(BF16)
+    ln2_all = (normed * norms[2] + norms[3]).astype(BF16)
+    cot_all = jnp.concatenate([jnp.concatenate(half, axis=1) for half in cot_parts], axis=0)
+
+    qkv_bias_here = lax.dynamic_slice_in_dim(qkv_bias, row * qkv_here, qkv_here, 0)
+    fc1_bias_here = lax.dynamic_slice_in_dim(fc1_bias, row * hidden_here, hidden_here, 0)
+
+    qkv_grad = jnp.zeros((own_feats, qkv_cols), F32)
+    fc1_grad = jnp.zeros((own_feats, hidden_cols), F32)
+    dense_grad = jnp.zeros((dense_weight.shape[0], own_feats), F32)
+    fc2_grad = jnp.zeros((fc2_weight.shape[0], own_feats), F32)
+
+    def first_grad(total, grad, width, at):
+        size = grad.shape[1]
+        pieces = swap_rows(lambda j: grad[j * own_feats : (j + 1) * own_feats])
+        summed = line_sum(jnp.concatenate(pieces, axis=0)).astype(F32)
+        for j in range(4):
+            total = lax.dynamic_update_slice(
+                total,
+                summed[j * own_feats : (j + 1) * own_feats],
+                (0, (row ^ j) * width + at),
+            )
+        return total
+
+    def second_grad(total, grad, width, at):
+        size = grad.shape[0]
+        pieces = swap_rows(lambda j: grad[:, j * own_feats : (j + 1) * own_feats])
+        summed = line_sum(jnp.concatenate(pieces, axis=0)).astype(F32)
+        for j in range(4):
+            total = lax.dynamic_update_slice(
+                total, summed[j * size : (j + 1) * size], ((row ^ j) * width + at, 0)
+            )
+        return total
+
+    acts, hidden_grads, hidden_sums = [], [], []
+    gain2 = jnp.zeros((D,), F32)
+    for k, at in enumerate(chunks):
+        hidden = (
+            jnp.dot(ln2_all, fc1_parts[k], preferred_element_type=F32)
+            + fc1_bias_here[at : at + CHUNK]
+        )
+        act, gelu_back = jax.vjp(partial(jax.nn.gelu, approximate=False), hidden)
+        act = act.astype(BF16)
+        grad_act = contract_cols(cot_all, fc2_parts[k])
+        grad_hidden = gelu_back(grad_act)[0].astype(BF16)
+        acts.append(act)
+        hidden_grads.append(grad_hidden)
+        hidden_sums.append(jnp.sum(grad_hidden, axis=0, dtype=F32))
+        fc2_grad = second_grad(
+            fc2_grad, contract_rows(act, cot_all).astype(BF16), hidden_here, at
+        )
+        grad = contract_rows(ln2_all, grad_hidden)
+        gain2 += jnp.sum(grad * fc1_parts[k].astype(F32), axis=1)
+        fc1_grad = first_grad(fc1_grad, grad.astype(BF16), hidden_here, at)
+
+    qkv = jnp.dot(ln1_all, qkv_here_weight, preferred_element_type=F32) + qkv_bias_here
+    grad_mix = contract_cols(cot_all, dense_here).astype(BF16)
+    slab_order = jnp.concatenate([slab_ids, (slab_ids + 2) % 4])
+    lengths_here = jnp.take(lengths, plane * 4 + slab_order, axis=0)
+    positions = jnp.concatenate([segment_layout(lengths_here[s], slab)[1] for s in range(4)])
+    begins = jnp.tile(jnp.arange(slab, dtype=jnp.int32), 4) - positions
+    cos_table, sin_table = rotary_tables(positions)
+    lane = jnp.arange(HD)
+    cos_table = jnp.pad(cos_table, ((0, 0), (0, HD - ROT)), constant_values=1.0)
+    sin_table = jnp.pad(sin_table, ((0, 0), (0, HD - ROT)))
+    low_table = jnp.where(lane < ROT // 2, -sin_table, 0.0)
+    high_table = jnp.where(lane < ROT // 2, 0.0, sin_table)
+    attn, grad_qkv = attention_both(
+        qkv,
+        grad_mix,
+        cos_table,
+        low_table,
+        high_table,
+        jnp.broadcast_to(begins[:, None], (rows, HD)),
+    )
+    dense_grad = second_grad(dense_grad, contract_rows(attn, cot_all).astype(BF16), attn_here, 0)
+    gain1 = jnp.zeros((D,), F32)
+    for at in range(0, qkv_here, CHUNK):
+        grad = contract_rows(ln1_all, grad_qkv[:, at : at + CHUNK])
+        gain1 += jnp.sum(grad * qkv_here_weight[:, at : at + CHUNK].astype(F32), axis=1)
+        qkv_grad = first_grad(qkv_grad, grad.astype(BF16), qkv_here, at)
+    qkv_sum = jnp.sum(grad_qkv, axis=0, dtype=F32)
+    hidden_sum = jnp.concatenate(hidden_sums)
+
+    def plane_scatter(part):
+        blocks = [part[:, j * own_feats : (j + 1) * own_feats] for j in range(4)]
+        sent = [row_swap(blocks[j].astype(BF16), 1) for j in (1, 3)]
+        chip = [blocks[2 * j] + sent[j].astype(F32) for j in range(2)]
+        sent = [col_swap(chip[j][own_rows:].astype(BF16)) for j in range(2)]
+        half = [chip[j][:own_rows] + sent[j].astype(F32) for j in range(2)]
+        return half[0] + row_swap(half[1].astype(BF16), 2).astype(F32)
+
+    branch = plane_scatter(
+        jnp.dot(
+            jnp.concatenate([attn] + acts, axis=1),
+            jnp.concatenate([dense_here] + fc2_parts, axis=0),
+            preferred_element_type=F32,
+        )
+    )
+    output = (layer_input.astype(F32) + branch + dense_bias + fc2_bias).astype(BF16)
+    output = line_route(output.reshape(2, slab, own_feats), deal_here).reshape(own_rows, own_feats)
+
+    fc1_here = jnp.concatenate(fc1_parts, axis=1)
+    grad_hidden = jnp.concatenate(hidden_grads, axis=1)
+    grad_normed = plane_scatter(
+        contract_cols(grad_qkv, qkv_here_weight) * norms[0]
+        + contract_cols(grad_hidden, fc1_here) * norms[2]
+    )
+    normed_own = normed[:own_rows, :own_feats]
+    row_sums = lax.psum(
+        (jnp.sum(grad_normed, axis=1), jnp.sum(grad_normed * normed_own, axis=1)), "row"
+    )
+    input_grad = cot_own.astype(F32) + inv_std[:own_rows] * (
+        grad_normed - row_sums[0][:, None] / D - normed_own * row_sums[1][:, None] / D
+    )
+
+    bias1 = jnp.dot(qkv_here_weight.astype(F32), qkv_sum, precision="highest")
+    bias2 = jnp.dot(fc1_here.astype(F32), hidden_sum, precision="highest")
+    gain1 = (gain1 - norms[1] * bias1) / norms[0]
+    gain2 = (gain2 - norms[3] * bias2) / norms[2]
+    norm_sums = jnp.stack([gain1, bias1, gain2, bias2]).reshape(4, 4, own_feats)
+    norm_sums = jnp.stack(
+        [lax.dynamic_index_in_dim(norm_sums, row ^ j, 1, keepdims=False) for j in range(4)], axis=1
+    )
+    bias_here = jnp.sum(cotangent, axis=0, dtype=F32)
+    bias_sum = jnp.zeros((4, own_feats), F32).at[row].set(bias_here)
+    qkv_sums = jnp.zeros((2, 4, qkv_here), F32).at[col, row].set(qkv_sum)
+    hidden_sums = jnp.zeros((2, 4, hidden_here), F32).at[col, row].set(hidden_sum)
+    small = lax.psum(
+        jnp.concatenate(
+            [norm_sums.reshape(-1), bias_sum.reshape(-1), qkv_sums.reshape(-1), hidden_sums.reshape(-1)]
+        ),
+        ("dp", "row", "col"),
+    )
+    sizes = [4 * D, D, 2 * qkv_cols]
+    norm_sums, bias_sum, qkv_sums, hidden_sums = jnp.split(
+        small, [sizes[0], sizes[0] + sizes[1], sum(sizes)]
+    )
+    norm_sums = lax.dynamic_index_in_dim(norm_sums.reshape(4, 4, own_feats), row, 1, keepdims=False)
+    bias_sum = lax.dynamic_index_in_dim(bias_sum.reshape(4, own_feats), row, 0, keepdims=False)
+    qkv_bias_grad = lax.dynamic_index_in_dim(qkv_sums.reshape(2, qkv_cols), col, 0, keepdims=False)
+    fc1_bias_grad = lax.dynamic_index_in_dim(
+        hidden_sums.reshape(2, hidden_cols), col, 0, keepdims=False
+    )
+    return (
+        output,
+        input_grad,
+        norm_sums[0],
+        norm_sums[1],
+        qkv_grad,
+        qkv_bias_grad,
+        dense_grad,
+        bias_sum,
+        norm_sums[2],
+        norm_sums[3],
+        fc1_grad,
+        fc1_bias_grad,
+        fc2_grad,
+        bias_sum,
+    )
+
+
 def solution(mesh):
+    grid = tuple(mesh.shape[axis] for axis in ("dp", "row", "col"))
     placed = (
         P(("dp", "col"), "row"),
         P(),
@@ -320,7 +675,7 @@
         P(("dp", "col"), "row"),
     )
     return jax.shard_map(
-        local,
+        dealt_layer if grid == (4, 4, 2) else local,
         mesh=mesh,
         in_specs=placed,
         out_specs=(

time: 2460 us -> 1550 us (0.63)
  waiting for transfers between devices: 1940 us -> 910 us
  starting transfers between devices: 0.49 us -> 162 us
  blocking collectives: 64.3 us -> 5.77 us
  other arithmetic: 187 us -> 142 us
    ppermute x0 -> x137, waiting for transfers between devices: none -> 841 us  [the longest x12 378 us: line_sum(): edge = lax.ppermute(full, 'dp', [(1, 0), (2, 3)])]
    psum x1, waiting for transfers between devices: 834 us -> 69.4 us  [dealt_layer(): lax.psum(jnp.concatenate([norm_sums.reshape(-1), bias_sum.reshape(-1), qk...]
    reduce_scatter x4 -> x0, waiting for transfers between devices: 669 us -> none  [the longest x1 395 us: local(): lax.psum_scatter(jnp.concatenate([jnp.dot(part_one, qkv_weight, preferred...]
    all_gather x7 -> x0, waiting for transfers between devices: 440 us -> none  [the longest x1 158 us: local(): grad_first_all = lax.all_gather(grad_first, 'row', axis=0, tiled=True)]
    ppermute x0 -> x137, starting transfers between devices: none -> 162 us  [the longest x85 58.1 us: row_swap(): return lax.ppermute(block, 'row', [(i, i ^ offset) for i in range(4)])]
    psum x4 -> x1, blocking collectives: 64.3 us -> 5.77 us  [dealt_layer(): lax.psum((jnp.sum(grad_normed, axis=1), jnp.sum(grad_normed * normed_own,...]
    concatenate x4 -> x20, other arithmetic: 78.4 us -> 40 us  [the longest x1 33 us: dealt_layer(): jnp.concatenate([jnp.concatenate(half, axis=1) for half in cot_parts], ax...]
    dot_general x4 -> x7, matrix products: 48.6 us -> 78.3 us  [contract_cols(): lax.dot_general(left_side, right_side, (((1,), (1,)), ((), ())), preferre...]
  transfers between devices with their start and end apart: 12 -> 138, of which waited for: 11 -> 55; matrix products, arithmetic and copies ran while one was open for 12% -> 26% of each run, Pallas kernels for 0% -> 1%
where the time goes in v1:
time: 1550 us; the launch traced here: 1540 us
  waiting for transfers between devices  910 us (59%)
  matrix products  198 us (13%)
  starting transfers between devices  162 us (10%)
  other arithmetic  142 us (9%)
  local copies, waits for them, and re-layouts  84.7 us (5%)
  between operations  17.7 us (1%)
  Pallas kernels  17.1 us (1%)
    ppermute x12, waiting for transfers between devices, line_sum(): edge = lax.ppermute(full, 'dp', [(1, 0), (2, 3)])  378 us
    ppermute x85, waiting for transfers between devices, row_swap(): return lax.ppermute(block, 'row', [(i, i ^ offset) for i in range(4)])  184 us
    ppermute x12, waiting for transfers between devices, line_sum(): arrived = lax.ppermute(block, 'dp', [(0, 1), (3, 2)])  182 us
    dot_general x7, matrix products, contract_cols(): lax.dot_general(left_side, right_side, (((1,), (1,)), ((), ())), preferre...  78.3 us
    psum x1, waiting for transfers between devices, dealt_layer(): lax.psum(jnp.concatenate([norm_sums.reshape(-1), bias_sum.reshape(-1), qk...  69.4 us
    ppermute x8, waiting for transfers between devices, col_swap(): return lax.ppermute(block, 'col', [(0, 1), (1, 0)])  67.7 us
    ppermute x85, starting transfers between devices, row_swap(): return lax.ppermute(block, 'row', [(i, i ^ offset) for i in range(4)])  58.1 us
    ppermute x12, starting transfers between devices, line_sum(): arrived = lax.ppermute(block, 'dp', [(0, 1), (3, 2)])  48.5 us
  transfers between devices with their start and end apart: 138, of which 55 were waited for; matrix products, arithmetic and copies ran while one was open for 26% of the time, Pallas kernels for 1%

profile of v1, /device:TPU:0, one launch (start us, length us, event | category | flops | bytes accessed | tf_op | source)
XLA Modules:
  0.0 1537.9 jit_solution(14095564607512289386)
XLA Ops:
  58.1 22.1 %collective-permute-done.50 = bf16[256,512]{1,0:T(8,128)(2,1)S(1)} collective-permute-done((bf16[256,512]{1,0:T(8,128)(2,1)}, bf16[256,512]{1,0:T(8,128)(2,1)S(1)}, u32[]{:S(2)}, u32[]{:S(2)}) %collective-permute-start.50) | collective-permute-done | bytes 262176 | tf_op jit(solution)/shard_map/ppermute | solution.py:309
  121.4 12.8 collective-permute-done.11
  134.6 16.5 %collective-permute-done.12 = bf16[512,768]{1,0:T(8,128)(2,1)S(1)} collective-permute-done((bf16[512,768]{1,0:T(8,128)(2,1)S(1)}, bf16[512,768]{1,0:T(8,128)(2,1)S(1)}, u32[]{:S(2)}, u32[]{:S(2)}) %collective-permute-start.12) | collective-permute-done | bytes 786464 | tf_op jit(solution)/shard_map/ppermute | solution.py:309
  165.2 11.7 convert_reduce_fusion
  176.9 11.5 collective-permute-done.18
  189.9 12.2 fusion
  212.7 11.0 convolution_add_fusion.qkv_ref
  227.1 33.0 %maximum_maximum_fusion.1 = bf16[2048,2048]{0,1:T(8,128)(2,1)S(1)} fusion(bf16[1024,512]{0,1:T(8,128)(2,1)S(1)} %collective-permute-done.23, bf16[1024,512]{0,1:T(8,128)(2,1)S(1)} %collective-permute-done.22, bf16[1024,512]{0,1:T(8,128)(2,1)S(1)} %collective-permute-done.21, bf16[1024,512]{0,1:T(8,128)(2,1)S(1)} %collective-permute-done.20, ...), kind=kLoop, calls=%fused_computation.10 | loop fusion | flops 67108864 | bytes 16777216 | tf_op jit(solution)/shard_map/concatenate | solution.py:497
  264.0 17.1 %shard_map.263 = (bf16[2048,256]{1,0:T(8,128)(2,1)S(1)}, bf16[2048,768]{1,0:T(8,128)(2,1)S(1)}) custom-call(f32[2048,768]{1,0:T(8,128)} %convolution_add_fusion.qkv_ref, bf16[2048,256]{1,0:T(8,128)(2,1)S(1)} %convolution_convert_fusion.5.back_ref, f32[2048,128]{1,0:T(8,128)S(1)} %pad.16.cos_ref, f32[2048,128]{1,0:T(8,128)S(1)} %get-tuple-element.201.low_ref, ...), custom_call_target="tpu_custom_call" | custom-call | flops 3758096384 | bytes 12582912 | tf_op jit(solution)/shard_map/pallas_call | solution.py:389
  317.2 10.4 constant_dynamic-update-slice_fusion.2
  448.6 25.5 %fusion.102 = (bf16[2048,2048]{0,1:T(8,128)(2,1)}, f32[2048,2048]{0,1:T(8,128)}) fusion(f32[2048]{0:T(1024)S(1)} %bitcast.152, bf16[512,256]{1,0:T(8,128)(2,1)} %copy-done.150, bf16[512,256]{1,0:T(8,128)(2,1)} %copy-done.149, bf16[512,256]{1,0:T(8,128)(2,1)} %copy-done.148, bf16[512,256]{1,0:T(8,128)(2,1)} %get-tuple-element.169, ...), kind=kOutput, calls=%fused_computation.448 | convolution fusion | flops 8690597888 | bytes 50348032 | tf_op jit(solution)/shard_map/dot_general | solution.py:56
  479.0 18.0 %fusion.101 = (bf16[2048,2048]{1,0:T(8,128)(2,1)S(1)}, f32[2048,2048]{1,0:T(8,128)}) fusion(bf16[2048,1280]{1,0:T(8,128)(2,1)} %get-tuple-element.133, bf16[1280,2048]{1,0:T(8,128)(2,1)} %copy-done.115), kind=kOutput, calls=%fused_computation.447 | convolution fusion | flops 10741612544 | bytes 35651584 | tf_op jit(solution)/shard_map/dot_general | solution.py:588
  500.4 69.4 %all-reduce.5.cloned.1.call-done = f32[24576]{0:T(1024)} async-done(((f32[24576]{0:T(1024)}), f32[24576]{0:T(1024)}) %all-reduce.5.cloned.1.call-update) | async-done | bytes 98320 | tf_op jit(solution)/shard_map/psum | solution.py:623
  704.5 39.2 %collective-permute-done.98 = bf16[2048,256]{1,0:T(8,128)(2,1)S(1)} collective-permute-done((bf16[2048,256]{1,0:T(8,128)(2,1)S(1)}, bf16[2048,256]{1,0:T(8,128)(2,1)S(1)}, u32[]{:S(2)}, u32[]{:S(2)}) %collective-permute-start.98) | collective-permute-done | bytes 1048608 | tf_op jit(solution)/shard_map/ppermute | solution.py:335
  752.3 36.3 %collective-permute-done.92 = bf16[2048,256]{1,0:T(8,128)(2,1)S(1)} collective-permute-done((bf16[2048,256]{1,0:T(8,128)(2,1)S(1)}, bf16[2048,256]{1,0:T(8,128)(2,1)S(1)}, u32[]{:S(2)}, u32[]{:S(2)}) %collective-permute-start.92) | collective-permute-done | bytes 1048608 | tf_op jit(solution)/shard_map/ppermute | solution.py:335
  796.7 14.4 collective-permute-done.122
  815.5 18.0 %collective-permute-done.80 = bf16[2048,256]{1,0:T(8,128)(2,1)S(1)} collective-permute-done((bf16[2048,256]{1,0:T(8,128)(2,1)S(1)}, bf16[2048,256]{1,0:T(8,128)(2,1)S(1)}, u32[]{:S(2)}, u32[]{:S(2)}) %collective-permute-start.80) | collective-permute-done | bytes 1048608 | tf_op jit(solution)/shard_map/ppermute | solution.py:335
  840.6 15.4 %collective-permute-done.116 = bf16[1024,512]{1,0:T(8,128)(2,1)S(1)} collective-permute-done((bf16[1024,512]{1,0:T(8,128)(2,1)S(1)}, bf16[1024,512]{1,0:T(8,128)(2,1)S(1)}, u32[]{:S(2)}, u32[]{:S(2)}) %collective-permute-start.116) | collective-permute-done | bytes 1048608 | tf_op jit(solution)/shard_map/ppermute | solution.py:335
  861.7 16.8 %collective-permute-done.86 = bf16[1024,512]{1,0:T(8,128)(2,1)S(1)} collective-permute-done((bf16[1024,512]{1,0:T(8,128)(2,1)S(1)}, bf16[1024,512]{1,0:T(8,128)(2,1)S(1)}, u32[]{:S(2)}, u32[]{:S(2)}) %collective-permute-start.86) | collective-permute-done | bytes 1048608 | tf_op jit(solution)/shard_map/ppermute | solution.py:335
  878.5 22.5 %collective-permute-done.74 = bf16[2048,256]{1,0:T(8,128)(2,1)S(1)} collective-permute-done((bf16[2048,256]{1,0:T(8,128)(2,1)S(1)}, bf16[2048,256]{1,0:T(8,128)(2,1)S(1)}, u32[]{:S(2)}, u32[]{:S(2)}) %collective-permute-start.74) | collective-permute-done | bytes 1048608 | tf_op jit(solution)/shard_map/ppermute | solution.py:335
  903.6 19.2 %collective-permute-done.68 = bf16[2048,256]{1,0:T(8,128)(2,1)S(1)} collective-permute-done((bf16[2048,256]{1,0:T(8,128)(2,1)S(1)}, bf16[2048,256]{1,0:T(8,128)(2,1)S(1)}, u32[]{:S(2)}, u32[]{:S(2)}) %collective-permute-start.68) | collective-permute-done | bytes 1048608 | tf_op jit(solution)/shard_map/ppermute | solution.py:335
  974.0 14.7 collective-permute-done.63
  991.4 42.3 %collective-permute-done.54 = bf16[1024,512]{1,0:T(8,128)(2,1)S(1)} collective-permute-done((bf16[1024,512]{1,0:T(8,128)(2,1)S(1)}, bf16[1024,512]{1,0:T(8,128)(2,1)S(1)}, u32[]{:S(2)}, u32[]{:S(2)}) %collective-permute-start.54) | collective-permute-done | bytes 1048608 | tf_op jit(solution)/shard_map/ppermute | solution.py:313
  1035.4 164.3 %collective-permute-done.118 = bf16[1024,512]{1,0:T(8,128)(2,1)S(1)} collective-permute-done((bf16[1024,512]{1,0:T(8,128)(2,1)S(1)}, bf16[1024,512]{1,0:T(8,128)(2,1)S(1)}, u32[]{:S(2)}, u32[]{:S(2)}) %collective-permute-start.118) | collective-permute-done | bytes 1048608 | tf_op jit(solution)/shard_map/ppermute | solution.py:339
  1208.9 63.6 %collective-permute-done.124 = bf16[1024,512]{1,0:T(8,128)(2,1)S(1)} collective-permute-done((bf16[1024,512]{1,0:T(8,128)(2,1)S(1)}, bf16[1024,512]{1,0:T(8,128)(2,1)S(1)}, u32[]{:S(2)}, u32[]{:S(2)}) %collective-permute-start.124) | collective-permute-done | bytes 1048608 | tf_op jit(solution)/shard_map/ppermute | solution.py:339
  1286.1 54.6 %collective-permute-done.94 = bf16[2048,256]{1,0:T(8,128)(2,1)S(1)} collective-permute-done((bf16[2048,256]{1,0:T(8,128)(2,1)S(1)}, bf16[2048,256]{1,0:T(8,128)(2,1)S(1)}, u32[]{:S(2)}, u32[]{:S(2)}) %collective-permute-start.94) | collective-permute-done | bytes 1048608 | tf_op jit(solution)/shard_map/ppermute | solution.py:339
  1344.3 20.1 %collective-permute-done.100 = bf16[2048,256]{1,0:T(8,128)(2,1)S(1)} collective-permute-done((bf16[2048,256]{1,0:T(8,128)(2,1)S(1)}, bf16[2048,256]{1,0:T(8,128)(2,1)S(1)}, u32[]{:S(2)}, u32[]{:S(2)}) %collective-permute-start.100) | collective-permute-done | bytes 1048608 | tf_op jit(solution)/shard_map/ppermute | solution.py:339
  1369.6 22.8 %collective-permute-done.88 = bf16[1024,512]{1,0:T(8,128)(2,1)S(1)} collective-permute-done((bf16[1024,512]{1,0:T(8,128)(2,1)S(1)}, bf16[1024,512]{1,0:T(8,128)(2,1)S(1)}, u32[]{:S(2)}, u32[]{:S(2)}) %collective-permute-start.88) | collective-permute-done | bytes 1048608 | tf_op jit(solution)/shard_map/ppermute | solution.py:339
  1394.3 53.0 %collective-permute-done.70 = bf16[2048,256]{1,0:T(8,128)(2,1)S(1)} collective-permute-done((bf16[2048,256]{1,0:T(8,128)(2,1)S(1)}, bf16[2048,256]{1,0:T(8,128)(2,1)S(1)}, u32[]{:S(2)}, u32[]{:S(2)}) %collective-permute-start.70) | collective-permute-done | bytes 1048608 | tf_op jit(solution)/shard_map/ppermute | solution.py:339
  1451.5 21.1 %collective-permute-done.55 = bf16[1024,512]{1,0:T(8,128)(2,1)S(1)} collective-permute-done((bf16[1024,512]{1,0:T(8,128)(2,1)S(1)}, bf16[1024,512]{1,0:T(8,128)(2,1)S(1)}, u32[]{:S(2)}, u32[]{:S(2)}) %collective-permute-start.55) | collective-permute-done | bytes 1048608 | tf_op jit(solution)/shard_map/ppermute | solution.py:309
  1476.4 11.9 collective-permute-done.57
  1509.9 17.6 %collective-permute-done.59 = bf16[2,512,512]{2,1,0:T(8,128)(2,1)} collective-permute-done((bf16[2,512,512]{2,1,0:T(8,128)(2,1)}, bf16[2,512,512]{2,1,0:T(8,128)(2,1)}, u32[]{:S(2)}, u32[]{:S(2)}) %collective-permute-start.59) | collective-permute-done | bytes 1048608 | tf_op jit(solution)/shard_map/ppermute | solution.py:324
  (867 shorter events, 581.6 us)
Async XLA Ops:
  7.2 562.6 %all-reduce.5.cloned.1.call-start = ((), (), s32[]{:S(2)}) async-start(), calls=%async_computation | async-start | bytes 196608 | tf_op jit(solution)/shard_map/psum | solution.py:623
  157.1 138.5 %collective-permute-start.27 = (bf16[512,256]{1,0:T(8,128)(2,1)}, bf16[512,256]{1,0:T(8,128)(2,1)}, u32[]{:S(2)}, u32[]{:S(2)}) collective-permute-start(bf16[512,256]{1,0:T(8,128)(2,1)} %get-tuple-element.181), channel_id=1, source_target_pairs={{0,2},{2,0},{4,6},{6,4},{1,3},{3,1},{5,7},{7,5},{8,10},{10,8},{12,... | collective-permute-start | bytes 786440 | tf_op jit(solution)/shard_map/ppermute | solution.py:309
  224.3 72.3 %collective-permute-start.28 = (bf16[512,256]{1,0:T(8,128)(2,1)}, bf16[512,256]{1,0:T(8,128)(2,1)}, u32[]{:S(2)}, u32[]{:S(2)}) collective-permute-start(bf16[512,256]{1,0:T(8,128)(2,1)} %get-tuple-element.180), channel_id=1, source_target_pairs={{0,4},{2,6},{4,0},{6,2},{1,5},{3,7},{5,1},{7,3},{8,12},{10,14},{12... | collective-permute-start | bytes 786440 | tf_op jit(solution)/shard_map/ppermute | solution.py:309
  224.8 72.3 %collective-permute-start.29 = (bf16[512,256]{1,0:T(8,128)(2,1)}, bf16[512,256]{1,0:T(8,128)(2,1)}, u32[]{:S(2)}, u32[]{:S(2)}) collective-permute-start(bf16[512,256]{1,0:T(8,128)(2,1)} %get-tuple-element.179), channel_id=1, source_target_pairs={{0,6},{2,4},{4,2},{6,0},{1,7},{3,5},{5,3},{7,1},{8,14},{10,12},{12... | collective-permute-start | bytes 786440 | tf_op jit(solution)/shard_map/ppermute | solution.py:309
  226.1 88.9 %collective-permute-start.30 = (bf16[512,256]{1,0:T(8,128)(2,1)S(1)}, bf16[512,256]{1,0:T(8,128)(2,1)}, u32[]{:S(2)}, u32[]{:S(2)}) collective-permute-start(bf16[512,256]{1,0:T(8,128)(2,1)S(1)} %copy-done.79), channel_id=1, source_target_pairs={{0,2},{2,0},{4,6},{6,4},{1,3},{3,1},{5,7},{7,5},{8,10},{10,8},{12,... | collective-permute-start | bytes 786440 | tf_op jit(solution)/shard_map/ppermute | solution.py:309
  226.5 89.5 %collective-permute-start.31 = (bf16[512,256]{1,0:T(8,128)(2,1)S(1)}, bf16[512,256]{1,0:T(8,128)(2,1)}, u32[]{:S(2)}, u32[]{:S(2)}) collective-permute-start(bf16[512,256]{1,0:T(8,128)(2,1)S(1)} %copy-done.78), channel_id=1, source_target_pairs={{0,4},{2,6},{4,0},{6,2},{1,5},{3,7},{5,1},{7,3},{8,12},{10,14},{12... | collective-permute-start | bytes 786440 | tf_op jit(solution)/shard_map/ppermute | solution.py:309
  357.1 214.3 %collective-permute-start.131 = (bf16[256,512]{1,0:T(8,128)(2,1)}, bf16[256,512]{1,0:T(8,128)(2,1)}, u32[]{:S(2)}, u32[]{:S(2)}) collective-permute-start(bf16[256,512]{1,0:T(8,128)(2,1)} %get-tuple-element.205), channel_id=1, source_target_pairs={{0,2},{2,0},{4,6},{6,4},{1,3},{3,1},{5,7},{7,5},{8,10},{10,8},{12,... | collective-permute-start | bytes 786440 | tf_op jit(solution)/shard_map/ppermute | solution.py:309
  357.8 214.9 %collective-permute-start.132 = (bf16[256,512]{1,0:T(8,128)(2,1)}, bf16[256,512]{1,0:T(8,128)(2,1)}, u32[]{:S(2)}, u32[]{:S(2)}) collective-permute-start(bf16[256,512]{1,0:T(8,128)(2,1)} %get-tuple-element.204), channel_id=1, source_target_pairs={{0,4},{2,6},{4,0},{6,2},{1,5},{3,7},{5,1},{7,3},{8,12},{10,14},{12... | collective-permute-start | bytes 786440 | tf_op jit(solution)/shard_map/ppermute | solution.py:309
  358.4 215.3 %collective-permute-start.133 = (bf16[256,512]{1,0:T(8,128)(2,1)}, bf16[256,512]{1,0:T(8,128)(2,1)}, u32[]{:S(2)}, u32[]{:S(2)}) collective-permute-start(bf16[256,512]{1,0:T(8,128)(2,1)} %get-tuple-element.203), channel_id=1, source_target_pairs={{0,6},{2,4},{4,2},{6,0},{1,7},{3,5},{5,3},{7,1},{8,14},{10,12},{12... | collective-permute-start | bytes 786440 | tf_op jit(solution)/shard_map/ppermute | solution.py:309
  362.6 211.6 %collective-permute-start.125 = (bf16[256,512]{1,0:T(8,128)(2,1)}, bf16[256,512]{1,0:T(8,128)(2,1)}, u32[]{:S(2)}, u32[]{:S(2)}) collective-permute-start(bf16[256,512]{1,0:T(8,128)(2,1)} %get-tuple-element.209), channel_id=1, source_target_pairs={{0,2},{2,0},{4,6},{6,4},{1,3},{3,1},{5,7},{7,5},{8,10},{10,8},{12,... | collective-permute-start | bytes 786440 | tf_op jit(solution)/shard_map/ppermute | solution.py:309
  363.4 211.7 %collective-permute-start.126 = (bf16[256,512]{1,0:T(8,128)(2,1)}, bf16[256,512]{1,0:T(8,128)(2,1)}, u32[]{:S(2)}, u32[]{:S(2)}) collective-permute-start(bf16[256,512]{1,0:T(8,128)(2,1)} %get-tuple-element.208), channel_id=1, source_target_pairs={{0,4},{2,6},{4,0},{6,2},{1,5},{3,7},{5,1},{7,3},{8,12},{10,14},{12... | collective-permute-start | bytes 786440 | tf_op jit(solution)/shard_map/ppermute | solution.py:309
  683.6 242.0 %collective-permute-start.60 = (bf16[2048,512]{0,1:T(8,128)(2,1)S(1)}, bf16[2048,512]{0,1:T(8,128)(2,1)S(1)}, u32[]{:S(2)}, u32[]{:S(2)}) collective-permute-start(bf16[2048,512]{0,1:T(8,128)(2,1)S(1)} %copy-done.39), channel_id=1, source_target_pairs={{0,2},{2,0},{4,6},{6,4},{1,3},{3,1},{5,7},{7,5},{8,10},{10,8},{12,... | collective-permute-start | bytes 6291464 | tf_op jit(solution)/shard_map/ppermute | solution.py:309
  697.9 92.1 %collective-permute-start.128 = (bf16[1024,512]{1,0:T(8,128)(2,1)S(1)}, bf16[1024,512]{1,0:T(8,128)(2,1)S(1)}, u32[]{:S(2)}, u32[]{:S(2)}) collective-permute-start(bf16[1024,512]{1,0:T(8,128)(2,1)S(1)} %pad_maximum_fusion.20), channel_id=1, source_target_pairs={{0,8},{24,16},{1,9},{25,17},{2,10},{26,18},{3,11},{27,19},{4,12},{... | collective-permute-start | bytes 3145736 | tf_op jit(solution)/shard_map/ppermute | solution.py:335
  700.7 87.9 %collective-permute-start.92 = (bf16[2048,256]{1,0:T(8,128)(2,1)S(1)}, bf16[2048,256]{1,0:T(8,128)(2,1)S(1)}, u32[]{:S(2)}, u32[]{:S(2)}) collective-permute-start(bf16[2048,256]{1,0:T(8,128)(2,1)S(1)} %pad_maximum_fusion.14), channel_id=1, source_target_pairs={{0,8},{24,16},{1,9},{25,17},{2,10},{26,18},{3,11},{27,19},{4,12},{... | collective-permute-start | bytes 3145736 | tf_op jit(solution)/shard_map/ppermute | solution.py:335
  743.7 67.4 %collective-permute-start.122 = (bf16[1024,512]{1,0:T(8,128)(2,1)S(1)}, bf16[1024,512]{1,0:T(8,128)(2,1)S(1)}, u32[]{:S(2)}, u32[]{:S(2)}) collective-permute-start(bf16[1024,512]{1,0:T(8,128)(2,1)S(1)} %pad_maximum_fusion.19), channel_id=1, source_target_pairs={{0,8},{24,16},{1,9},{25,17},{2,10},{26,18},{3,11},{27,19},{4,12},{... | collective-permute-start | bytes 3145736 | tf_op jit(solution)/shard_map/ppermute | solution.py:335
  749.5 84.1 %collective-permute-start.80 = (bf16[2048,256]{1,0:T(8,128)(2,1)S(1)}, bf16[2048,256]{1,0:T(8,128)(2,1)S(1)}, u32[]{:S(2)}, u32[]{:S(2)}) collective-permute-start(bf16[2048,256]{1,0:T(8,128)(2,1)S(1)} %pad_maximum_fusion.12), channel_id=1, source_target_pairs={{0,8},{24,16},{1,9},{25,17},{2,10},{26,18},{3,11},{27,19},{4,12},{... | collective-permute-start | bytes 3145736 | tf_op jit(solution)/shard_map/ppermute | solution.py:335
  788.6 138.7 %collective-permute-start.62 = (bf16[2048,512]{0,1:T(8,128)(2,1)S(1)}, bf16[2048,512]{0,1:T(8,128)(2,1)S(1)}, u32[]{:S(2)}, u32[]{:S(2)}) collective-permute-start(bf16[2048,512]{0,1:T(8,128)(2,1)S(1)} %copy-done.38), channel_id=1, source_target_pairs={{0,2},{2,0},{4,6},{6,4},{1,3},{3,1},{5,7},{7,5},{8,10},{10,8},{12,... | collective-permute-start | bytes 6291464 | tf_op jit(solution)/shard_map/ppermute | solution.py:309
  789.9 66.1 %collective-permute-start.116 = (bf16[1024,512]{1,0:T(8,128)(2,1)S(1)}, bf16[1024,512]{1,0:T(8,128)(2,1)S(1)}, u32[]{:S(2)}, u32[]{:S(2)}) collective-permute-start(bf16[1024,512]{1,0:T(8,128)(2,1)S(1)} %pad_maximum_fusion.18), channel_id=1, source_target_pairs={{0,8},{24,16},{1,9},{25,17},{2,10},{26,18},{3,11},{27,19},{4,12},{... | collective-permute-start | bytes 3145736 | tf_op jit(solution)/shard_map/ppermute | solution.py:335
  811.1 67.4 %collective-permute-start.86 = (bf16[1024,512]{1,0:T(8,128)(2,1)S(1)}, bf16[1024,512]{1,0:T(8,128)(2,1)S(1)}, u32[]{:S(2)}, u32[]{:S(2)}) collective-permute-start(bf16[1024,512]{1,0:T(8,128)(2,1)S(1)} %pad_maximum_fusion.13), channel_id=1, source_target_pairs={{0,8},{24,16},{1,9},{25,17},{2,10},{26,18},{3,11},{27,19},{4,12},{... | collective-permute-start | bytes 3145736 | tf_op jit(solution)/shard_map/ppermute | solution.py:335
  833.5 67.4 %collective-permute-start.74 = (bf16[2048,256]{1,0:T(8,128)(2,1)S(1)}, bf16[2048,256]{1,0:T(8,128)(2,1)S(1)}, u32[]{:S(2)}, u32[]{:S(2)}) collective-permute-start(bf16[2048,256]{1,0:T(8,128)(2,1)S(1)} %pad_maximum_fusion.11), channel_id=1, source_target_pairs={{0,8},{24,16},{1,9},{25,17},{2,10},{26,18},{3,11},{27,19},{4,12},{... | collective-permute-start | bytes 3145736 | tf_op jit(solution)/shard_map/ppermute | solution.py:335
  856.0 66.7 %collective-permute-start.68 = (bf16[2048,256]{1,0:T(8,128)(2,1)S(1)}, bf16[2048,256]{1,0:T(8,128)(2,1)S(1)}, u32[]{:S(2)}, u32[]{:S(2)}) collective-permute-start(bf16[2048,256]{1,0:T(8,128)(2,1)S(1)} %pad_maximum_fusion.10), channel_id=1, source_target_pairs={{0,8},{24,16},{1,9},{25,17},{2,10},{26,18},{3,11},{27,19},{4,12},{... | collective-permute-start | bytes 3145736 | tf_op jit(solution)/shard_map/ppermute | solution.py:335
  964.2 528.6 %collective-permute-start.61 = (bf16[1024,512]{0,1:T(8,128)(2,1)}, bf16[1024,512]{0,1:T(8,128)(2,1)S(1)}, u32[]{:S(2)}, u32[]{:S(2)}) collective-permute-start(bf16[1024,512]{0,1:T(8,128)(2,1)} %slice.901), channel_id=1, source_target_pairs={{0,1},{1,0},{2,3},{3,2},{4,5},{5,4},{6,7},{7,6},{8,9},{9,8},{10,11... | collective-permute-start | bytes 3145736 | tf_op jit(solution)/shard_map/ppermute | solution.py:313
  968.1 65.6 %collective-permute-start.54 = (bf16[1024,512]{1,0:T(8,128)(2,1)S(1)}, bf16[1024,512]{1,0:T(8,128)(2,1)S(1)}, u32[]{:S(2)}, u32[]{:S(2)}) collective-permute-start(bf16[1024,512]{1,0:T(8,128)(2,1)S(1)} %slice.902), channel_id=1, source_target_pairs={{0,1},{1,0},{2,3},{3,2},{4,5},{5,4},{6,7},{7,6},{8,9},{9,8},{10,11... | collective-permute-start | bytes 3145736 | tf_op jit(solution)/shard_map/ppermute | solution.py:313
  968.5 231.2 %collective-permute-start.118 = (bf16[1024,512]{1,0:T(8,128)(2,1)S(1)}, bf16[1024,512]{1,0:T(8,128)(2,1)S(1)}, u32[]{:S(2)}, u32[]{:S(2)}) collective-permute-start(bf16[1024,512]{1,0:T(8,128)(2,1)S(1)} %add_convert_fusion.8), channel_id=1, source_target_pairs={{8,0},{16,24},{9,1},{17,25},{10,2},{18,26},{11,3},{19,27},{12,4},{... | collective-permute-start | bytes 3145736 | tf_op jit(solution)/shard_map/ppermute | solution.py:339
  971.6 479.8 %collective-permute-start.52 = (bf16[1024,512]{1,0:T(8,128)(2,1)}, bf16[1024,512]{1,0:T(8,128)(2,1)S(1)}, u32[]{:S(2)}, u32[]{:S(2)}) collective-permute-start(bf16[1024,512]{1,0:T(8,128)(2,1)} %slice.903), channel_id=1, source_target_pairs={{0,1},{1,0},{2,3},{3,2},{4,5},{5,4},{6,7},{7,6},{8,9},{9,8},{10,11... | collective-permute-start | bytes 3145736 | tf_op jit(solution)/shard_map/ppermute | solution.py:313
  988.8 293.4 %collective-permute-start.136 = (bf16[1024,512]{1,0:T(8,128)(2,1)S(1)}, bf16[1024,512]{1,0:T(8,128)(2,1)S(1)}, u32[]{:S(2)}, u32[]{:S(2)}) collective-permute-start(bf16[1024,512]{1,0:T(8,128)(2,1)S(1)} %add_convert_fusion.2), channel_id=1, source_target_pairs={{8,0},{16,24},{9,1},{17,25},{10,2},{18,26},{11,3},{19,27},{12,4},{... | collective-permute-start | bytes 3145736 | tf_op jit(solution)/shard_map/ppermute | solution.py:339
  1033.7 242.7 %collective-permute-start.130 = (bf16[1024,512]{1,0:T(8,128)(2,1)S(1)}, bf16[1024,512]{1,0:T(8,128)(2,1)S(1)}, u32[]{:S(2)}, u32[]{:S(2)}) collective-permute-start(bf16[1024,512]{1,0:T(8,128)(2,1)S(1)} %add_convert_fusion.4), channel_id=1, source_target_pairs={{8,0},{16,24},{9,1},{17,25},{10,2},{18,26},{11,3},{19,27},{12,4},{... | collective-permute-start | bytes 3145736 | tf_op jit(solution)/shard_map/ppermute | solution.py:339
  1199.7 72.8 %collective-permute-start.124 = (bf16[1024,512]{1,0:T(8,128)(2,1)S(1)}, bf16[1024,512]{1,0:T(8,128)(2,1)S(1)}, u32[]{:S(2)}, u32[]{:S(2)}) collective-permute-start(bf16[1024,512]{1,0:T(8,128)(2,1)S(1)} %add_convert_fusion.6), channel_id=1, source_target_pairs={{8,0},{16,24},{9,1},{17,25},{10,2},{18,26},{11,3},{19,27},{12,4},{... | collective-permute-start | bytes 3145736 | tf_op jit(solution)/shard_map/ppermute | solution.py:339
  1272.5 95.4 %collective-permute-start.112 = (bf16[2048,256]{1,0:T(8,128)(2,1)S(1)}, bf16[2048,256]{1,0:T(8,128)(2,1)S(1)}, u32[]{:S(2)}, u32[]{:S(2)}) collective-permute-start(bf16[2048,256]{1,0:T(8,128)(2,1)S(1)} %add_convert_fusion.10), channel_id=1, source_target_pairs={{8,0},{16,24},{9,1},{17,25},{10,2},{18,26},{11,3},{19,27},{12,4},{... | collective-permute-start | bytes 3145736 | tf_op jit(solution)/shard_map/ppermute | solution.py:339
  1276.4 89.6 %collective-permute-start.106 = (bf16[2048,256]{1,0:T(8,128)(2,1)S(1)}, bf16[2048,256]{1,0:T(8,128)(2,1)S(1)}, u32[]{:S(2)}, u32[]{:S(2)}) collective-permute-start(bf16[2048,256]{1,0:T(8,128)(2,1)S(1)} %add_convert_fusion.12), channel_id=1, source_target_pairs={{8,0},{16,24},{9,1},{17,25},{10,2},{18,26},{11,3},{19,27},{12,4},{... | collective-permute-start | bytes 3145736 | tf_op jit(solution)/shard_map/ppermute | solution.py:339
  1366.0 110.2 %collective-permute-start.82 = (bf16[2048,256]{1,0:T(8,128)(2,1)S(1)}, bf16[2048,256]{1,0:T(8,128)(2,1)S(1)}, u32[]{:S(2)}, u32[]{:S(2)}) collective-permute-start(bf16[2048,256]{1,0:T(8,128)(2,1)S(1)} %add_convert_fusion.20), channel_id=1, source_target_pairs={{8,0},{16,24},{9,1},{17,25},{10,2},{18,26},{11,3},{19,27},{12,4},{... | collective-permute-start | bytes 3145736 | tf_op jit(solution)/shard_map/ppermute | solution.py:339
  1367.8 82.5 %collective-permute-start.76 = (bf16[2048,256]{1,0:T(8,128)(2,1)S(1)}, bf16[2048,256]{1,0:T(8,128)(2,1)S(1)}, u32[]{:S(2)}, u32[]{:S(2)}) collective-permute-start(bf16[2048,256]{1,0:T(8,128)(2,1)S(1)} %add_convert_fusion.22), channel_id=1, source_target_pairs={{8,0},{16,24},{9,1},{17,25},{10,2},{18,26},{11,3},{19,27},{12,4},{... | collective-permute-start | bytes 3145736 | tf_op jit(solution)/shard_map/ppermute | solution.py:339
  (278 other events, 7398.2 us)
Sparse Core Ops, SparseCore 0:
  448.7 121.0 all-reduce.4

commit v2 on v0

--- a/solution.py
+++ b/solution.py
@@ -4,12 +4,17 @@
 import jax
 import jax.numpy as jnp
 from jax import lax
+from jax.experimental import pallas as pl
+from jax.experimental.pallas import tpu as pltpu
 from jax.sharding import PartitionSpec as P
 
 D = 2048
 HD = 128
 ROT = 32
 QBLK = 512
+CHUNK = 256
+BF16 = jnp.bfloat16
+F32 = jnp.float32
 
 
 norm_epsilon = 1e-05
@@ -300,7 +305,1088 @@
     )
 
 
+UNIT = 256
+TILE = 512
+
+
+def product(left, right, dims):
+    return lax.dot_general(left, right, (dims, ((), ())), preferred_element_type=F32)
+
+
+def fold_lanes(values):
+    total = values[:, :128]
+    for at in range(128, values.shape[1], 128):
+        total = total + values[:, at : at + 128]
+    return total
+
+
+class Copies:
+    def __init__(self, send_sems, recv_sems):
+        self.send_sems, self.recv_sems, self.used = send_sems, recv_sems, 0
+
+    def make(self, source, target, device):
+        number = self.used
+        self.used += 1
+
+        def build():
+            return pltpu.make_async_remote_copy(
+                src_ref=source(),
+                dst_ref=target(),
+                send_sem=self.send_sems.at[number],
+                recv_sem=self.recv_sems.at[number],
+                device_id=device,
+                device_id_type=pl.DeviceIdType.MESH,
+            )
+
+        return build
+
+
+def attention_head(qkv, back, cos, low, high, allowed):
+    scale = 1.0 / math.sqrt(HD)
+
+    def turn(values):
+        return values * cos + pltpu.roll(values, HD - 16, 1) * low + pltpu.roll(values, 16, 1) * high
+
+    def turn_back(values):
+        return (
+            values * cos
+            + pltpu.roll(values * high, HD - 16, 1)
+            + pltpu.roll(values * low, 16, 1)
+        )
+
+    query = turn(qkv[:, :HD]).astype(BF16)
+    key = turn(qkv[:, HD : 2 * HD]).astype(BF16)
+    value = qkv[:, 2 * HD :].astype(BF16)
+    scores = product(query, key, ((1,), (1,))) * scale
+    scores = jnp.where(allowed, scores, masked_score)
+    weight = jnp.exp(scores - jnp.max(scores, axis=1, keepdims=True))
+    probs = weight * (1.0 / jnp.sum(weight, axis=1, keepdims=True))
+    probs_low = probs.astype(BF16)
+    attn = product(probs_low, value, ((1,), (0,))).astype(BF16)
+    grad_probs = product(back, value, ((1,), (1,)))
+    centre = jnp.sum(probs * grad_probs, axis=1, keepdims=True)
+    grad_scores = (probs * (grad_probs - centre)).astype(BF16)
+    grad_query = product(grad_scores, key, ((1,), (0,))) * scale
+    grad_key = product(grad_scores, query, ((0,), (0,))) * scale
+    grad_value = product(probs_low, back, ((0,), (0,)))
+    return attn, [turn_back(grad_query), turn_back(grad_key), grad_value]
+
+
+def layer_kernel(
+    codes,
+    x_own,
+    cot_in,
+    norm_own,
+    bias_in,
+    out_bias,
+    qkv_w,
+    dense_w,
+    fc1_w,
+    fc2_w,
+    cos_in,
+    low_in,
+    high_in,
+    begin_in,
+    first_sum,
+    second_sum,
+    output,
+    grad_norm,
+    cot_own,
+    stats,
+    gain_q,
+    bias_q,
+    gain_f,
+    bias_f,
+    unit_sums,
+    x_all,
+    cot_all,
+    ln1,
+    ln2,
+    w1,
+    w2,
+    acts,
+    grads,
+    first_part,
+    second_part,
+    first_here,
+    second_here,
+    first_in,
+    second_in,
+    first_half,
+    second_half,
+    first_other,
+    second_other,
+    out_part,
+    out_core,
+    out_chip,
+    out_x,
+    out_half,
+    out_y,
+    out_item,
+    dx_part,
+    dx_core,
+    dx_chip,
+    dx_x,
+    dx_half,
+    dx_y,
+    cot_up,
+    cot_down,
+    cot_far,
+    cot_send,
+    cot_edge,
+    out_up,
+    out_down,
+    out_far,
+    out_send,
+    out_edge,
+    acc,
+    norm_all,
+    gain_acc,
+    sum_acc,
+    send_sems,
+    recv_sems,
+    local_sems,
+):
+    z, r, c = lax.axis_index("dp"), lax.axis_index("row"), lax.axis_index("col")
+    y, core = r // 2, r % 2
+    mid = ((z + 1) // 2) % 2
+    upper = z // 2
+    z_in = mid * (3 - z) + (1 - mid) * (1 + upper)
+    z_out = 3 * upper
+    is_mid, is_edge = mid == 1, mid == 0
+    peer = [r, 2 * y + (1 - core), 2 * (1 - y) + core, 2 * (1 - y) + (1 - core)]
+    slabs, slab, feats = x_own.shape
+    own_rows = slabs * slab
+    rows = 2 * own_rows
+    hidden_here = fc1_w.shape[1] // 4
+    qkv_here = qkv_w.shape[1] // 4
+    attn_here = dense_w.shape[0] // 4
+    to_row = [{"row": peer[j]} for j in range(4)]
+    to_col = {"col": 1 - c}
+    to_in = {"dp": z_in}
+    to_out = {"dp": z_out}
+    copies = Copies(send_sems, recv_sems)
+    sent = []
+
+    barrier = pltpu.get_barrier_semaphore()
+
+    def greet(device):
+        pl.semaphore_signal(barrier, inc=1, device_id=device, device_id_type=pl.DeviceIdType.MESH)
+
+    for j in (1, 2, 3):
+        greet(to_row[j])
+    greet(to_col)
+    greet(to_in)
+
+    @pl.when(is_mid)
+    def _():
+        greet(to_out)
+        pl.semaphore_wait(barrier, 6)
+
+    @pl.when(is_edge)
+    def _():
+        pl.semaphore_wait(barrier, 5)
+
+    def start(copy):
+        copy().start()
+        sent.append(copy)
+
+    def when(flag, action):
+        pl.when(flag)(action)
+
+    local_used = [0]
+
+    def local(source, target):
+        number = local_used[0]
+        local_used[0] += 1
+
+        def build():
+            return pltpu.make_async_copy(source(), target(), local_sems.at[number])
+
+        build().start()
+        return build
+
+    own_half = pl.ds(c * own_rows, own_rows)
+    far_half = pl.ds((1 - c) * own_rows, own_rows)
+
+    class Gather:
+        def __init__(self, own, whole):
+            self.whole = whole
+            block = lambda j, half: whole.at[peer[j], pl.ds(slabs * half, slabs)]
+            self.to_y = copies.make(lambda: own, lambda: block(0, c), to_row[2])
+            self.to_x = copies.make(lambda: own, lambda: block(0, c), to_col)
+            self.to_core = copies.make(lambda: own, lambda: block(0, c), to_row[1])
+            self.y_to_x = copies.make(lambda: block(2, c), lambda: block(2, c), to_col)
+            self.y_to_core = copies.make(
+                lambda: block(2, c), lambda: block(2, c), to_row[1]
+            )
+            self.x_to_core = copies.make(
+                lambda: block(0, 1 - c), lambda: block(0, 1 - c), to_row[1]
+            )
+            self.xy_to_core = copies.make(
+                lambda: block(2, 1 - c), lambda: block(2, 1 - c), to_row[1]
+            )
+            self.own = own
+
+        def begin(self):
+            start(self.to_y)
+            start(self.to_x)
+            start(self.to_core)
+            self.kept = local(lambda: self.own, lambda: self.whole.at[r, pl.ds(slabs * c, slabs)])
+
+        def after_y(self):
+            self.to_y().wait_recv()
+            start(self.y_to_x)
+            start(self.y_to_core)
+
+        def after_x(self):
+            self.to_x().wait_recv()
+            start(self.x_to_core)
+            self.y_to_x().wait_recv()
+            start(self.xy_to_core)
+
+        def end(self):
+            self.kept().wait()
+            for copy in (self.to_core, self.y_to_core, self.x_to_core, self.xy_to_core):
+                copy().wait_recv()
+
+    def choose(code_at, refs, target):
+        def body(*blocks):
+            code = codes[code_at + pl.program_id(0)]
+            value = blocks[0][...]
+            for which in range(1, len(refs)):
+                value = jnp.where(code == which, blocks[which][...], value)
+            blocks[-1][...] = value
+
+        block = pl.BlockSpec((1, slab, feats), lambda q: (q, 0, 0))
+        pltpu.emit_pipeline(
+            body, grid=(2,), in_specs=[block] * len(refs), out_specs=[block]
+        )(*refs, target)
+
+    class Route:
+        def __init__(self, item, code_at, up, down, far, send, edge, target):
+            self.item, self.code_at, self.up, self.down = item, code_at, up, down
+            self.far, self.send, self.edge, self.target = far, send, edge, target
+            self.upward = copies.make(lambda: item, lambda: up, {"dp": z + 1})
+            self.downward = copies.make(lambda: item, lambda: down, {"dp": z - 1})
+            self.far_up = copies.make(lambda: up, lambda: far, to_in)
+            self.far_down = copies.make(lambda: down, lambda: far, to_in)
+            self.outward = copies.make(lambda: send, lambda: edge, to_out)
+
+        def begin(self):
+            when(z < 2, lambda: self.upward().start())
+            when(z > 1, lambda: self.downward().start())
+
+        def relay(self):
+            def from_below():
+                self.upward().wait_recv()
+                self.far_up().start()
+                self.downward().wait_recv()
+
+            def from_above():
+                self.downward().wait_recv()
+                self.far_down().start()
+                self.upward().wait_recv()
+
+            when(z == 1, from_below)
+            when(z == 2, from_above)
+
+        def hand_out(self):
+            def middle():
+                when(z == 1, lambda: self.far_down().wait_recv())
+                when(z == 2, lambda: self.far_up().wait_recv())
+                choose(
+                    self.code_at + 2, [self.item, self.up, self.down, self.far], self.send
+                )
+                self.outward().start()
+                choose(self.code_at, [self.item, self.up, self.down, self.far], self.target)
+
+            when(is_mid, middle)
+
+        def take(self):
+            def edge():
+                self.outward().wait_recv()
+                choose(self.code_at, [self.item, self.edge], self.target)
+
+            when(is_edge, edge)
+
+        def finish(self):
+            when(z < 2, lambda: self.upward().wait_send())
+            when(z > 1, lambda: self.downward().wait_send())
+            when(z == 1, lambda: self.far_up().wait_send())
+            when(z == 2, lambda: self.far_down().wait_send())
+            when(is_mid, lambda: self.outward().wait_send())
+
+    x_gather = Gather(x_own, x_all)
+    cot_slabs = cot_in
+    cot_route = Route(
+        cot_slabs, 0, cot_up, cot_down, cot_far, cot_send, cot_edge, cot_own
+    )
+    norm_copies = [
+        copies.make(lambda: norm_own, lambda: norm_all.at[r], to_row[j]) for j in (1, 2, 3)
+    ]
+
+    class Fetch:
+        def __init__(self, first, first_at, first_width, at, second, second_at, second_width, low):
+            def first_source(j):
+                lanes = pl.multiple_of(peer[j] * first_width + first_at, 256)
+                size = UNIT if first is fc1_w else qkv_here
+                return first.at[:, pl.ds(lanes, size)]
+
+            def second_source(j):
+                size = UNIT
+                begin = pl.multiple_of(peer[j] * second_width + second_at, 256)
+                return second.at[pl.ds(begin, size)]
+
+            size = UNIT if first is fc1_w else qkv_here
+            first_target = lambda: w1.at[r, :, pl.ds(at, size)]
+            second_target = lambda: w2.at[r, pl.ds(low, UNIT)]
+            self.remote = []
+            for j in (1, 2, 3):
+                self.remote.append(
+                    copies.make(partial(first_source, j), first_target, to_row[j])
+                )
+                self.remote.append(
+                    copies.make(partial(second_source, j), second_target, to_row[j])
+                )
+            self.kept = [(partial(first_source, 0), first_target), (partial(second_source, 0), second_target)]
+
+        def begin(self):
+            for copy in self.remote:
+                start(copy)
+            self.kept = [local(*pair) for pair in self.kept]
+
+        def end(self):
+            for copy in self.remote:
+                copy().wait_recv()
+            for copy in self.kept:
+                copy().wait()
+
+    attn_fetch = Fetch(qkv_w, 0, qkv_here, 0, dense_w, 0, attn_here, 0)
+    mlp_fetch = [
+        Fetch(fc1_w, at, hidden_here, qkv_here + at, fc2_w, at, hidden_here, attn_here + at)
+        for at in range(0, hidden_here, UNIT)
+    ]
+
+    class Unit:
+        def __init__(self, kind, at):
+            self.kind, self.at = kind, at
+            if kind == 1:
+                self.view = lambda ref, s: ref.at[s, :, pl.ds(at, UNIT)]
+                self.whole = lambda ref: ref.at[:, :, pl.ds(at, UNIT)]
+                self.block = pl.BlockSpec((1, feats, UNIT), lambda s: (s, 0, at // UNIT))
+                self.refs = (first_part, first_here, first_in, first_half, first_other, first_sum)
+            else:
+                self.view = lambda ref, s: ref.at[s, pl.ds(at, UNIT)]
+                self.whole = lambda ref: ref.at[:, pl.ds(at, UNIT)]
+                self.block = pl.BlockSpec((1, UNIT, feats), lambda s: (s, at // UNIT, 0))
+                self.refs = (
+                    second_part,
+                    second_here,
+                    second_in,
+                    second_half,
+                    second_other,
+                    second_sum,
+                )
+            part, here, arrived, half, other, total = self.refs
+            self.spread = [
+                copies.make(
+                    partial(lambda j: self.view(part, peer[j]), j),
+                    lambda: self.view(here, r),
+                    to_row[j],
+                )
+                for j in (1, 2, 3)
+            ]
+            self.inward = copies.make(lambda: self.whole(here), lambda: self.whole(arrived), to_in)
+            self.across = copies.make(lambda: self.whole(half), lambda: self.whole(other), to_in)
+            self.outward = copies.make(lambda: self.whole(total), lambda: self.whole(total), to_out)
+
+        def send(self):
+            part, here = self.refs[:2]
+            for copy in self.spread:
+                start(copy)
+            self.kept = local(lambda: self.view(part, r), lambda: self.view(here, r))
+
+        def collect(self):
+            for copy in self.spread:
+                copy().wait_recv()
+            self.kept().wait()
+            when(is_edge, lambda: self.inward().start())
+
+        def add(self, left, right, target):
+            def body(left_block, right_block, target_block):
+                target_block[...] = (
+                    left_block[...].astype(F32) + right_block[...].astype(F32)
+                ).astype(BF16)
+
+            pltpu.emit_pipeline(
+                body, grid=(4,), in_specs=[self.block] * 2, out_specs=[self.block]
+            )(left, right, target)
+
+        def halve(self):
+            part, here, arrived, half, other, total = self.refs
+
+            def middle():
+                self.inward().wait_recv()
+                self.add(here, arrived, half)
+                self.across().start()
+
+            when(is_mid, middle)
+
+        def close(self):
+            part, here, arrived, half, other, total = self.refs
+
+            def middle():
+                self.across().wait_recv()
+                self.add(half, other, total)
+                self.outward().start()
+
+            when(is_mid, middle)
+
+        def finish(self):
+            def edge():
+                self.outward().wait_recv()
+                self.inward().wait_send()
+
+            def middle():
+                self.across().wait_send()
+                self.outward().wait_send()
+
+            when(is_edge, edge)
+            when(is_mid, middle)
+
+    mlp_units = [
+        [Unit(2, attn_here + at), Unit(1, qkv_here + at)] for at in range(0, hidden_here, UNIT)
+    ]
+    attn_units = [Unit(2, 0)] + [Unit(1, at) for at in range(0, qkv_here, UNIT)]
+
+    def norm_body(x_ref, one_ref, two_ref, stat_ref):
+        wide = jnp.concatenate([x_ref[j, 0] for j in range(4)], axis=1).astype(F32)
+        norms = jnp.concatenate([norm_all[j] for j in range(4)], axis=1)
+        mean = jnp.sum(wide, axis=1, keepdims=True) / D
+        square = jnp.sum(wide * wide, axis=1, keepdims=True) / D
+        inv_std = lax.rsqrt(square - mean * mean + norm_epsilon)
+        normed = (wide - mean) * inv_std
+        one_ref[...] = (normed * norms[0:1] + norms[1:2]).astype(BF16)
+        two_ref[...] = (normed * norms[2:3] + norms[3:4]).astype(BF16)
+        lane = lax.broadcasted_iota(jnp.int32, stat_ref.shape, 1)
+        stat_ref[...] = jnp.where(lane < 64, mean, inv_std)
+
+    def norm_stage():
+        tile = 256
+        flat = pl.BlockSpec((tile, D), lambda i: (i, 0))
+        pltpu.emit_pipeline(
+            norm_body,
+            grid=(rows // tile,),
+            in_specs=[
+                pl.BlockSpec(
+                    (4, 1, tile, feats), lambda i: (0, i * tile // slab, i % (slab // tile), 0)
+                )
+            ],
+            out_specs=[flat, flat, pl.BlockSpec((tile, 128), lambda i: (i, 0))],
+        )(x_all, ln1, ln2, stats)
+
+    def mlp_stage(k):
+        at = k * UNIT
+        bias = bias_in[0:1, qkv_here + at : qkv_here + at + UNIT]
+
+        def body(ln_ref, cot_ref, first_ref, second_ref, act_ref, grad_ref):
+            step = pl.program_id(0)
+
+            @pl.when(step == 0)
+            def _():
+                acc[:, : 2 * UNIT, :] = jnp.zeros((4, 2 * UNIT, feats), F32)
+                sum_acc[:, :UNIT] = jnp.zeros((8, UNIT), F32)
+
+            hidden = bias
+            grad_act = None
+            for j in range(4):
+                lanes = slice(j * feats, (j + 1) * feats)
+                hidden = hidden + product(ln_ref[:, lanes], first_ref[j], ((1,), (0,)))
+                term = product(cot_ref[j, 0], second_ref[j], ((1,), (1,)))
+                grad_act = term if j == 0 else grad_act + term
+            curve = 0.5 * (1.0 + lax.erf(hidden * math.sqrt(0.5)))
+            bell = jnp.exp(-0.5 * hidden * hidden) * (1.0 / math.sqrt(2.0 * math.pi))
+            act = (hidden * curve).astype(BF16)
+            grad_hidden = (grad_act * (curve + hidden * bell)).astype(BF16)
+            act_ref[...] = act
+            grad_ref[...] = grad_hidden
+            sum_acc[0:1, :UNIT] += jnp.sum(grad_hidden.astype(F32), axis=0, keepdims=True)
+            for j in range(4):
+                lanes = slice(j * feats, (j + 1) * feats)
+                acc[j, :UNIT] += product(act, cot_ref[j, 0], ((0,), (0,)))
+                acc[j, UNIT : 2 * UNIT] += product(grad_hidden, ln_ref[:, lanes], ((0,), (0,)))
+
+        pltpu.emit_pipeline(
+            body,
+            grid=(rows // TILE,),
+            in_specs=[
+                pl.BlockSpec((TILE, D), lambda i: (i, 0)),
+                pl.BlockSpec((4, 1, slab, feats), lambda i: (0, i, 0, 0)),
+                pl.BlockSpec((4, feats, UNIT), lambda i: (0, 0, (qkv_here + at) // UNIT)),
+                pl.BlockSpec((4, UNIT, feats), lambda i: (0, (attn_here + at) // UNIT, 0)),
+            ],
+            out_specs=[
+                pl.BlockSpec((TILE, UNIT), lambda i: (i, (attn_here + at) // UNIT)),
+                pl.BlockSpec((TILE, UNIT), lambda i: (i, (qkv_here + at) // UNIT)),
+            ],
+        )(ln2, cot_all, w1, w2, acts, grads)
+        grad_stage(UNIT, qkv_here + at, attn_here + at, 1, k == 0)
+        unit_sums[:, qkv_here + at : qkv_here + at + UNIT] = sum_acc[:, :UNIT]
+
+    def grad_stage(width, first_at, second_at, which, fresh):
+        def body(first_ref, part_one, part_two):
+            j = pl.program_id(0)
+            grad = acc[j, UNIT : UNIT + width].T
+            weight = first_ref[0].astype(F32)
+            part_one[0] = grad.astype(BF16)
+            part_two[0] = acc[j, :UNIT].astype(BF16)
+            here = pl.ds(j * feats, feats)
+            gains = fold_lanes(grad * weight)
+            biases = fold_lanes(weight * sum_acc[0:1, :width])
+            if fresh:
+                gain_acc[2 * which, here] = gains
+                gain_acc[2 * which + 1, here] = biases
+            else:
+                gain_acc[2 * which, here] += gains
+                gain_acc[2 * which + 1, here] += biases
+
+        lanes = slice(first_at, first_at + width)
+        block = pl.BlockSpec((1, feats, width), lambda j: (j, 0, 0))
+        pltpu.emit_pipeline(
+            body,
+            grid=(4,),
+            in_specs=[block],
+            out_specs=[block, pl.BlockSpec((1, UNIT, feats), lambda j: (j, second_at // UNIT, 0))],
+        )(w1.at[:, :, lanes], first_part.at[:, :, lanes], second_part)
+
+    def attention_stage():
+        heads = qkv_here // (3 * HD)
+        bias = bias_in[0:1, :qkv_here]
+
+        def body(
+            ln_ref, cot_ref, first_ref, second_ref, cos, low, high, begin, act_ref, grad_ref
+        ):
+            step = pl.program_id(0)
+
+            @pl.when(step == 0)
+            def _():
+                acc[...] = jnp.zeros(acc.shape, F32)
+                sum_acc[...] = jnp.zeros(sum_acc.shape, F32)
+
+            qkv = bias
+            back = None
+            for j in range(4):
+                lanes = slice(j * feats, (j + 1) * feats)
+                qkv = qkv + product(ln_ref[:, lanes], first_ref[j], ((1,), (0,)))
+                term = product(cot_ref[j, 0], second_ref[j], ((1,), (1,)))
+                back = term if j == 0 else back + term
+            back = back.astype(BF16)
+            at = lax.broadcasted_iota(jnp.int32, (TILE, TILE), 0)
+            of = lax.broadcasted_iota(jnp.int32, (TILE, TILE), 1)
+            allowed = (of <= at) & (of >= begin[:, :1])
+            for h in range(heads):
+                attn, grads_here = attention_head(
+                    qkv[:, h * 3 * HD : (h + 1) * 3 * HD],
+                    back[:, h * HD : (h + 1) * HD],
+                    cos[...],
+                    low[...],
+                    high[...],
+                    allowed,
+                )
+                act_ref[:, h * HD : (h + 1) * HD] = attn
+                for i in range(3):
+                    at_lane = (h * 3 + i) * HD
+                    grad_ref[:, at_lane : at_lane + HD] = grads_here[i].astype(BF16)
+            attn, grad = act_ref[...], grad_ref[...]
+            sum_acc[0:1, :qkv_here] += jnp.sum(grad.astype(F32), axis=0, keepdims=True)
+            for j in range(4):
+                lanes = slice(j * feats, (j + 1) * feats)
+                acc[j, :UNIT] += product(attn, cot_ref[j, 0], ((0,), (0,)))
+                acc[j, UNIT:] += product(grad, ln_ref[:, lanes], ((0,), (0,)))
+
+        table = pl.BlockSpec((TILE, HD), lambda i: (i, 0))
+        pltpu.emit_pipeline(
+            body,
+            grid=(rows // TILE,),
+            in_specs=[
+                pl.BlockSpec((TILE, D), lambda i: (i, 0)),
+                pl.BlockSpec((4, 1, slab, feats), lambda i: (0, i, 0, 0)),
+                pl.BlockSpec((4, feats, qkv_here), lambda i: (0, 0, 0)),
+                pl.BlockSpec((4, UNIT, feats), lambda i: (0, 0, 0)),
+                table,
+                table,
+                table,
+                table,
+            ],
+            out_specs=[
+                pl.BlockSpec((TILE, UNIT), lambda i: (i, 0)),
+                pl.BlockSpec((TILE, qkv_here), lambda i: (i, 0)),
+            ],
+        )(
+            ln1,
+            cot_all,
+            w1.at[:, :, :qkv_here],
+            w2,
+            cos_in,
+            low_in,
+            high_in,
+            begin_in,
+            acts,
+            grads.at[:, :qkv_here],
+        )
+        grad_stage(qkv_here, 0, 0, 0, True)
+        unit_sums[:, :qkv_here] = sum_acc[:, :qkv_here]
+
+    def out_stage():
+        def body(act_ref, second_ref, part_ref):
+            part_ref[0] = product(act_ref[...], second_ref[0], ((1,), (0,))).astype(BF16)
+
+        pltpu.emit_pipeline(
+            body,
+            grid=(4, rows // TILE),
+            in_specs=[
+                pl.BlockSpec((TILE, acts.shape[1]), lambda n, i: (i, 0)),
+                pl.BlockSpec((1, w2.shape[1], feats), lambda n, i: (n, 0, 0)),
+            ],
+            out_specs=[pl.BlockSpec((1, TILE, feats), lambda n, i: (n, i, 0))],
+        )(acts, w2, out_part)
+
+    def dx_stage():
+        def body(grad_ref, first_ref, part_ref):
+            norms = norm_all[pl.program_id(0)]
+            one = product(grad_ref[:, :qkv_here], first_ref[0, :, :qkv_here], ((1,), (1,)))
+            two = product(grad_ref[:, qkv_here:], first_ref[0, :, qkv_here:], ((1,), (1,)))
+            part_ref[0] = (one * norms[0:1] + two * norms[2:3]).astype(BF16)
+
+        pltpu.emit_pipeline(
+            body,
+            grid=(4, rows // TILE),
+            in_specs=[
+                pl.BlockSpec((TILE, grads.shape[1]), lambda n, i: (i, 0)),
+                pl.BlockSpec((1, feats, w1.shape[2]), lambda n, i: (n, 0, 0)),
+            ],
+            out_specs=[pl.BlockSpec((1, TILE, feats), lambda n, i: (n, i, 0))],
+        )(grads, w1, dx_part)
+
+    class Scatter:
+        def __init__(self, part, from_core, chip, from_x, half, from_y):
+            self.part, self.from_core, self.chip = part, from_core, chip
+            self.from_x, self.half, self.from_y = from_x, half, from_y
+            self.to_core = [
+                copies.make(
+                    partial(lambda j: part.at[peer[j]], j),
+                    partial(lambda j: from_core.at[peer[j] // 2], j),
+                    to_row[1],
+                )
+                for j in (1, 3)
+            ]
+            self.to_x = copies.make(
+                lambda: chip.at[:, far_half], lambda: from_x, to_col
+            )
+            self.to_y = copies.make(lambda: half.at[1 - y], lambda: from_y, to_row[2])
+
+        def begin(self):
+            for copy in self.to_core:
+                start(copy)
+
+        def second(self):
+            for copy in self.to_core:
+                copy().wait_recv()
+
+            def body(left, right, target):
+                target[...] = (left[...].astype(F32) + right[...].astype(F32)).astype(BF16)
+
+            block = pl.BlockSpec((1, TILE, feats), lambda s, i: (s, i, 0))
+            pltpu.emit_pipeline(
+                body,
+                grid=(2, rows // TILE),
+                in_specs=[
+                    pl.BlockSpec((1, TILE, feats), lambda s, i: (2 * s + core, i, 0)),
+                    block,
+                ],
+                out_specs=[block],
+            )(self.part, self.from_core, self.chip)
+            start(self.to_x)
+
+        def third(self):
+            self.to_x().wait_recv()
+
+            def body(left, right, target):
+                target[...] = (left[...].astype(F32) + right[...].astype(F32)).astype(BF16)
+
+            block = pl.BlockSpec((1, TILE, feats), lambda s, i: (s, i, 0))
+            tiles = own_rows // TILE
+            pltpu.emit_pipeline(
+                body,
+                grid=(2, tiles),
+                in_specs=[
+                    pl.BlockSpec((1, TILE, feats), lambda s, i: (s, c * tiles + i, 0)),
+                    block,
+                ],
+                out_specs=[block],
+            )(self.chip, self.from_x, self.half)
+            start(self.to_y)
+
+        def last(self, body, extra, target):
+            self.to_y().wait_recv()
+            flat = pl.BlockSpec((1, slab, feats), lambda i: (i, 0, 0))
+            pltpu.emit_pipeline(
+                body,
+                grid=(own_rows // TILE,),
+                in_specs=[
+                    pl.BlockSpec((1, TILE, feats), lambda i: (y, i, 0)),
+                    pl.BlockSpec((TILE, feats), lambda i: (i, 0)),
+                    flat,
+                ],
+                out_specs=[flat],
+            )(self.half, self.from_y, extra, target)
+
+    out_scatter = Scatter(out_part, out_core, out_chip, out_x, out_half, out_y)
+    dx_scatter = Scatter(dx_part, dx_core, dx_chip, dx_x, dx_half, dx_y)
+    out_route = Route(
+        out_item, 4, out_up, out_down, out_far, out_send, out_edge, output
+    )
+
+    def finish_output():
+        def body(half_ref, y_ref, x_ref, item_ref):
+            item_ref[0] = (
+                half_ref[0].astype(F32)
+                + y_ref[...].astype(F32)
+                + x_ref[0].astype(F32)
+                + out_bias[0:1]
+            ).astype(BF16)
+
+        out_scatter.last(body, x_own, out_item)
+
+    def finish_grad():
+        def body(half_ref, y_ref, x_ref, target_ref):
+            target_ref[0] = half_ref[0].astype(F32) + y_ref[...].astype(F32)
+
+        dx_scatter.last(body, x_own, grad_norm)
+
+    x_gather.begin()
+    cot_route.begin()
+    norm_all[r] = norm_own[...]
+    for copy in norm_copies:
+        start(copy)
+    x_gather.after_y()
+    mlp_fetch[0].begin()
+    cot_route.relay()
+    x_gather.after_x()
+    cot_route.hand_out()
+    cot_route.take()
+    cot_gather = Gather(cot_own, cot_all)
+    cot_gather.begin()
+    mlp_fetch[1].begin()
+    x_gather.end()
+    for copy in norm_copies:
+        copy().wait_recv()
+    norm_stage()
+    cot_gather.after_y()
+    attn_fetch.begin()
+    cot_gather.after_x()
+    cot_gather.end()
+    mlp_fetch[0].end()
+    mlp_stage(0)
+    for unit in mlp_units[0]:
+        unit.send()
+    mlp_fetch[1].end()
+    mlp_stage(1)
+    for unit in mlp_units[0]:
+        unit.collect()
+    for unit in mlp_units[1]:
+        unit.send()
+    mlp_fetch[2].begin()
+    mlp_fetch[3].begin()
+    mlp_units[0][0].halve()
+    attn_fetch.end()
+    attention_stage()
+    for unit in mlp_units[1]:
+        unit.collect()
+    for unit in attn_units:
+        unit.send()
+    mlp_units[0][1].halve()
+    mlp_units[0][0].close()
+    mlp_units[1][0].halve()
+    mlp_units[0][1].close()
+    mlp_fetch[2].end()
+    mlp_stage(2)
+    for unit in attn_units:
+        unit.collect()
+    for unit in mlp_units[2]:
+        unit.send()
+    mlp_units[1][1].halve()
+    mlp_units[1][0].close()
+    mlp_fetch[3].end()
+    mlp_stage(3)
+    for unit in mlp_units[2]:
+        unit.collect()
+    for unit in mlp_units[3]:
+        unit.send()
+    attn_units[0].halve()
+    mlp_units[1][1].close()
+    out_stage()
+    out_scatter.begin()
+    dx_stage()
+    for unit in mlp_units[3]:
+        unit.collect()
+    attn_units[1].halve()
+    attn_units[0].close()
+    out_scatter.second()
+    dx_scatter.begin()
+    attn_units[2].halve()
+    attn_units[1].close()
+    out_scatter.third()
+    dx_scatter.second()
+    attn_units[3].halve()
+    attn_units[2].close()
+    finish_output()
+    out_route.begin()
+    dx_scatter.third()
+    mlp_units[2][0].halve()
+    attn_units[3].close()
+    out_route.relay()
+    finish_grad()
+    mlp_units[2][1].halve()
+    mlp_units[2][0].close()
+    out_route.hand_out()
+    mlp_units[3][0].halve()
+    mlp_units[2][1].close()
+    out_route.take()
+    mlp_units[3][1].halve()
+    mlp_units[3][0].close()
+    gain_q[...] = gain_acc[0]
+    bias_q[...] = gain_acc[1]
+    gain_f[...] = gain_acc[2]
+    bias_f[...] = gain_acc[3]
+    mlp_units[3][1].close()
+    for unit in sum(mlp_units, []) + attn_units:
+        unit.finish()
+    cot_route.finish()
+    out_route.finish()
+    for copy in sent:
+        copy().wait_send()
+
+
+def line_codes(sources, plane):
+    middle = (plane == 1) | (plane == 2)
+    own = sources[:, 0] * 0
+
+    def code(wanted):
+        up, down = plane - 1, plane + 1
+        coded = jnp.where(wanted == up, 1, jnp.where(wanted == down, 2, 3))
+        coded = jnp.where(middle, coded, 1)
+        return jnp.where(wanted == plane, own, coded)
+
+    take = lax.dynamic_index_in_dim(sources, plane, 1, keepdims=False)
+    hand = jnp.where(plane == 1, sources[:, 0], sources[:, 3])
+    return jnp.concatenate([code(take), code(hand)]).astype(jnp.int32)
+
+
+def dealt_layer(
+    layer_input,
+    lengths,
+    deal_table,
+    ln1_gain,
+    ln1_bias,
+    qkv_weight,
+    qkv_bias,
+    dense_weight,
+    dense_bias,
+    ln2_gain,
+    ln2_bias,
+    fc1_weight,
+    fc1_bias,
+    fc2_weight,
+    fc2_bias,
+    cotangent,
+):
+    plane = lax.axis_index("dp")
+    row = lax.axis_index("row")
+    col = lax.axis_index("col")
+    own_rows, feats = layer_input.shape
+    rows = 2 * own_rows
+    slab = own_rows // 2
+    qkv_cols = qkv_weight.shape[1]
+    qkv_here = qkv_cols // 4
+    attn_here = dense_weight.shape[0] // 4
+    hidden_cols = fc1_weight.shape[1]
+    hidden_here = hidden_cols // 4
+    first_cols = qkv_here + hidden_here
+    second_rows = attn_here + hidden_here
+
+    deal_here = lax.dynamic_slice_in_dim(deal_table, 2 * col, 2, 0)
+    undeal_here = jnp.argmax(
+        deal_here[:, None, :] == jnp.arange(4, dtype=jnp.int32)[None, :, None], axis=2
+    ).astype(jnp.int32)
+    codes = jnp.concatenate([line_codes(undeal_here, plane), line_codes(deal_here, plane)])
+    lengths_here = lax.dynamic_slice_in_dim(lengths, plane * 4, 4, 0)
+    positions = jnp.concatenate([segment_layout(lengths_here[s], slab)[1] for s in range(4)])
+    begins = jnp.tile(jnp.arange(slab, dtype=jnp.int32), 4) - positions
+    cos_table, sin_table = rotary_tables(positions)
+    lane = jnp.arange(HD)
+    cos_table = jnp.pad(cos_table, ((0, 0), (0, HD - ROT)), constant_values=1.0)
+    sin_table = jnp.pad(sin_table, ((0, 0), (0, HD - ROT)))
+    low_table = jnp.where(lane < ROT // 2, -sin_table, 0.0)
+    high_table = jnp.where(lane < ROT // 2, 0.0, sin_table)
+    begins = jnp.broadcast_to(begins[:, None], (rows, HD))
+    norms = jnp.stack([ln1_gain, ln1_bias, ln2_gain, ln2_bias])
+    norms = jnp.concatenate([norms, norms])
+    bias_here = jnp.concatenate(
+        [
+            lax.dynamic_slice_in_dim(qkv_bias, row * qkv_here, qkv_here, 0),
+            lax.dynamic_slice_in_dim(fc1_bias, row * hidden_here, hidden_here, 0),
+        ]
+    )
+    bias_here = jnp.broadcast_to(bias_here[None], (8, first_cols))
+    out_bias = jnp.broadcast_to((dense_bias + fc2_bias)[None], (8, feats))
+
+    low = lambda *shape: jax.ShapeDtypeStruct(shape, BF16)
+    wide = lambda *shape: jax.ShapeDtypeStruct(shape, F32)
+    first = low(4, feats, first_cols)
+    second = low(4, second_rows, feats)
+    item = low(2, slab, feats)
+    outputs = [first, second, item, wide(2, slab, feats), item, wide(rows, 128)]
+    in_vmem = [wide(D, 128)] * 4 + [wide(8, first_cols)]
+    scatter = [
+        low(4, rows, feats),
+        low(2, rows, feats),
+        low(2, rows, feats),
+        low(2, own_rows, feats),
+        low(2, own_rows, feats),
+        low(own_rows, feats),
+    ]
+    buffers = (
+        [low(4, 4, slab, feats)] * 2
+        + [low(rows, D)] * 2
+        + [first, second, low(rows, second_rows), low(rows, first_cols)]
+        + [first, second] * 5
+        + scatter
+        + [item]
+        + scatter
+        + [item] * 10
+    )
+    any_space = pl.BlockSpec(memory_space=pl.ANY)
+    vmem = pl.BlockSpec(memory_space=pltpu.VMEM)
+    copies = 150
+    results = pl.pallas_call(
+        layer_kernel,
+        in_specs=[pl.BlockSpec(memory_space=pltpu.SMEM)]
+        + [any_space] * 2
+        + [vmem] * 3
+        + [any_space] * 8,
+        out_specs=[any_space] * len(outputs)
+        + [vmem] * len(in_vmem)
+        + [any_space] * len(buffers),
+        out_shape=outputs + in_vmem + buffers,
+        scratch_shapes=[
+            pltpu.VMEM((4, UNIT + qkv_here, feats), F32),
+            pltpu.VMEM((4, 8, feats), F32),
+            pltpu.VMEM((4, D, 128), F32),
+            pltpu.VMEM((8, qkv_here), F32),
+            pltpu.SemaphoreType.DMA((copies,)),
+            pltpu.SemaphoreType.DMA((copies,)),
+            pltpu.SemaphoreType.DMA((32,)),
+        ],
+        compiler_params=pltpu.CompilerParams(
+            collective_id=0, has_side_effects=True, vmem_limit_bytes=60 * 1024 * 1024
+        ),
+        cost_estimate=pl.CostEstimate(
+            flops=6 * rows * D * (first_cols + second_rows),
+            bytes_accessed=200 * 1024 * 1024,
+            transcendentals=rows * hidden_here,
+        ),
+    )(
+        codes,
+        layer_input.reshape(2, slab, feats),
+        cotangent.reshape(2, slab, feats),
+        norms,
+        bias_here,
+        out_bias,
+        qkv_weight,
+        dense_weight,
+        fc1_weight,
+        fc2_weight,
+        cos_table,
+        low_table,
+        high_table,
+        begins,
+    )
+    first_sum, second_sum, output, grad_norm, cot_own, stats = results[:6]
+    gain1, bias1, gain2, bias2 = [jnp.sum(part, axis=1) for part in results[6:10]]
+    unit_sums = results[10][0]
+    output = output.reshape(own_rows, feats)
+
+    def first_grad(part):
+        return part.transpose(1, 0, 2).reshape(feats, -1).astype(F32)
+
+    def second_grad(part):
+        return part.reshape(-1, feats).astype(F32)
+
+    qkv_grad = first_grad(first_sum[:, :, :qkv_here])
+    fc1_grad = first_grad(first_sum[:, :, qkv_here:])
+    dense_grad = second_grad(second_sum[:, :attn_here])
+    fc2_grad = second_grad(second_sum[:, attn_here:])
+
+    stats_own = lax.dynamic_slice_in_dim(stats, col * own_rows, own_rows, 0)
+    mean, inv_std = stats_own[:, :1], stats_own[:, 127:]
+    normed_own = (layer_input.astype(F32) - mean) * inv_std
+    grad_normed = grad_norm.reshape(own_rows, feats)
+    row_sums = lax.psum(
+        (jnp.sum(grad_normed, axis=1), jnp.sum(grad_normed * normed_own, axis=1)), "row"
+    )
+    input_grad = cot_own.reshape(own_rows, feats).astype(F32) + inv_std * (
+        grad_normed - row_sums[0][:, None] / D - normed_own * row_sums[1][:, None] / D
+    )
+
+    norm_sums = jnp.stack([gain1, bias1, gain2, bias2])
+    bias_part = jnp.sum(cotangent, axis=0, dtype=F32)
+    bias_sum = jnp.zeros((4, feats), F32).at[row].set(bias_part)
+    qkv_sums = jnp.zeros((2, 4, qkv_here), F32).at[col, row].set(unit_sums[:qkv_here])
+    hidden_sums = jnp.zeros((2, 4, hidden_here), F32).at[col, row].set(unit_sums[qkv_here:])
+    small = lax.psum(
+        jnp.concatenate(
+            [
+                norm_sums.reshape(-1),
+                bias_sum.reshape(-1),
+                qkv_sums.reshape(-1),
+                hidden_sums.reshape(-1),
+            ]
+        ),
+        ("dp", "row", "col"),
+    )
+    norm_sums, bias_sum, qkv_sums, hidden_sums = jnp.split(
+        small, [4 * D, 5 * D, 5 * D + 2 * qkv_cols]
+    )
+    norm_sums = lax.dynamic_index_in_dim(norm_sums.reshape(4, 4, feats), row, 1, keepdims=False)
+    bias_sum = lax.dynamic_index_in_dim(bias_sum.reshape(4, feats), row, 0, keepdims=False)
+    qkv_bias_grad = lax.dynamic_index_in_dim(qkv_sums.reshape(2, qkv_cols), col, 0, keepdims=False)
+    fc1_bias_grad = lax.dynamic_index_in_dim(
+        hidden_sums.reshape(2, hidden_cols), col, 0, keepdims=False
+    )
+    gain1 = (norm_sums[0] - ln1_bias * norm_sums[1]) / ln1_gain
+    gain2 = (norm_sums[2] - ln2_bias * norm_sums[3]) / ln2_gain
+    return (
+        output,
+        input_grad,
+        gain1,
+        norm_sums[1],
+        qkv_grad,
+        qkv_bias_grad,
+        dense_grad,
+        bias_sum,
+        gain2,
+        norm_sums[3],
+        fc1_grad,
+        fc1_bias_grad,
+        fc2_grad,
+        bias_sum,
+    )
+
+
 def solution(mesh):
+    grid = tuple(mesh.shape[axis] for axis in ("dp", "row", "col"))
     placed = (
         P(("dp", "col"), "row"),
         P(),
@@ -320,7 +1406,7 @@
         P(("dp", "col"), "row"),
     )
     return jax.shard_map(
-        local,
+        dealt_layer if grid == (4, 4, 2) else local,
         mesh=mesh,
         in_specs=placed,
         out_specs=(

time: 2460 us -> 817 us (0.33)
  waiting for transfers between devices: 1940 us -> 51.7 us
  Pallas kernels: 0 us -> 635 us
  matrix products: 183 us -> 0 us
  other arithmetic: 187 us -> 41.8 us
  blocking collectives: 64.3 us -> 10.6 us
    psum x1, waiting for transfers between devices: 834 us -> 51.7 us  [dealt_layer(): lax.psum(jnp.concatenate([norm_sums.reshape(-1), bias_sum.reshape(-1), qk...]
    reduce_scatter x4 -> x0, waiting for transfers between devices: 669 us -> none  [the longest x1 395 us: local(): lax.psum_scatter(jnp.concatenate([jnp.dot(part_one, qkv_weight, preferred...]
    pallas_call x0 -> x1, Pallas kernels: none -> 635 us  [dealt_layer(): pl.pallas_call(layer_kernel, in_specs=[pl.BlockSpec(memory_space=pltpu.SM...]
    all_gather x7 -> x0, waiting for transfers between devices: 440 us -> none  [the longest x1 158 us: local(): grad_first_all = lax.all_gather(grad_first, 'row', axis=0, tiled=True)]
    dot_general x18 -> x0, matrix products: 183 us -> none  [the longest x4 49 us: contract_rows(): lax.dot_general(left_side, right_side, (((0,), (0,)), ((), ())), preferre...]
    concatenate x4 -> x3, other arithmetic: 78.4 us -> 1.25 us  [the longest x1 0.65 us: dealt_layer(): jnp.concatenate([norm_sums.reshape(-1), bias_sum.reshape(-1), qkv_sums.re...]
    psum x4 -> x1, blocking collectives: 64.3 us -> 10.6 us  [dealt_layer(): lax.psum((jnp.sum(grad_normed, axis=1), jnp.sum(grad_normed * normed_own,...]
    reduce_sum x10 -> x7, other arithmetic: 35.5 us -> 7.77 us  [the longest x4 5.04 us: dealt_layer(): jnp.sum(part, axis=1)]
  transfers between devices with their start and end apart: 12 -> 1, of which waited for: 11 -> 1; matrix products, arithmetic and copies ran while one was open for 12% -> 8% of each run, Pallas kernels for 0% -> 0%
where the time goes in v2:
time: 817 us; the launch traced here: 805 us
  Pallas kernels  635 us (78%)
  waiting for transfers between devices  51.7 us (6%)
  local copies, waits for them, and re-layouts  50.2 us (6%)
  other arithmetic  41.8 us (5%)
  between operations  14.9 us (2%)
  blocking collectives  10.6 us (1%)
    pallas_call x1, Pallas kernels, dealt_layer(): pl.pallas_call(layer_kernel, in_specs=[pl.BlockSpec(memory_space=pltpu.SM...  635 us
    psum x1, waiting for transfers between devices, dealt_layer(): lax.psum(jnp.concatenate([norm_sums.reshape(-1), bias_sum.reshape(-1), qk...  51.7 us
    unnamed x50, local copies, waits for them, and re-layouts  18.2 us
  transfers between devices with their start and end apart: 1, of which 1 were waited for; matrix products, arithmetic and copies ran while one was open for 8% of the time, Pallas kernels for 0%

profile of v2, /device:TPU:0, one launch (start us, length us, event | category | flops | bytes accessed | tf_op | source)
XLA Modules:
  0.0 804.6 jit_solution(18329893162810477539)
XLA Ops:
  10.0 1.0 fusion.3
  13.0 1.5 pad_select_fusion
  14.5 1.0 pad.16.cos_in
  15.5 0.8 dynamic_slice.41
  18.7 0.7 and_reduce_fusion
  19.4 1.3 broadcast_in_dim.157.begin_in
  21.9 635.3 %shard_map.263 = (bf16[4,512,1792]{2,1,0:T(8,128)(2,1)}, bf16[4,1280,512]{2,1,0:T(8,128)(2,1)}, bf16[2,512,512]{2,1,0:T(8,128)(2,1)}, f32[2,512,512]{2,1,0:T(8,1...) custom-call(s32[8]{0:T(128)} %pad_add_fusion.1.codes, ...), custom_call_target="tpu_custom_call" | custom-call | flops 77309411328 | bytes 209715200 | tf_op jit(solution)/shard_map/pallas_call | solution.py:1273
  657.2 1.5 fusion.7
  658.7 1.4 fusion.8
  660.3 1.6 reduce_sum.148
  661.9 1.6 reduce_sum.149
  663.5 1.6 reduce_sum.150
  665.7 0.7 and_reduce_fusion.1
  668.1 6.6 convert_bitcast_fusion
  674.7 5.2 convert_bitcast_fusion.1
  679.9 2.5 slice.167
  682.3 1.3 slice.163
  683.6 4.9 bitcast_convert_fusion
  688.8 1.7 dynamic-slice_reduce_fusion.1
  690.5 2.3 fusion.2
  692.8 10.6 %all-reduce.2 = (f32[1024]{0:T(1024)S(1)}, f32[1024]{0:T(1024)S(1)}) all-reduce(f32[1024]{0:T(1024)S(1)} %fusion.2, f32[1024]{0:T(1024)S(1)} %bitcast.120), channel_id=1, replica_groups=mesh['dp'=4,'row'=4,'col'=2] {'row'}, use_global_device_ids=true, to_apply=%region_16.17 | all-reduce | flops 2048 | bytes 16384 | tf_op jit(solution)/shard_map/psum | solution.py:1336
  703.4 3.2 convert_add_fusion
  706.7 1.7 bitcast_convert_fusion.1
  708.3 8.7 %copy.61 = f32[512,4,1024]{0,2,1:T(8,128)} copy(f32[512,4,1024]{2,0,1:T(8,128)} %convert_bitcast_fusion) | data formatting | bytes 16777216 | tf_op jit(solution)/shard_map/convert_element_type | solution.py:1322
  717.1 8.9 %copy.63 = f32[512,4096]{1,0:T(8,128)} copy(f32[512,4096]{0,1:T(8,128)} %bitcast.95) | data formatting | bytes 16777216
  726.0 6.6 copy.60
  732.6 6.7 copy.62
  739.3 51.7 %all-reduce.5.cloned.1.call-done = f32[24576]{0:T(1024)} async-done(((f32[24576]{0:T(1024)}), f32[24576]{0:T(1024)}) %all-reduce.5.cloned.1.call-update) | async-done | bytes 98320 | tf_op jit(solution)/shard_map/psum | solution.py:1348
  791.0 0.8 fusion.21
  792.4 0.7 split.26
  793.8 0.7 split.27
  796.3 1.0 copy.81
  (110 shorter events, 14.0 us)
Async XLA Ops:
  7.2 0.7 copy-start
  7.2 783.8 %all-reduce.5.cloned.1.call-start = ((), (), s32[]{:S(2)}) async-start(), calls=%async_computation | async-start | bytes 196608 | tf_op jit(solution)/shard_map/psum | solution.py:1348
  9.9 7.1 copy-start.13
  9.9 7.1 copy-start.14
  10.0 7.2 copy-start.15
  10.0 8.1 %copy-start.6 = (f32[512]{0:T(512)S(1)}, f32[512]{0:T(512)}, u32[]{:S(2)}) copy-start(f32[512]{0:T(512)} %param.31) | copy-start | bytes 6148
  10.0 8.0 %copy-start.7 = (f32[512]{0:T(512)S(1)}, f32[512]{0:T(512)}, u32[]{:S(2)}) copy-start(f32[512]{0:T(512)} %param.32) | copy-start | bytes 6148
  10.0 8.0 copy-start.8
  10.0 8.0 copy-start.9
  10.0 8.7 %copy-start.16 = (s32[3]{0:T(128)S(1)}, s32[3]{0:T(128)}, u32[]{:S(2)}) copy-start(s32[3]{0:T(128)} %constant.163.clone.1) | copy-start | bytes 40
  21.9 638.2 %copy-start.3 = (bf16[1024,512]{1,0:T(8,128)(2,1)S(1)}, bf16[1024,512]{1,0:T(8,128)(2,1)}, u32[]{:S(2)}) copy-start(bf16[1024,512]{1,0:T(8,128)(2,1)} %param.37) | copy-start | bytes 3145732
  657.2 7.8 copy-start.5
  657.2 8.5 %copy-start.17 = (s32[2]{0:T(128)S(1)}, s32[2]{0:T(128)}, u32[]{:S(2)}) copy-start(s32[2]{0:T(128)} %constant.161.clone.1) | copy-start | bytes 28
  683.6 4.9 copy-start.2
  732.6 63.7 %copy-start.4 = (bf16[2,512,512]{2,1,0:T(8,128)(2,1)S(1)}, bf16[2,512,512]{2,1,0:T(8,128)(2,1)}, u32[]{:S(2)}) copy-start(bf16[2,512,512]{2,1,0:T(8,128)(2,1)} %get-tuple-element.63) | copy-start | bytes 3145732
  732.6 64.7 %copy-start.1 = (s32[16,4]{0,1:T(4,128)S(1)}, s32[16,4]{0,1:T(4,128)}, u32[]{:S(2)}) copy-start(s32[16,4]{0,1:T(4,128)} %param.23) | copy-start | bytes 772
  794.5 2.8 copy-start.12
  794.5 2.8 copy-start.10
  794.5 2.7 copy-start.11
Sparse Core Ops, SparseCore 0:
  668.2 122.7 all-reduce.4

commit v3 on v2

--- a/solution.py
+++ b/solution.py
@@ -3,6 +3,7 @@
 
 import jax
 import jax.numpy as jnp
+import numpy as np
 from jax import lax
 from jax.experimental import pallas as pl
 from jax.experimental.pallas import tpu as pltpu
@@ -373,31 +374,27 @@
 
 
 def layer_kernel(
-    codes,
+    lengths,
+    deal_table,
     x_own,
     cot_in,
     norm_own,
-    bias_in,
+    qkv_bias,
+    fc1_bias,
     out_bias,
+    turns,
     qkv_w,
     dense_w,
     fc1_w,
     fc2_w,
-    cos_in,
-    low_in,
-    high_in,
-    begin_in,
     first_sum,
     second_sum,
     output,
+    input_grad,
+    small_sum,
     grad_norm,
     cot_own,
     stats,
-    gain_q,
-    bias_q,
-    gain_f,
-    bias_f,
-    unit_sums,
     x_all,
     cot_all,
     ln1,
@@ -443,6 +440,17 @@
     norm_all,
     gain_acc,
     sum_acc,
+    unit_sums,
+    small_part,
+    small_row,
+    small_units,
+    small_col,
+    small_here,
+    small_in,
+    small_half,
+    small_other,
+    row_part,
+    row_sums,
     send_sems,
     recv_sems,
     local_sems,
@@ -510,117 +518,165 @@
     far_half = pl.ds((1 - c) * own_rows, own_rows)
 
     class Gather:
-        def __init__(self, own, whole):
-            self.whole = whole
-            block = lambda j, half: whole.at[peer[j], pl.ds(slabs * half, slabs)]
-            self.to_y = copies.make(lambda: own, lambda: block(0, c), to_row[2])
-            self.to_x = copies.make(lambda: own, lambda: block(0, c), to_col)
-            self.to_core = copies.make(lambda: own, lambda: block(0, c), to_row[1])
-            self.y_to_x = copies.make(lambda: block(2, c), lambda: block(2, c), to_col)
-            self.y_to_core = copies.make(
-                lambda: block(2, c), lambda: block(2, c), to_row[1]
+        def __init__(self, own, whole, by_row):
+            self.own, self.whole = own, whole
+
+            def place(j, half, q):
+                return lambda: whole.at[peer[j], slabs * half + q]
+
+            def own_slab(q):
+                return lambda: own.at[q]
+
+            ids = range(slabs)
+            self.to_y = [copies.make(own_slab(q), place(0, c, q), to_row[2]) for q in ids]
+            self.to_x = [copies.make(own_slab(q), place(0, c, q), to_col) for q in ids]
+            self.to_core = [copies.make(own_slab(q), place(0, c, q), to_row[1]) for q in ids]
+            self.y_core = [copies.make(place(2, c, q), place(2, c, q), to_row[1]) for q in ids]
+            self.x_core = [
+                copies.make(place(0, 1 - c, q), place(0, 1 - c, q), to_row[1]) for q in ids
+            ]
+            self.far_core = [
+                copies.make(place(2, 1 - c, q), place(2, 1 - c, q), to_row[1]) for q in ids
+            ]
+            self.by_row = by_row
+            self.far = [
+                copies.make(place(0, 1 - c, q), place(0, 1 - c, q), to_row[2])
+                if q in by_row
+                else copies.make(place(2, c, q), place(2, c, q), to_col)
+                for q in ids
+            ]
+            self.kept = [None] * slabs
+
+        def begin(self, q):
+            start(self.to_y[q])
+            start(self.to_x[q])
+            start(self.to_core[q])
+            self.kept[q] = local(
+                lambda: self.own.at[q], lambda: self.whole.at[r, slabs * c + q]
             )
-            self.x_to_core = copies.make(
-                lambda: block(0, 1 - c), lambda: block(0, 1 - c), to_row[1]
-            )
-            self.xy_to_core = copies.make(
-                lambda: block(2, 1 - c), lambda: block(2, 1 - c), to_row[1]
-            )
-            self.own = own
-
-        def begin(self):
-            start(self.to_y)
-            start(self.to_x)
-            start(self.to_core)
-            self.kept = local(lambda: self.own, lambda: self.whole.at[r, pl.ds(slabs * c, slabs)])
-
-        def after_y(self):
-            self.to_y().wait_recv()
-            start(self.y_to_x)
-            start(self.y_to_core)
-
-        def after_x(self):
-            self.to_x().wait_recv()
-            start(self.x_to_core)
-            self.y_to_x().wait_recv()
-            start(self.xy_to_core)
-
-        def end(self):
-            self.kept().wait()
-            for copy in (self.to_core, self.y_to_core, self.x_to_core, self.xy_to_core):
-                copy().wait_recv()
-
-    def choose(code_at, refs, target):
+
+        def after_y(self, q):
+            self.to_y[q]().wait_recv()
+            if q not in self.by_row:
+                start(self.far[q])
+            start(self.y_core[q])
+
+        def after_x(self, q):
+            self.to_x[q]().wait_recv()
+            if q in self.by_row:
+                start(self.far[q])
+            start(self.x_core[q])
+
+        def after_far(self, q):
+            self.far[q]().wait_recv()
+            start(self.far_core[q])
+
+        def end(self, q):
+            self.kept[q]().wait()
+            for group in (self.to_core, self.y_core, self.x_core, self.far_core):
+                group[q]().wait_recv()
+
+    def choose(q, goes, plane, refs, target):
         def body(*blocks):
-            code = codes[code_at + pl.program_id(0)]
             value = blocks[0][...]
-            for which in range(1, len(refs)):
-                value = jnp.where(code == which, blocks[which][...], value)
+            for (source, _), block in zip(refs[1:], blocks[1:]):
+                value = jnp.where(goes(q, source, plane), block[...], value)
             blocks[-1][...] = value
 
-        block = pl.BlockSpec((1, slab, feats), lambda q: (q, 0, 0))
+        tile = slab // 4
+        block = pl.BlockSpec((tile, feats), lambda i: (i, 0))
         pltpu.emit_pipeline(
-            body, grid=(2,), in_specs=[block] * len(refs), out_specs=[block]
-        )(*refs, target)
+            body, grid=(4,), in_specs=[block] * len(refs), out_specs=[block]
+        )(*[ref.at[q] for _, ref in refs], target.at[q])
 
     class Route:
-        def __init__(self, item, code_at, up, down, far, send, edge, target):
-            self.item, self.code_at, self.up, self.down = item, code_at, up, down
+        def __init__(self, item, goes, up, down, far, send, edge, target):
+            self.item, self.goes, self.up, self.down = item, goes, up, down
             self.far, self.send, self.edge, self.target = far, send, edge, target
-            self.upward = copies.make(lambda: item, lambda: up, {"dp": z + 1})
-            self.downward = copies.make(lambda: item, lambda: down, {"dp": z - 1})
-            self.far_up = copies.make(lambda: up, lambda: far, to_in)
-            self.far_down = copies.make(lambda: down, lambda: far, to_in)
-            self.outward = copies.make(lambda: send, lambda: edge, to_out)
-
-        def begin(self):
-            when(z < 2, lambda: self.upward().start())
-            when(z > 1, lambda: self.downward().start())
-
-        def relay(self):
+
+            def at(ref, q):
+                return lambda: ref.at[q]
+
+            ids = range(slabs)
+            self.upward = [copies.make(at(item, q), at(up, q), {"dp": z + 1}) for q in ids]
+            self.downward = [copies.make(at(item, q), at(down, q), {"dp": z - 1}) for q in ids]
+            self.far_up = [copies.make(at(up, q), at(far, q), to_in) for q in ids]
+            self.far_down = [copies.make(at(down, q), at(far, q), to_in) for q in ids]
+            self.outward = [copies.make(at(send, q), at(edge, q), to_out) for q in ids]
+
+        def begin(self, q):
+            when(z < 2, lambda: self.upward[q]().start())
+            when(z > 1, lambda: self.downward[q]().start())
+
+        def relay(self, q):
             def from_below():
-                self.upward().wait_recv()
-                self.far_up().start()
-                self.downward().wait_recv()
+                self.upward[q]().wait_recv()
+                self.far_up[q]().start()
 
             def from_above():
-                self.downward().wait_recv()
-                self.far_down().start()
-                self.upward().wait_recv()
+                self.downward[q]().wait_recv()
+                self.far_down[q]().start()
 
             when(z == 1, from_below)
             when(z == 2, from_above)
 
-        def hand_out(self):
+        def hand_out(self, q):
             def middle():
-                when(z == 1, lambda: self.far_down().wait_recv())
-                when(z == 2, lambda: self.far_up().wait_recv())
-                choose(
-                    self.code_at + 2, [self.item, self.up, self.down, self.far], self.send
-                )
-                self.outward().start()
-                choose(self.code_at, [self.item, self.up, self.down, self.far], self.target)
+                def below():
+                    self.downward[q]().wait_recv()
+                    self.far_down[q]().wait_recv()
+
+                def above():
+                    self.upward[q]().wait_recv()
+                    self.far_up[q]().wait_recv()
+
+                when(z == 1, below)
+                when(z == 2, above)
+                refs = [
+                    (z, self.item),
+                    (z - 1, self.up),
+                    (z + 1, self.down),
+                    (3 * (2 - z), self.far),
+                ]
+                choose(q, self.goes, z_out, refs, self.send)
+                self.outward[q]().start()
+                choose(q, self.goes, z, refs, self.target)
 
             when(is_mid, middle)
 
-        def take(self):
+        def take(self, q):
             def edge():
-                self.outward().wait_recv()
-                choose(self.code_at, [self.item, self.edge], self.target)
+                self.outward[q]().wait_recv()
+                block = pl.BlockSpec((slab // 4, feats), lambda i: (i, 0))
+
+                def body(edge_ref, item_ref, target_ref):
+                    mine = self.goes(q, z, z)
+                    target_ref[...] = jnp.where(mine, item_ref[...], edge_ref[...])
+
+                pltpu.emit_pipeline(
+                    body, grid=(4,), in_specs=[block] * 2, out_specs=[block]
+                )(self.edge.at[q], self.item.at[q], self.target.at[q])
 
             when(is_edge, edge)
 
         def finish(self):
-            when(z < 2, lambda: self.upward().wait_send())
-            when(z > 1, lambda: self.downward().wait_send())
-            when(z == 1, lambda: self.far_up().wait_send())
-            when(z == 2, lambda: self.far_down().wait_send())
-            when(is_mid, lambda: self.outward().wait_send())
-
-    x_gather = Gather(x_own, x_all)
-    cot_slabs = cot_in
+            for q in range(slabs):
+                when(z < 2, lambda: self.upward[q]().wait_send())
+                when(z > 1, lambda: self.downward[q]().wait_send())
+                when(z == 1, lambda: self.far_up[q]().wait_send())
+                when(z == 2, lambda: self.far_down[q]().wait_send())
+                when(is_mid, lambda: self.outward[q]().wait_send())
+
+    def undealt(q, source, plane):
+        return deal_table[slabs * c + q, source] == plane
+
+    def dealt(q, source, plane):
+        return deal_table[slabs * c + q, plane] == source
+
+    x_gather = Gather(x_own, x_all, ())
+    cot_gather = Gather(cot_own, cot_all, (1,))
     cot_route = Route(
-        cot_slabs, 0, cot_up, cot_down, cot_far, cot_send, cot_edge, cot_own
+        cot_in, undealt, cot_up, cot_down, cot_far, cot_send, cot_edge, cot_own
     )
     norm_copies = [
         copies.make(lambda: norm_own, lambda: norm_all.at[r], to_row[j]) for j in (1, 2, 3)
@@ -673,13 +729,9 @@
             self.kind, self.at = kind, at
             if kind == 1:
                 self.view = lambda ref, s: ref.at[s, :, pl.ds(at, UNIT)]
-                self.whole = lambda ref: ref.at[:, :, pl.ds(at, UNIT)]
-                self.block = pl.BlockSpec((1, feats, UNIT), lambda s: (s, 0, at // UNIT))
                 self.refs = (first_part, first_here, first_in, first_half, first_other, first_sum)
             else:
                 self.view = lambda ref, s: ref.at[s, pl.ds(at, UNIT)]
-                self.whole = lambda ref: ref.at[:, pl.ds(at, UNIT)]
-                self.block = pl.BlockSpec((1, UNIT, feats), lambda s: (s, at // UNIT, 0))
                 self.refs = (
                     second_part,
                     second_here,
@@ -697,60 +749,92 @@
                 )
                 for j in (1, 2, 3)
             ]
-            self.inward = copies.make(lambda: self.whole(here), lambda: self.whole(arrived), to_in)
-            self.across = copies.make(lambda: self.whole(half), lambda: self.whole(other), to_in)
-            self.outward = copies.make(lambda: self.whole(total), lambda: self.whole(total), to_out)
-
-        def send(self):
+            def half_of(ref, which):
+                first_slot = 2 * (y if which == 0 else 1 - y)
+                if kind == 1:
+                    return ref.at[pl.ds(first_slot, 2), :, pl.ds(at, UNIT)]
+                return ref.at[pl.ds(first_slot, 2), pl.ds(at, UNIT)]
+
+            def half_copy(source, target, which, device):
+                return copies.make(
+                    lambda: half_of(source, which), lambda: half_of(target, which), device
+                )
+
+            self.inward = [half_copy(here, arrived, which, to_in) for which in (0, 1)]
+            self.across = [half_copy(half, other, which, to_in) for which in (0, 1)]
+            self.outward = [half_copy(total, total, which, to_out) for which in (0, 1)]
+
+        def send(self, which):
             part, here = self.refs[:2]
-            for copy in self.spread:
-                start(copy)
-            self.kept = local(lambda: self.view(part, r), lambda: self.view(here, r))
-
-        def collect(self):
-            for copy in self.spread:
-                copy().wait_recv()
-            self.kept().wait()
-            when(is_edge, lambda: self.inward().start())
-
-        def add(self, left, right, target):
+            if which == 0:
+                start(self.spread[0])
+                self.kept = local(lambda: self.view(part, r), lambda: self.view(here, r))
+            else:
+                self.spread[1]().start()
+                self.spread[2]().start()
+
+        def sent_far(self):
+            self.spread[1]().wait_send()
+            self.spread[2]().wait_send()
+
+        def collect(self, which):
+            if which == 0:
+                self.spread[0]().wait_recv()
+                self.kept().wait()
+            else:
+                self.spread[1]().wait_recv()
+                self.spread[2]().wait_recv()
+
+        def add(self, which, left, right, target):
+            first_slot = 2 * (y if which == 0 else 1 - y)
+            if self.kind == 1:
+                block = pl.BlockSpec(
+                    (1, feats, UNIT), lambda s: (first_slot + s, 0, self.at // UNIT)
+                )
+            else:
+                block = pl.BlockSpec(
+                    (1, UNIT, feats), lambda s: (first_slot + s, self.at // UNIT, 0)
+                )
+
             def body(left_block, right_block, target_block):
                 target_block[...] = (
                     left_block[...].astype(F32) + right_block[...].astype(F32)
                 ).astype(BF16)
 
-            pltpu.emit_pipeline(
-                body, grid=(4,), in_specs=[self.block] * 2, out_specs=[self.block]
-            )(left, right, target)
-
-        def halve(self):
+            pltpu.emit_pipeline(body, grid=(2,), in_specs=[block] * 2, out_specs=[block])(
+                left, right, target
+            )
+
+        def halve(self, which):
             part, here, arrived, half, other, total = self.refs
 
             def middle():
-                self.inward().wait_recv()
-                self.add(here, arrived, half)
-                self.across().start()
+                self.collect(which)
+                self.inward[which]().wait_recv()
+                self.add(which, here, arrived, half)
+                self.across[which]().start()
 
             when(is_mid, middle)
 
-        def close(self):
+        def close(self, which):
             part, here, arrived, half, other, total = self.refs
 
             def middle():
-                self.across().wait_recv()
-                self.add(half, other, total)
-                self.outward().start()
+                self.across[which]().wait_recv()
+                self.add(which, half, other, total)
+                self.outward[which]().start()
 
             when(is_mid, middle)
 
-        def finish(self):
+        def finish(self, which, unsent):
             def edge():
-                self.outward().wait_recv()
-                self.inward().wait_send()
+                self.outward[which]().wait_recv()
+                if unsent:
+                    self.inward[which]().wait_send()
 
             def middle():
-                self.across().wait_send()
-                self.outward().wait_send()
+                self.across[which]().wait_send()
+                self.outward[which]().wait_send()
 
             when(is_edge, edge)
             when(is_mid, middle)
@@ -788,7 +872,7 @@
 
     def mlp_stage(k):
         at = k * UNIT
-        bias = bias_in[0:1, qkv_here + at : qkv_here + at + UNIT]
+        bias = fc1_bias[r, :, at : at + UNIT]
 
         def body(ln_ref, cot_ref, first_ref, second_ref, act_ref, grad_ref):
             step = pl.program_id(0)
@@ -832,7 +916,7 @@
             ],
         )(ln2, cot_all, w1, w2, acts, grads)
         grad_stage(UNIT, qkv_here + at, attn_here + at, 1, k == 0)
-        unit_sums[:, qkv_here + at : qkv_here + at + UNIT] = sum_acc[:, :UNIT]
+        unit_sums[0:1, qkv_here + at : qkv_here + at + UNIT] = sum_acc[0:1, :UNIT]
 
     def grad_stage(width, first_at, second_at, which, fresh):
         def body(first_ref, part_one, part_two):
@@ -860,20 +944,11 @@
             out_specs=[block, pl.BlockSpec((1, UNIT, feats), lambda j: (j, second_at // UNIT, 0))],
         )(w1.at[:, :, lanes], first_part.at[:, :, lanes], second_part)
 
-    def attention_stage():
+    def attention_slab(s):
         heads = qkv_here // (3 * HD)
-        bias = bias_in[0:1, :qkv_here]
-
-        def body(
-            ln_ref, cot_ref, first_ref, second_ref, cos, low, high, begin, act_ref, grad_ref
-        ):
-            step = pl.program_id(0)
-
-            @pl.when(step == 0)
-            def _():
-                acc[...] = jnp.zeros(acc.shape, F32)
-                sum_acc[...] = jnp.zeros(sum_acc.shape, F32)
-
+        bias = qkv_bias[r]
+
+        def body(ln_ref, cot_ref, first_ref, second_ref, act_ref, grad_ref):
             qkv = bias
             back = None
             for j in range(4):
@@ -884,14 +959,25 @@
             back = back.astype(BF16)
             at = lax.broadcasted_iota(jnp.int32, (TILE, TILE), 0)
             of = lax.broadcasted_iota(jnp.int32, (TILE, TILE), 1)
+            token = lax.broadcasted_iota(jnp.int32, (TILE, HD), 0)
+            lane = lax.broadcasted_iota(jnp.int32, (TILE, HD), 1)
+            begin = jnp.zeros((TILE, HD), jnp.int32)
+            edge = 0
+            for k in range(lengths.shape[1] - 1):
+                edge = edge + lengths[4 * z + s, k]
+                begin = jnp.where(token >= edge, edge, begin)
             allowed = (of <= at) & (of >= begin[:, :1])
+            angle = (token - begin).astype(F32) * turns[0:1]
+            cos, sin = jnp.cos(angle), jnp.sin(angle)
+            low = jnp.where(lane < ROT // 2, -sin, 0.0)
+            high = jnp.where(lane < ROT // 2, 0.0, sin)
             for h in range(heads):
                 attn, grads_here = attention_head(
                     qkv[:, h * 3 * HD : (h + 1) * 3 * HD],
                     back[:, h * HD : (h + 1) * HD],
-                    cos[...],
-                    low[...],
-                    high[...],
+                    cos,
+                    low,
+                    high,
                     allowed,
                 )
                 act_ref[:, h * HD : (h + 1) * HD] = attn
@@ -899,74 +985,69 @@
                     at_lane = (h * 3 + i) * HD
                     grad_ref[:, at_lane : at_lane + HD] = grads_here[i].astype(BF16)
             attn, grad = act_ref[...], grad_ref[...]
-            sum_acc[0:1, :qkv_here] += jnp.sum(grad.astype(F32), axis=0, keepdims=True)
+            sums = jnp.sum(grad.astype(F32), axis=0, keepdims=True)
+            sum_acc[0:1, :qkv_here] = sums if s == 0 else sum_acc[0:1, :qkv_here] + sums
             for j in range(4):
                 lanes = slice(j * feats, (j + 1) * feats)
-                acc[j, :UNIT] += product(attn, cot_ref[j, 0], ((0,), (0,)))
-                acc[j, UNIT:] += product(grad, ln_ref[:, lanes], ((0,), (0,)))
-
-        table = pl.BlockSpec((TILE, HD), lambda i: (i, 0))
+                second_term = product(attn, cot_ref[j, 0], ((0,), (0,)))
+                first_term = product(grad, ln_ref[:, lanes], ((0,), (0,)))
+                acc[j, :UNIT] = second_term if s == 0 else acc[j, :UNIT] + second_term
+                acc[j, UNIT:] = first_term if s == 0 else acc[j, UNIT:] + first_term
+
         pltpu.emit_pipeline(
             body,
-            grid=(rows // TILE,),
+            grid=(1,),
             in_specs=[
-                pl.BlockSpec((TILE, D), lambda i: (i, 0)),
-                pl.BlockSpec((4, 1, slab, feats), lambda i: (0, i, 0, 0)),
+                pl.BlockSpec((TILE, D), lambda i: (s, 0)),
+                pl.BlockSpec((4, 1, slab, feats), lambda i: (0, s, 0, 0)),
                 pl.BlockSpec((4, feats, qkv_here), lambda i: (0, 0, 0)),
                 pl.BlockSpec((4, UNIT, feats), lambda i: (0, 0, 0)),
-                table,
-                table,
-                table,
-                table,
             ],
             out_specs=[
-                pl.BlockSpec((TILE, UNIT), lambda i: (i, 0)),
-                pl.BlockSpec((TILE, qkv_here), lambda i: (i, 0)),
+                pl.BlockSpec((TILE, UNIT), lambda i: (s, 0)),
+                pl.BlockSpec((TILE, qkv_here), lambda i: (s, 0)),
             ],
         )(
             ln1,
             cot_all,
             w1.at[:, :, :qkv_here],
             w2,
-            cos_in,
-            low_in,
-            high_in,
-            begin_in,
             acts,
             grads.at[:, :qkv_here],
         )
-        grad_stage(qkv_here, 0, 0, 0, True)
-        unit_sums[:, :qkv_here] = sum_acc[:, :qkv_here]
-
-    def out_stage():
+        if s == 3:
+            grad_stage(qkv_here, 0, 0, 0, True)
+            unit_sums[0:1, :qkv_here] = sum_acc[0:1, :qkv_here]
+
+    def out_stage(n):
         def body(act_ref, second_ref, part_ref):
             part_ref[0] = product(act_ref[...], second_ref[0], ((1,), (0,))).astype(BF16)
 
         pltpu.emit_pipeline(
             body,
-            grid=(4, rows // TILE),
+            grid=(rows // TILE,),
             in_specs=[
-                pl.BlockSpec((TILE, acts.shape[1]), lambda n, i: (i, 0)),
-                pl.BlockSpec((1, w2.shape[1], feats), lambda n, i: (n, 0, 0)),
+                pl.BlockSpec((TILE, acts.shape[1]), lambda i: (i, 0)),
+                pl.BlockSpec((1, w2.shape[1], feats), lambda i: (n, 0, 0)),
             ],
-            out_specs=[pl.BlockSpec((1, TILE, feats), lambda n, i: (n, i, 0))],
+            out_specs=[pl.BlockSpec((1, TILE, feats), lambda i: (n, i, 0))],
         )(acts, w2, out_part)
 
-    def dx_stage():
+    def dx_stage(n):
         def body(grad_ref, first_ref, part_ref):
-            norms = norm_all[pl.program_id(0)]
+            norms = norm_all[n]
             one = product(grad_ref[:, :qkv_here], first_ref[0, :, :qkv_here], ((1,), (1,)))
             two = product(grad_ref[:, qkv_here:], first_ref[0, :, qkv_here:], ((1,), (1,)))
             part_ref[0] = (one * norms[0:1] + two * norms[2:3]).astype(BF16)
 
         pltpu.emit_pipeline(
             body,
-            grid=(4, rows // TILE),
+            grid=(rows // TILE,),
             in_specs=[
-                pl.BlockSpec((TILE, grads.shape[1]), lambda n, i: (i, 0)),
-                pl.BlockSpec((1, feats, w1.shape[2]), lambda n, i: (n, 0, 0)),
+                pl.BlockSpec((TILE, grads.shape[1]), lambda i: (i, 0)),
+                pl.BlockSpec((1, feats, w1.shape[2]), lambda i: (n, 0, 0)),
             ],
-            out_specs=[pl.BlockSpec((1, TILE, feats), lambda n, i: (n, i, 0))],
+            out_specs=[pl.BlockSpec((1, TILE, feats), lambda i: (n, i, 0))],
         )(grads, w1, dx_part)
 
     class Scatter:
@@ -1045,7 +1126,7 @@
     out_scatter = Scatter(out_part, out_core, out_chip, out_x, out_half, out_y)
     dx_scatter = Scatter(dx_part, dx_core, dx_chip, dx_x, dx_half, dx_y)
     out_route = Route(
-        out_item, 4, out_up, out_down, out_far, out_send, out_edge, output
+        out_item, dealt, out_up, out_down, out_far, out_send, out_edge, output
     )
 
     def finish_output():
@@ -1059,129 +1140,379 @@
 
         out_scatter.last(body, x_own, out_item)
 
+    row_copies = [
+        copies.make(lambda: row_part, lambda: row_sums.at[r], to_row[j]) for j in (1, 2, 3)
+    ]
+
+    def sum_grad():
+        dx_scatter.to_y().wait_recv()
+
+        def body(half_ref, y_ref, x_ref, stat_ref, target_ref):
+            grad = half_ref[0].astype(F32) + y_ref[...].astype(F32)
+            target_ref[...] = grad
+            normed = (x_ref[0].astype(F32) - stat_ref[:, :1]) * stat_ref[:, 127:]
+            one = jnp.sum(grad, axis=1, keepdims=True)
+            two = jnp.sum(grad * normed, axis=1, keepdims=True)
+            lane = lax.broadcasted_iota(jnp.int32, (TILE, 128), 1)
+            both = jnp.where(lane == 0, one, jnp.where(lane == 1, two, 0.0))
+            row_part[pl.program_id(0)] = both.T[:8]
+
+        pltpu.emit_pipeline(
+            body,
+            grid=(own_rows // TILE,),
+            in_specs=[
+                pl.BlockSpec((1, TILE, feats), lambda i: (y, i, 0)),
+                pl.BlockSpec((TILE, feats), lambda i: (i, 0)),
+                pl.BlockSpec((1, slab, feats), lambda i: (i, 0, 0)),
+                pl.BlockSpec((TILE, 128), lambda i: (slabs * c + i, 0)),
+            ],
+            out_specs=[pl.BlockSpec((TILE, feats), lambda i: (i, 0))],
+        )(dx_half, dx_y, x_own, stats, grad_norm)
+        for copy in row_copies:
+            start(copy)
+        row_sums[r] = row_part[...]
+
     def finish_grad():
-        def body(half_ref, y_ref, x_ref, target_ref):
-            target_ref[0] = half_ref[0].astype(F32) + y_ref[...].astype(F32)
-
-        dx_scatter.last(body, x_own, grad_norm)
-
-    x_gather.begin()
-    cot_route.begin()
+        for copy in row_copies:
+            copy().wait_recv()
+
+        def body(grad_ref, cot_ref, x_ref, stat_ref, target_ref):
+            step = pl.program_id(0)
+            sums = row_sums[0, step] + row_sums[1, step] + row_sums[2, step] + row_sums[3, step]
+            sums = jnp.concatenate([sums, jnp.zeros((120, TILE), F32)], axis=0).T * (1.0 / D)
+            normed = (x_ref[0].astype(F32) - stat_ref[:, :1]) * stat_ref[:, 127:]
+            target_ref[0] = cot_ref[0].astype(F32) + stat_ref[:, 127:] * (
+                grad_ref[...] - sums[:, 0:1] - normed * sums[:, 1:2]
+            )
+
+        flat = pl.BlockSpec((1, slab, feats), lambda i: (i, 0, 0))
+        pltpu.emit_pipeline(
+            body,
+            grid=(own_rows // TILE,),
+            in_specs=[
+                pl.BlockSpec((TILE, feats), lambda i: (i, 0)),
+                flat,
+                flat,
+                pl.BlockSpec((TILE, 128), lambda i: (slabs * c + i, 0)),
+            ],
+            out_specs=[flat],
+        )(grad_norm, cot_own, x_own, stats, input_grad)
+
+    sums_wide = small_units.shape[2]
+    small_copies = [
+        copies.make(
+            partial(lambda j: small_part.at[peer[j]], j), lambda: small_row.at[r], to_row[j]
+        )
+        for j in (1, 2, 3)
+    ]
+    unit_copies = [
+        copies.make(lambda: unit_sums, lambda: small_units.at[r], to_row[j]) for j in (1, 2, 3)
+    ]
+    col_copy = copies.make(
+        lambda: small_here.at[:, pl.ds(sums_wide, feats)], lambda: small_col, to_col
+    )
+    small_inward = copies.make(lambda: small_here, lambda: small_in, to_in)
+    small_across = copies.make(lambda: small_half, lambda: small_other, to_in)
+    small_outward = copies.make(lambda: small_in, lambda: small_in, to_out)
+
+    def small_begin():
+        for j in range(4):
+            rows_here = [
+                jnp.sum(gain_acc[k, j * feats : (j + 1) * feats].T, axis=0, keepdims=True)
+                for k in range(4)
+            ]
+            small_part[j] = jnp.concatenate(rows_here + [jnp.zeros((4, feats), F32)], axis=0)
+        for copy in small_copies + unit_copies:
+            start(copy)
+        small_row[r] = small_part[r]
+        small_units[r] = unit_sums[...]
+
+    def small_second():
+        for copy in small_copies + unit_copies:
+            copy().wait_recv()
+        small_here[...] = jnp.zeros(small_here.shape, F32)
+        for j in range(4):
+            small_here[j : j + 1, :sums_wide] = small_units[j, 0:1]
+        small_here[:, sums_wide:] = small_row[0] + small_row[1] + small_row[2] + small_row[3]
+
+        def body(cot_ref):
+            total = jnp.sum(cot_ref[0].astype(F32), axis=0, keepdims=True)
+            small_here[4:5, sums_wide:] += total
+
+        pltpu.emit_pipeline(
+            body,
+            grid=(slabs,),
+            in_specs=[pl.BlockSpec((1, slab, feats), lambda i: (i, 0, 0))],
+        )(cot_own)
+        start(col_copy)
+
+    def small_third():
+        col_copy().wait_recv()
+        col_copy().wait_send()
+        small_here[:, sums_wide:] += small_col[...]
+        when(is_edge, lambda: small_inward().start())
+
+    def small_halve():
+        def middle():
+            small_inward().wait_recv()
+            small_half[...] = small_here[...] + small_in[...]
+            small_across().start()
+
+        when(is_mid, middle)
+
+    def small_close():
+        def middle():
+            small_across().wait_recv()
+            small_in[...] = small_half[...] + small_other[...]
+            small_outward().start()
+
+        when(is_mid, middle)
+
+    def small_finish():
+        def edge():
+            small_outward().wait_recv()
+            small_inward().wait_send()
+
+        def middle():
+            small_across().wait_send()
+            small_outward().wait_send()
+
+        when(is_edge, edge)
+        when(is_mid, middle)
+        total = small_in[...]
+        small_sum[:, :sums_wide] = total[:, :sums_wide]
+        norms = norm_own[...]
+        sums = total[:, sums_wide:]
+        gains = [
+            (sums[k : k + 1] - norms[k + 1 : k + 2] * sums[k + 1 : k + 2]) / norms[k : k + 1]
+            for k in (0, 2)
+        ]
+        small_sum[:, sums_wide:] = jnp.concatenate(
+            [gains[0], sums[1:2], gains[1], sums[3:4], sums[4:]], axis=0
+        )
+
+    near, far = 0, 1
+    line, crossing = [], []
+    begun, halved, closed, crossed = [0], [0], [0], [0]
+    flight = 2
+
+    def queue(units, which):
+        for unit in units:
+            if which == near:
+                unit.send(near)
+                crossing.append(unit)
+            line.append((unit, which))
+
+    def cross(count):
+        for _ in range(min(count, len(crossing) - crossed[0])):
+            at = crossed[0]
+            if at >= flight:
+                crossing[at - flight].sent_far()
+            crossing[at].send(far)
+            crossed[0] += 1
+
+    def lead():
+        while begun[0] < min(len(line), halved[0] + 3):
+            at = begun[0]
+
+            def edge():
+                unit, which = line[at]
+                unit.collect(which)
+                if at >= flight:
+                    before, its_half = line[at - flight]
+                    before.inward[its_half]().wait_send()
+                unit.inward[which]().start()
+
+            when(is_edge, edge)
+            begun[0] += 1
+
+    def serve(count):
+        for _ in range(count):
+            lead()
+            ahead = halved[0]
+            if ahead < len(line):
+                line[ahead][0].halve(line[ahead][1])
+                halved[0] += 1
+            if closed[0] < ahead:
+                line[closed[0]][0].close(line[closed[0]][1])
+                closed[0] += 1
+
+    slab_ids = range(slabs)
+    for q in slab_ids:
+        x_gather.begin(q)
+    cot_route.begin(0)
     norm_all[r] = norm_own[...]
     for copy in norm_copies:
         start(copy)
-    x_gather.after_y()
+    cot_route.relay(0)
+    cot_route.begin(1)
+    for q in slab_ids:
+        x_gather.after_y(q)
     mlp_fetch[0].begin()
-    cot_route.relay()
-    x_gather.after_x()
-    cot_route.hand_out()
-    cot_route.take()
-    cot_gather = Gather(cot_own, cot_all)
-    cot_gather.begin()
-    mlp_fetch[1].begin()
-    x_gather.end()
+    cot_route.relay(1)
+    cot_route.hand_out(0)
+    for q in slab_ids:
+        x_gather.after_x(q)
+    cot_route.take(0)
+    cot_gather.begin(0)
+    for q in slab_ids:
+        x_gather.after_far(q)
+    cot_route.hand_out(1)
+    for q in slab_ids:
+        x_gather.end(q)
     for copy in norm_copies:
         copy().wait_recv()
-    norm_stage()
-    cot_gather.after_y()
+    when(is_mid, norm_stage)
+    cot_route.take(1)
+    cot_gather.begin(1)
+    cot_gather.after_y(0)
+    cot_gather.after_x(0)
+    when(is_edge, norm_stage)
+    cot_gather.after_y(1)
+    mlp_fetch[1].begin()
+    cot_gather.after_x(1)
+    for q in slab_ids:
+        cot_gather.after_far(q)
+    for q in slab_ids:
+        cot_gather.end(q)
+    mlp_fetch[0].end()
+    mlp_fetch[2].begin()
+    mlp_stage(0)
+    queue(mlp_units[0], near)
+    lead()
+    mlp_fetch[1].end()
+    mlp_fetch[3].begin()
+    mlp_stage(1)
+    queue(mlp_units[1], near)
+    serve(1)
+    mlp_fetch[2].end()
     attn_fetch.begin()
-    cot_gather.after_x()
-    cot_gather.end()
-    mlp_fetch[0].end()
-    mlp_stage(0)
-    for unit in mlp_units[0]:
-        unit.send()
-    mlp_fetch[1].end()
-    mlp_stage(1)
-    for unit in mlp_units[0]:
-        unit.collect()
-    for unit in mlp_units[1]:
-        unit.send()
-    mlp_fetch[2].begin()
-    mlp_fetch[3].begin()
-    mlp_units[0][0].halve()
-    attn_fetch.end()
-    attention_stage()
-    for unit in mlp_units[1]:
-        unit.collect()
-    for unit in attn_units:
-        unit.send()
-    mlp_units[0][1].halve()
-    mlp_units[0][0].close()
-    mlp_units[1][0].halve()
-    mlp_units[0][1].close()
-    mlp_fetch[2].end()
     mlp_stage(2)
-    for unit in attn_units:
-        unit.collect()
-    for unit in mlp_units[2]:
-        unit.send()
-    mlp_units[1][1].halve()
-    mlp_units[1][0].close()
+    queue(mlp_units[2], near)
+    serve(2)
     mlp_fetch[3].end()
     mlp_stage(3)
-    for unit in mlp_units[2]:
-        unit.collect()
-    for unit in mlp_units[3]:
-        unit.send()
-    attn_units[0].halve()
-    mlp_units[1][1].close()
-    out_stage()
+    queue(mlp_units[3], near)
+    serve(4)
+    attn_fetch.end()
+    cross(2)
+    attention_slab(0)
+    serve(1)
+    cross(1)
+    queue(mlp_units[0], far)
+    attention_slab(1)
+    serve(1)
+    cross(1)
+    queue(mlp_units[1][:1], far)
+    attention_slab(2)
+    serve(1)
+    cross(1)
+    attention_slab(3)
+    queue(attn_units, near)
+    serve(1)
+    cross(1)
+    for n in range(4):
+        out_stage(n)
+        if n % 2:
+            serve(1)
+            cross(1)
     out_scatter.begin()
-    dx_stage()
-    for unit in mlp_units[3]:
-        unit.collect()
-    attn_units[1].halve()
-    attn_units[0].close()
+    queue(mlp_units[1][1:] + mlp_units[2], far)
+    dx_stage(0)
     out_scatter.second()
+    dx_stage(1)
+    serve(1)
+    cross(1)
+    dx_stage(2)
+    serve(1)
+    dx_stage(3)
     dx_scatter.begin()
-    attn_units[2].halve()
-    attn_units[1].close()
+    small_begin()
+    serve(1)
+    cross(1)
+    small_second()
+    queue(mlp_units[3], far)
+    serve(1)
     out_scatter.third()
+    cross(1)
     dx_scatter.second()
-    attn_units[3].halve()
-    attn_units[2].close()
+    serve(1)
+    small_third()
+    serve(1)
+    cross(1)
+    queue(attn_units, far)
     finish_output()
-    out_route.begin()
+    out_route.begin(0)
+    serve(1)
+    cross(1)
+    small_halve()
+    out_route.relay(0)
+    out_route.begin(1)
     dx_scatter.third()
-    mlp_units[2][0].halve()
-    attn_units[3].close()
-    out_route.relay()
+    serve(1)
+    cross(1)
+    small_close()
+    out_route.relay(1)
+    serve(1)
+    cross(4)
+    out_route.hand_out(0)
+    serve(1)
+    sum_grad()
+    out_route.hand_out(1)
+    serve(1)
+    out_route.take(0)
     finish_grad()
-    mlp_units[2][1].halve()
-    mlp_units[2][0].close()
-    out_route.hand_out()
-    mlp_units[3][0].halve()
-    mlp_units[2][1].close()
-    out_route.take()
-    mlp_units[3][1].halve()
-    mlp_units[3][0].close()
-    gain_q[...] = gain_acc[0]
-    bias_q[...] = gain_acc[1]
-    gain_f[...] = gain_acc[2]
-    bias_f[...] = gain_acc[3]
-    mlp_units[3][1].close()
-    for unit in sum(mlp_units, []) + attn_units:
-        unit.finish()
+    serve(1)
+    out_route.take(1)
+    while closed[0] < len(line):
+        serve(1)
+    for at, (unit, which) in enumerate(line):
+        unit.finish(which, at >= len(line) - flight)
+    for unit in crossing[len(crossing) - flight :]:
+        unit.sent_far()
+    small_finish()
     cot_route.finish()
     out_route.finish()
     for copy in sent:
-        copy().wait_send()
-
-
-def line_codes(sources, plane):
-    middle = (plane == 1) | (plane == 2)
-    own = sources[:, 0] * 0
-
-    def code(wanted):
-        up, down = plane - 1, plane + 1
-        coded = jnp.where(wanted == up, 1, jnp.where(wanted == down, 2, 3))
-        coded = jnp.where(middle, coded, 1)
-        return jnp.where(wanted == plane, own, coded)
-
-    take = lax.dynamic_index_in_dim(sources, plane, 1, keepdims=False)
-    hand = jnp.where(plane == 1, sources[:, 0], sources[:, 3])
-    return jnp.concatenate([code(take), code(hand)]).astype(jnp.int32)
+        if copy is not col_copy:
+            copy().wait_send()
+
+
+def widen_body(first_ref, dense_ref, fc2_ref, qkv_out, fc1_out, dense_out, fc2_out):
+    qkv_here = qkv_out.shape[1]
+    qkv_out[...] = first_ref[0, :, :qkv_here].astype(F32)
+    fc1_out[...] = first_ref[0, :, qkv_here:].astype(F32)
+    dense_out[...] = dense_ref[0].astype(F32)
+    fc2_out[...] = fc2_ref[0].astype(F32)
+
+
+def widen(first_sum, second_sum, qkv_here, attn_here):
+    feats, first_cols = first_sum.shape[1:]
+    hidden_here = first_cols - qkv_here
+    tiles = hidden_here // attn_here
+    tile = feats // tiles
+    return pl.pallas_call(
+        widen_body,
+        grid=(4, tiles),
+        in_specs=[
+            pl.BlockSpec((1, tile, first_cols), lambda s, i: (s, i, 0)),
+            pl.BlockSpec((1, attn_here // tiles, feats), lambda s, i: (s, i, 0)),
+            pl.BlockSpec((1, attn_here, feats), lambda s, i: (s, 1 + i, 0)),
+        ],
+        out_specs=[
+            pl.BlockSpec((tile, qkv_here), lambda s, i: (i, s)),
+            pl.BlockSpec((tile, hidden_here), lambda s, i: (i, s)),
+            pl.BlockSpec((attn_here // tiles, feats), lambda s, i: (s * tiles + i, 0)),
+            pl.BlockSpec((attn_here, feats), lambda s, i: (s * tiles + i, 0)),
+        ],
+        out_shape=[
+            jax.ShapeDtypeStruct((feats, 4 * qkv_here), F32),
+            jax.ShapeDtypeStruct((feats, 4 * hidden_here), F32),
+            jax.ShapeDtypeStruct((4 * attn_here, feats), F32),
+            jax.ShapeDtypeStruct((4 * hidden_here, feats), F32),
+        ],
+        compiler_params=pltpu.CompilerParams(vmem_limit_bytes=32 * 1024 * 1024),
+    )(first_sum, second_sum, second_sum)
 
 
 def dealt_layer(
@@ -1202,9 +1533,6 @@
     fc2_bias,
     cotangent,
 ):
-    plane = lax.axis_index("dp")
-    row = lax.axis_index("row")
-    col = lax.axis_index("col")
     own_rows, feats = layer_input.shape
     rows = 2 * own_rows
     slab = own_rows // 2
@@ -1216,39 +1544,19 @@
     first_cols = qkv_here + hidden_here
     second_rows = attn_here + hidden_here
 
-    deal_here = lax.dynamic_slice_in_dim(deal_table, 2 * col, 2, 0)
-    undeal_here = jnp.argmax(
-        deal_here[:, None, :] == jnp.arange(4, dtype=jnp.int32)[None, :, None], axis=2
-    ).astype(jnp.int32)
-    codes = jnp.concatenate([line_codes(undeal_here, plane), line_codes(deal_here, plane)])
-    lengths_here = lax.dynamic_slice_in_dim(lengths, plane * 4, 4, 0)
-    positions = jnp.concatenate([segment_layout(lengths_here[s], slab)[1] for s in range(4)])
-    begins = jnp.tile(jnp.arange(slab, dtype=jnp.int32), 4) - positions
-    cos_table, sin_table = rotary_tables(positions)
-    lane = jnp.arange(HD)
-    cos_table = jnp.pad(cos_table, ((0, 0), (0, HD - ROT)), constant_values=1.0)
-    sin_table = jnp.pad(sin_table, ((0, 0), (0, HD - ROT)))
-    low_table = jnp.where(lane < ROT // 2, -sin_table, 0.0)
-    high_table = jnp.where(lane < ROT // 2, 0.0, sin_table)
-    begins = jnp.broadcast_to(begins[:, None], (rows, HD))
-    norms = jnp.stack([ln1_gain, ln1_bias, ln2_gain, ln2_bias])
-    norms = jnp.concatenate([norms, norms])
-    bias_here = jnp.concatenate(
-        [
-            lax.dynamic_slice_in_dim(qkv_bias, row * qkv_here, qkv_here, 0),
-            lax.dynamic_slice_in_dim(fc1_bias, row * hidden_here, hidden_here, 0),
-        ]
-    )
-    bias_here = jnp.broadcast_to(bias_here[None], (8, first_cols))
-    out_bias = jnp.broadcast_to((dense_bias + fc2_bias)[None], (8, feats))
+    norms = jnp.stack([ln1_gain, ln1_bias, ln2_gain, ln2_bias] * 2)
+    out_bias = (dense_bias + fc2_bias).reshape(1, feats)
+    turns = 1.0 / 10000.0 ** (np.arange(0, ROT, 2) / ROT)
+    turns = np.concatenate([turns, turns, np.zeros(HD - ROT)])
+    turns = np.broadcast_to(turns.astype(np.float32), (8, HD))
 
     low = lambda *shape: jax.ShapeDtypeStruct(shape, BF16)
     wide = lambda *shape: jax.ShapeDtypeStruct(shape, F32)
     first = low(4, feats, first_cols)
     second = low(4, second_rows, feats)
     item = low(2, slab, feats)
-    outputs = [first, second, item, wide(2, slab, feats), item, wide(rows, 128)]
-    in_vmem = [wide(D, 128)] * 4 + [wide(8, first_cols)]
+    small_shape = (8, first_cols + feats)
+    outputs = [first, second, item, wide(2, slab, feats)]
     scatter = [
         low(4, rows, feats),
         low(2, rows, feats),
@@ -1258,7 +1566,8 @@
         low(own_rows, feats),
     ]
     buffers = (
-        [low(4, 4, slab, feats)] * 2
+        [wide(own_rows, feats), item, wide(rows, 128)]
+        + [low(4, 4, slab, feats)] * 2
         + [low(rows, D)] * 2
         + [first, second, low(rows, second_rows), low(rows, first_cols)]
         + [first, second] * 5
@@ -1269,22 +1578,29 @@
     )
     any_space = pl.BlockSpec(memory_space=pl.ANY)
     vmem = pl.BlockSpec(memory_space=pltpu.VMEM)
-    copies = 150
+    smem = pl.BlockSpec(memory_space=pltpu.SMEM)
+    copies = 250
     results = pl.pallas_call(
         layer_kernel,
-        in_specs=[pl.BlockSpec(memory_space=pltpu.SMEM)]
-        + [any_space] * 2
-        + [vmem] * 3
-        + [any_space] * 8,
-        out_specs=[any_space] * len(outputs)
-        + [vmem] * len(in_vmem)
-        + [any_space] * len(buffers),
-        out_shape=outputs + in_vmem + buffers,
+        in_specs=[smem] * 2 + [any_space] * 2 + [vmem] * 5 + [any_space] * 4,
+        out_specs=[any_space] * 4 + [vmem] + [any_space] * len(buffers),
+        out_shape=outputs + [wide(*small_shape)] + buffers,
         scratch_shapes=[
             pltpu.VMEM((4, UNIT + qkv_here, feats), F32),
             pltpu.VMEM((4, 8, feats), F32),
             pltpu.VMEM((4, D, 128), F32),
             pltpu.VMEM((8, qkv_here), F32),
+            pltpu.VMEM((8, first_cols), F32),
+            pltpu.VMEM((4, 8, feats), F32),
+            pltpu.VMEM((4, 8, feats), F32),
+            pltpu.VMEM((4, 8, first_cols), F32),
+            pltpu.VMEM((8, feats), F32),
+            pltpu.VMEM(small_shape, F32),
+            pltpu.VMEM(small_shape, F32),
+            pltpu.VMEM(small_shape, F32),
+            pltpu.VMEM(small_shape, F32),
+            pltpu.VMEM((2, 8, slab), F32),
+            pltpu.VMEM((4, 2, 8, slab), F32),
             pltpu.SemaphoreType.DMA((copies,)),
             pltpu.SemaphoreType.DMA((copies,)),
             pltpu.SemaphoreType.DMA((32,)),
@@ -1298,90 +1614,38 @@
             transcendentals=rows * hidden_here,
         ),
     )(
-        codes,
+        lengths,
+        deal_table,
         layer_input.reshape(2, slab, feats),
         cotangent.reshape(2, slab, feats),
         norms,
-        bias_here,
+        qkv_bias.reshape(4, 1, qkv_here),
+        fc1_bias.reshape(4, 1, hidden_here),
         out_bias,
+        turns,
         qkv_weight,
         dense_weight,
         fc1_weight,
         fc2_weight,
-        cos_table,
-        low_table,
-        high_table,
-        begins,
-    )
-    first_sum, second_sum, output, grad_norm, cot_own, stats = results[:6]
-    gain1, bias1, gain2, bias2 = [jnp.sum(part, axis=1) for part in results[6:10]]
-    unit_sums = results[10][0]
-    output = output.reshape(own_rows, feats)
-
-    def first_grad(part):
-        return part.transpose(1, 0, 2).reshape(feats, -1).astype(F32)
-
-    def second_grad(part):
-        return part.reshape(-1, feats).astype(F32)
-
-    qkv_grad = first_grad(first_sum[:, :, :qkv_here])
-    fc1_grad = first_grad(first_sum[:, :, qkv_here:])
-    dense_grad = second_grad(second_sum[:, :attn_here])
-    fc2_grad = second_grad(second_sum[:, attn_here:])
-
-    stats_own = lax.dynamic_slice_in_dim(stats, col * own_rows, own_rows, 0)
-    mean, inv_std = stats_own[:, :1], stats_own[:, 127:]
-    normed_own = (layer_input.astype(F32) - mean) * inv_std
-    grad_normed = grad_norm.reshape(own_rows, feats)
-    row_sums = lax.psum(
-        (jnp.sum(grad_normed, axis=1), jnp.sum(grad_normed * normed_own, axis=1)), "row"
-    )
-    input_grad = cot_own.reshape(own_rows, feats).astype(F32) + inv_std * (
-        grad_normed - row_sums[0][:, None] / D - normed_own * row_sums[1][:, None] / D
-    )
-
-    norm_sums = jnp.stack([gain1, bias1, gain2, bias2])
-    bias_part = jnp.sum(cotangent, axis=0, dtype=F32)
-    bias_sum = jnp.zeros((4, feats), F32).at[row].set(bias_part)
-    qkv_sums = jnp.zeros((2, 4, qkv_here), F32).at[col, row].set(unit_sums[:qkv_here])
-    hidden_sums = jnp.zeros((2, 4, hidden_here), F32).at[col, row].set(unit_sums[qkv_here:])
-    small = lax.psum(
-        jnp.concatenate(
-            [
-                norm_sums.reshape(-1),
-                bias_sum.reshape(-1),
-                qkv_sums.reshape(-1),
-                hidden_sums.reshape(-1),
-            ]
-        ),
-        ("dp", "row", "col"),
-    )
-    norm_sums, bias_sum, qkv_sums, hidden_sums = jnp.split(
-        small, [4 * D, 5 * D, 5 * D + 2 * qkv_cols]
-    )
-    norm_sums = lax.dynamic_index_in_dim(norm_sums.reshape(4, 4, feats), row, 1, keepdims=False)
-    bias_sum = lax.dynamic_index_in_dim(bias_sum.reshape(4, feats), row, 0, keepdims=False)
-    qkv_bias_grad = lax.dynamic_index_in_dim(qkv_sums.reshape(2, qkv_cols), col, 0, keepdims=False)
-    fc1_bias_grad = lax.dynamic_index_in_dim(
-        hidden_sums.reshape(2, hidden_cols), col, 0, keepdims=False
-    )
-    gain1 = (norm_sums[0] - ln1_bias * norm_sums[1]) / ln1_gain
-    gain2 = (norm_sums[2] - ln2_bias * norm_sums[3]) / ln2_gain
+    )
+    first_sum, second_sum, output, input_grad, small = results[:5]
+    qkv_grad, fc1_grad, dense_grad, fc2_grad = widen(first_sum, second_sum, qkv_here, attn_here)
+    norm_sums = small[:5, first_cols:]
     return (
-        output,
-        input_grad,
-        gain1,
+        output.reshape(own_rows, feats),
+        input_grad.reshape(own_rows, feats),
+        norm_sums[0],
         norm_sums[1],
         qkv_grad,
-        qkv_bias_grad,
+        small[:4, :qkv_here].reshape(qkv_cols),
         dense_grad,
-        bias_sum,
-        gain2,
+        norm_sums[4],
+        norm_sums[2],
         norm_sums[3],
         fc1_grad,
-        fc1_bias_grad,
+        small[:4, qkv_here:first_cols].reshape(hidden_cols),
         fc2_grad,
-        bias_sum,
+        norm_sums[4],
     )
 
 

time: 817 us -> 673 us (0.82)
  waiting for transfers between devices: 51.7 us -> 0 us
  other arithmetic: 41.8 us -> 1.28 us
  local copies, waits for them, and re-layouts: 50.2 us -> 16.7 us
  between operations: 14.9 us -> 0.85 us
  blocking collectives: 10.6 us -> 0 us
    psum x1 -> x0, waiting for transfers between devices: 51.7 us -> none  [dealt_layer(): lax.psum(jnp.concatenate([norm_sums.reshape(-1), bias_sum.reshape(-1), qk...]
    convert_element_type x4 -> x0, other arithmetic: 18.3 us -> none  [the longest x2 11.8 us: first_grad(): return part.transpose(1, 0, 2).reshape(feats, -1).astype(F32)]
    convert_element_type x2 -> x0, local copies, waits for them, and re-layouts: 15.3 us -> none  [first_grad(): return part.transpose(1, 0, 2).reshape(feats, -1).astype(F32)]
    psum x1 -> x0, blocking collectives: 10.6 us -> none  [dealt_layer(): lax.psum((jnp.sum(grad_normed, axis=1), jnp.sum(grad_normed * normed_own,...]
    reduce_sum x15 -> x0, other arithmetic: 8.45 us -> none  [the longest x4 5.04 us: dealt_layer(): jnp.sum(part, axis=1)]
    unnamed x50 -> x16, local copies, waits for them, and re-layouts: 18.2 us -> 11.2 us
    pallas_call x1 -> x2, Pallas kernels: 635 us -> 642 us  [the longest x1 632 us: dealt_layer(): pl.pallas_call(layer_kernel, in_specs=[smem] * 2 + [any_space] * 2 + [vme...]
  transfers between devices with their start and end apart: 1 -> 0, of which waited for: 1 -> 0; matrix products, arithmetic and copies ran while one was open for 8% -> 0% of each run, Pallas kernels for 0% -> 0%
where the time goes in v3:
time: 673 us; the launch traced here: 661 us
  Pallas kernels  642 us (95%)
  local copies, waits for them, and re-layouts  16.7 us (2%)
    pallas_call x1, Pallas kernels, dealt_layer(): pl.pallas_call(layer_kernel, in_specs=[smem] * 2 + [any_space] * 2 + [vme...  632 us

profile of v3, /device:TPU:0, one launch (start us, length us, event | category | flops | bytes accessed | tf_op | source)
XLA Modules:
  0.0 660.9 jit_solution(977205017441927062)
XLA Ops:
  0.6 1.3 add.3
  1.9 1.4 copy.31.lengths
  3.3 1.4 stack.23.norm_own
  4.7 1.2 jit_solution_.3.turns
  6.0 631.9 %shard_map.272 = (bf16[4,512,1792]{2,1,0:T(8,128)(2,1)}, bf16[4,1280,512]{2,1,0:T(8,128)(2,1)}, bf16[2,512,512]{2,1,0:T(8,128)(2,1)}, f32[2,512,512]{2,1,0:T(8,1...) custom-call(s32[16,4]{1,0:T(8,128)} %copy.31.lengths, ...), custom_call_target="tpu_custom_call" | custom-call | flops 77309411328 | bytes 209715200 | tf_op jit(solution)/shard_map/pallas_call | solution.py:1583
  637.9 1.5 fusion
  639.4 0.0 copy-start.4
  639.4 0.7 slice.30
  640.1 0.8 slice_bitcast_fusion
  640.9 0.6 copy.34
  641.5 0.6 reshape.62
  642.1 0.0 copy-start
  642.1 2.5 copy-done
  644.6 0.0 copy-start.1
  644.6 3.1 copy-done.1
  647.7 0.0 copy-start.3
  647.7 0.0 copy-start.2
  647.7 10.2 %shard_map.273 = (f32[512,3072]{1,0:T(8,128)}, f32[512,4096]{1,0:T(8,128)}, f32[1024,512]{1,0:T(8,128)}, f32[4096,512]{1,0:T(8,128)}) custom-call(bf16[4,512,1792]{2,1,0:T(8,128)(2,1)S(1)} %copy-done.1, bf16[4,1280,512]{2,1,0:T(8,128)(2,1)S(1)} %copy-done, bf16[4,1280,512]{2,1,0:T(8,128)(2,1)S(1)} %copy-done), custom_call_target="tpu_custom_call" | custom-call | tf_op jit(solution)/shard_map/pallas_call | solution.py:1494
  657.8 0.0 copy-done.4
  657.8 0.6 copy.38
  658.4 0.0 copy-done.3
  658.4 1.0 copy.39
  659.4 0.0 copy-done.2
  659.4 1.3 copy.40
Async XLA Ops:
  639.4 18.5 %copy-start.4 = (f32[1,512]{1,0:T(1,128)}, f32[1,512]{1,0:T(1,128)S(1)}, u32[]{:S(2)}) copy-start(f32[1,512]{1,0:T(1,128)S(1)} %get-tuple-element.34) | copy-start | bytes 6148
  642.1 2.5 copy-start
  644.6 3.1 copy-start.1
  647.7 10.8 %copy-start.3 = (bf16[2,512,512]{2,1,0:T(8,128)(2,1)S(1)}, bf16[2,512,512]{2,1,0:T(8,128)(2,1)}, u32[]{:S(2)}) copy-start(bf16[2,512,512]{2,1,0:T(8,128)(2,1)} %get-tuple-element.23) | copy-start | bytes 3145732
  647.7 11.7 %copy-start.2 = (f32[2,512,512]{2,1,0:T(8,128)S(1)}, f32[2,512,512]{2,1,0:T(8,128)}, u32[]{:S(2)}) copy-start(f32[2,512,512]{2,1,0:T(8,128)} %get-tuple-element.24) | copy-start | bytes 6291460

commit v4 on v3

--- a/solution.py
+++ b/solution.py
@@ -405,14 +405,6 @@
     grads,
     first_part,
     second_part,
-    first_here,
-    second_here,
-    first_in,
-    second_in,
-    first_half,
-    second_half,
-    first_other,
-    second_other,
     out_part,
     out_core,
     out_chip,
@@ -438,7 +430,12 @@
     out_edge,
     acc,
     norm_all,
-    gain_acc,
+    first_in,
+    second_in,
+    first_other,
+    second_other,
+    first_slot,
+    second_slot,
     sum_acc,
     unit_sums,
     small_part,
@@ -682,166 +679,194 @@
         copies.make(lambda: norm_own, lambda: norm_all.at[r], to_row[j]) for j in (1, 2, 3)
     ]
 
+    odd = z % 2
+    across_row = 2 * (1 - y) + core + odd * (1 - 2 * core)
+    to_across = {"row": across_row}
+    to_pair = {"dp": z + 1 - 2 * odd}
+
     class Fetch:
-        def __init__(self, first, first_at, first_width, at, second, second_at, second_width, low):
-            def first_source(j):
-                lanes = pl.multiple_of(peer[j] * first_width + first_at, 256)
-                size = UNIT if first is fc1_w else qkv_here
-                return first.at[:, pl.ds(lanes, size)]
-
-            def second_source(j):
-                size = UNIT
-                begin = pl.multiple_of(peer[j] * second_width + second_at, 256)
-                return second.at[pl.ds(begin, size)]
-
+        def __init__(
+            self, paired, first, first_at, first_width, at, second, second_at, second_width, low
+        ):
             size = UNIT if first is fc1_w else qkv_here
-            first_target = lambda: w1.at[r, :, pl.ds(at, size)]
-            second_target = lambda: w2.at[r, pl.ds(low, UNIT)]
-            self.remote = []
-            for j in (1, 2, 3):
-                self.remote.append(
-                    copies.make(partial(first_source, j), first_target, to_row[j])
-                )
-                self.remote.append(
-                    copies.make(partial(second_source, j), second_target, to_row[j])
-                )
-            self.kept = [(partial(first_source, 0), first_target), (partial(second_source, 0), second_target)]
+
+            def first_source(taker):
+                lanes = pl.multiple_of(taker * first_width + first_at, 256)
+                return lambda: first.at[:, pl.ds(lanes, size)]
+
+            def second_source(taker):
+                begin = pl.multiple_of(taker * second_width + second_at, 256)
+                return lambda: second.at[pl.ds(begin, UNIT)]
+
+            def first_target(giver):
+                return lambda: w1.at[giver, :, pl.ds(at, size)]
+
+            def second_target(giver):
+                return lambda: w2.at[giver, pl.ds(low, UNIT)]
+
+            pairs = ((first_source, first_target), (second_source, second_target))
+            self.beside = [copies.make(f(peer[1]), t(r), to_row[1]) for f, t in pairs]
+            self.paired = paired
+            if paired:
+                self.over = [copies.make(f(across_row), t(r), to_across) for f, t in pairs]
+                self.shared = [
+                    copies.make(t(across_row), t(across_row), to_pair) for _, t in pairs
+                ]
+            else:
+                self.over = [
+                    copies.make(f(peer[j]), t(r), to_row[j]) for f, t in pairs for j in (2, 3)
+                ]
+            self.kept = [(f(r), t(r)) for f, t in pairs]
 
         def begin(self):
-            for copy in self.remote:
+            for copy in self.over + self.beside:
                 start(copy)
             self.kept = [local(*pair) for pair in self.kept]
 
+        def share(self):
+            for copy, onward in zip(self.over, self.shared):
+                copy().wait_recv()
+                start(onward)
+
         def end(self):
-            for copy in self.remote:
+            for copy in self.beside + (self.shared if self.paired else self.over):
                 copy().wait_recv()
             for copy in self.kept:
                 copy().wait()
 
-    attn_fetch = Fetch(qkv_w, 0, qkv_here, 0, dense_w, 0, attn_here, 0)
+    attn_fetch = Fetch(False, qkv_w, 0, qkv_here, 0, dense_w, 0, attn_here, 0)
     mlp_fetch = [
-        Fetch(fc1_w, at, hidden_here, qkv_here + at, fc2_w, at, hidden_here, attn_here + at)
+        Fetch(at < 3 * UNIT, fc1_w, at, hidden_here, qkv_here + at, fc2_w, at, hidden_here, attn_here + at)
         for at in range(0, hidden_here, UNIT)
     ]
 
+    kinds = [0, 0, 0]
+    keep = upper
+
     class Unit:
-        def __init__(self, kind, at):
-            self.kind, self.at = kind, at
+        def __init__(self, kind, at, width=UNIT):
+            place, offset = kinds[kind] // UNIT, kinds[kind] % UNIT
+            kinds[kind] += width
             if kind == 1:
-                self.view = lambda ref, s: ref.at[s, :, pl.ds(at, UNIT)]
-                self.refs = (first_part, first_here, first_in, first_half, first_other, first_sum)
+                part, self.total = first_part, first_sum
+
+                def held(ref, index):
+                    return ref.at[index, :, :, pl.ds(offset, width)]
+
+                self.arrived, self.other = held(first_in, place), held(first_other, place)
+                self.slot = partial(held, first_slot)
+                half = feats // 2
+                self.whole = lambda: part.at[:, :, pl.ds(at, width)]
+
+                def region(which, index):
+                    return self.total.at[index, pl.ds(which * half, half), pl.ds(at, width)]
+
             else:
-                self.view = lambda ref, s: ref.at[s, pl.ds(at, UNIT)]
-                self.refs = (
-                    second_part,
-                    second_here,
-                    second_in,
-                    second_half,
-                    second_other,
-                    second_sum,
-                )
-            part, here, arrived, half, other, total = self.refs
+                part, self.total = second_part, second_sum
+                self.arrived = second_in.at[place, :, pl.ds(offset, width)]
+                self.other = second_other.at[place, :, pl.ds(offset // 2, width // 2)]
+                self.slot = lambda index: second_slot.at[index, :, pl.ds(offset, width)]
+                half = width // 2
+                self.whole = lambda: part.at[:, pl.ds(at, width)]
+
+                def region(which, index):
+                    return self.total.at[index, pl.ds(at + which * half, half)]
+
+            self.half, self.region = half, region
+            every = slice(None)
+            self.inward = copies.make(self.whole, lambda: self.arrived, to_in)
+            self.across = copies.make(
+                lambda: self.arrived.at[:, pl.ds((1 - keep) * half, half)],
+                lambda: self.other,
+                to_in,
+            )
             self.spread = [
                 copies.make(
-                    partial(lambda j: self.view(part, peer[j]), j),
-                    lambda: self.view(here, r),
+                    partial(lambda j: self.other.at[peer[j]], j),
+                    lambda: region(keep, r),
                     to_row[j],
                 )
                 for j in (1, 2, 3)
             ]
-            def half_of(ref, which):
-                first_slot = 2 * (y if which == 0 else 1 - y)
-                if kind == 1:
-                    return ref.at[pl.ds(first_slot, 2), :, pl.ds(at, UNIT)]
-                return ref.at[pl.ds(first_slot, 2), pl.ds(at, UNIT)]
-
-            def half_copy(source, target, which, device):
-                return copies.make(
-                    lambda: half_of(source, which), lambda: half_of(target, which), device
-                )
-
-            self.inward = [half_copy(here, arrived, which, to_in) for which in (0, 1)]
-            self.across = [half_copy(half, other, which, to_in) for which in (0, 1)]
-            self.outward = [half_copy(total, total, which, to_out) for which in (0, 1)]
-
-        def send(self, which):
-            part, here = self.refs[:2]
-            if which == 0:
-                start(self.spread[0])
-                self.kept = local(lambda: self.view(part, r), lambda: self.view(here, r))
-            else:
-                self.spread[1]().start()
-                self.spread[2]().start()
-
-        def sent_far(self):
-            self.spread[1]().wait_send()
-            self.spread[2]().wait_send()
-
-        def collect(self, which):
-            if which == 0:
-                self.spread[0]().wait_recv()
-                self.kept().wait()
-            else:
-                self.spread[1]().wait_recv()
-                self.spread[2]().wait_recv()
-
-        def add(self, which, left, right, target):
-            first_slot = 2 * (y if which == 0 else 1 - y)
-            if self.kind == 1:
-                block = pl.BlockSpec(
-                    (1, feats, UNIT), lambda s: (first_slot + s, 0, self.at // UNIT)
-                )
-            else:
-                block = pl.BlockSpec(
-                    (1, UNIT, feats), lambda s: (first_slot + s, self.at // UNIT, 0)
-                )
-
-            def body(left_block, right_block, target_block):
-                target_block[...] = (
-                    left_block[...].astype(F32) + right_block[...].astype(F32)
-                ).astype(BF16)
-
-            pltpu.emit_pipeline(body, grid=(2,), in_specs=[block] * 2, out_specs=[block])(
-                left, right, target
+            self.over = copies.make(
+                lambda: region(keep, every), lambda: region(keep, every), to_in
             )
-
-        def halve(self, which):
-            part, here, arrived, half, other, total = self.refs
+            self.outward = [
+                copies.make(lambda: region(keep, every), lambda: region(keep, every), to_out),
+                copies.make(
+                    lambda: region(1 - keep, every), lambda: region(1 - keep, every), to_out
+                ),
+            ]
+            self.load, self.store = local_used[0], local_used[0] + 1
+            local_used[0] += 2
+
+        def loading(self, turn):
+            return pltpu.make_async_copy(
+                self.whole(), self.slot(turn % 2), local_sems.at[self.load]
+            )
+
+        def storing(self):
+            return pltpu.make_async_copy(
+                self.other.at[r], self.region(keep, r), local_sems.at[self.store]
+            )
+
+        def add(self, target, term, offset):
+            step = 64
+
+            def body(i, carry):
+                here = pl.ds(pl.multiple_of(i * step, step), step)
+                there = pl.ds(pl.multiple_of(offset + i * step, step), step)
+                target[:, here] = (target[:, here].astype(F32) + term[:, there].astype(F32)).astype(BF16)
+                return carry
+
+            lax.fori_loop(0, target.shape[1] // step, body, 0)
+
+        def sum_chip_pair(self, turn):
+            self.loading(turn).wait()
+            self.inward().wait_recv()
+            self.add(self.arrived, self.slot(turn % 2), 0)
+            self.across().start()
+
+        def sum_line(self):
+            self.across().wait_recv()
+            self.add(self.other, self.arrived, keep * self.half)
+            for copy in self.spread:
+                copy().start()
+            self.storing().start()
+
+        def pass_kept(self):
+            for copy in self.spread:
+                copy().wait_recv()
+            self.storing().wait()
+            self.over().start()
+            self.outward[0]().start()
+
+        def pass_other(self):
+            self.over().wait_recv()
+            self.outward[1]().start()
+
+        def finish(self, unsent):
+            def edge():
+                for copy in self.outward:
+                    copy().wait_recv()
+                if unsent:
+                    self.inward().wait_send()
 
             def middle():
-                self.collect(which)
-                self.inward[which]().wait_recv()
-                self.add(which, here, arrived, half)
-                self.across[which]().start()
-
-            when(is_mid, middle)
-
-        def close(self, which):
-            part, here, arrived, half, other, total = self.refs
-
-            def middle():
-                self.across[which]().wait_recv()
-                self.add(which, half, other, total)
-                self.outward[which]().start()
-
-            when(is_mid, middle)
-
-        def finish(self, which, unsent):
-            def edge():
-                self.outward[which]().wait_recv()
-                if unsent:
-                    self.inward[which]().wait_send()
-
-            def middle():
-                self.across[which]().wait_send()
-                self.outward[which]().wait_send()
+                for copy in [self.across, self.over] + self.spread + self.outward:
+                    copy().wait_send()
 
             when(is_edge, edge)
             when(is_mid, middle)
 
-    mlp_units = [
-        [Unit(2, attn_here + at), Unit(1, qkv_here + at)] for at in range(0, hidden_here, UNIT)
-    ]
+    def chunk_units(at):
+        width = UNIT // 2 if at in (0, hidden_here - UNIT) else UNIT
+        parts = range(at, at + UNIT, width)
+        return [Unit(2, attn_here + part, width) for part in parts] + [
+            Unit(1, qkv_here + part, width) for part in parts
+        ]
+
+    mlp_units = [chunk_units(at) for at in range(0, hidden_here, UNIT)]
     attn_units = [Unit(2, 0)] + [Unit(1, at) for at in range(0, qkv_here, UNIT)]
 
     def norm_body(x_ref, one_ref, two_ref, stat_ref):
@@ -925,15 +950,20 @@
             weight = first_ref[0].astype(F32)
             part_one[0] = grad.astype(BF16)
             part_two[0] = acc[j, :UNIT].astype(BF16)
-            here = pl.ds(j * feats, feats)
-            gains = fold_lanes(grad * weight)
-            biases = fold_lanes(weight * sum_acc[0:1, :width])
-            if fresh:
-                gain_acc[2 * which, here] = gains
-                gain_acc[2 * which + 1, here] = biases
-            else:
-                gain_acc[2 * which, here] += gains
-                gain_acc[2 * which + 1, here] += biases
+            terms = [fold_lanes(grad * weight), fold_lanes(weight * sum_acc[0:1, :width])]
+            ones = jnp.ones((8, 128), F32)
+            for k in (0, 1):
+                sums = lax.dot_general(
+                    ones,
+                    terms[k],
+                    (((1,), (1,)), ((), ())),
+                    precision=lax.Precision.HIGHEST,
+                    preferred_element_type=F32,
+                )[0:1]
+                at = 2 * which + k
+                if not fresh:
+                    sums = sums + small_part[j, at : at + 1]
+                small_part[j, at : at + 1] = sums
 
         lanes = slice(first_at, first_at + width)
         block = pl.BlockSpec((1, feats, width), lambda j: (j, 0, 0))
@@ -945,6 +975,7 @@
         )(w1.at[:, :, lanes], first_part.at[:, :, lanes], second_part)
 
     def attention_slab(s):
+        once = pl.Buffered(1)
         heads = qkv_here // (3 * HD)
         bias = qkv_bias[r]
 
@@ -998,14 +1029,14 @@
             body,
             grid=(1,),
             in_specs=[
-                pl.BlockSpec((TILE, D), lambda i: (s, 0)),
-                pl.BlockSpec((4, 1, slab, feats), lambda i: (0, s, 0, 0)),
-                pl.BlockSpec((4, feats, qkv_here), lambda i: (0, 0, 0)),
-                pl.BlockSpec((4, UNIT, feats), lambda i: (0, 0, 0)),
+                pl.BlockSpec((TILE, D), lambda i: (s, 0), pipeline_mode=once),
+                pl.BlockSpec((4, 1, slab, feats), lambda i: (0, s, 0, 0), pipeline_mode=once),
+                pl.BlockSpec((4, feats, qkv_here), lambda i: (0, 0, 0), pipeline_mode=once),
+                pl.BlockSpec((4, UNIT, feats), lambda i: (0, 0, 0), pipeline_mode=once),
             ],
             out_specs=[
-                pl.BlockSpec((TILE, UNIT), lambda i: (s, 0)),
-                pl.BlockSpec((TILE, qkv_here), lambda i: (s, 0)),
+                pl.BlockSpec((TILE, UNIT), lambda i: (s, 0), pipeline_mode=once),
+                pl.BlockSpec((TILE, qkv_here), lambda i: (s, 0), pipeline_mode=once),
             ],
         )(
             ln1,
@@ -1216,12 +1247,7 @@
     small_outward = copies.make(lambda: small_in, lambda: small_in, to_out)
 
     def small_begin():
-        for j in range(4):
-            rows_here = [
-                jnp.sum(gain_acc[k, j * feats : (j + 1) * feats].T, axis=0, keepdims=True)
-                for k in range(4)
-            ]
-            small_part[j] = jnp.concatenate(rows_here + [jnp.zeros((4, feats), F32)], axis=0)
+        small_part[:, 4:] = jnp.zeros((4, 4, feats), F32)
         for copy in small_copies + unit_copies:
             start(copy)
         small_row[r] = small_part[r]
@@ -1291,51 +1317,50 @@
             [gains[0], sums[1:2], gains[1], sums[3:4], sums[4:]], axis=0
         )
 
-    near, far = 0, 1
-    line, crossing = [], []
-    begun, halved, closed, crossed = [0], [0], [0], [0]
+    line = []
+    begun, loaded, served = [0], [0], [0]
     flight = 2
 
-    def queue(units, which):
-        for unit in units:
-            if which == near:
-                unit.send(near)
-                crossing.append(unit)
-            line.append((unit, which))
-
-    def cross(count):
-        for _ in range(min(count, len(crossing) - crossed[0])):
-            at = crossed[0]
-            if at >= flight:
-                crossing[at - flight].sent_far()
-            crossing[at].send(far)
-            crossed[0] += 1
-
     def lead():
-        while begun[0] < min(len(line), halved[0] + 3):
+        while begun[0] < min(len(line), served[0] + 2):
             at = begun[0]
 
             def edge():
-                unit, which = line[at]
-                unit.collect(which)
                 if at >= flight:
-                    before, its_half = line[at - flight]
-                    before.inward[its_half]().wait_send()
-                unit.inward[which]().start()
+                    line[at - flight].inward().wait_send()
+                line[at].inward().start()
 
             when(is_edge, edge)
             begun[0] += 1
-
-    def serve(count):
+        while loaded[0] < min(len(line), served[0] + 2):
+            at = loaded[0]
+            when(is_mid, lambda: line[at].loading(at).start())
+            loaded[0] += 1
+
+    def queue(units):
+        line.extend(units)
+        lead()
+
+    def serve(count, closing=False):
         for _ in range(count):
+            at = served[0]
+            if at >= len(line) and not closing:
+                return
             lead()
-            ahead = halved[0]
-            if ahead < len(line):
-                line[ahead][0].halve(line[ahead][1])
-                halved[0] += 1
-            if closed[0] < ahead:
-                line[closed[0]][0].close(line[closed[0]][1])
-                closed[0] += 1
+
+            def middle():
+                if 0 <= at - 3 < len(line):
+                    line[at - 3].pass_other()
+                if 0 <= at - 2 < len(line):
+                    line[at - 2].pass_kept()
+                if 0 <= at - 1 < len(line):
+                    line[at - 1].sum_line()
+                if at < len(line):
+                    line[at].sum_chip_pair(at)
+
+            when(is_mid, middle)
+            served[0] += 1
+            lead()
 
     slab_ids = range(slabs)
     for q in slab_ids:
@@ -1355,121 +1380,102 @@
         x_gather.after_x(q)
     cot_route.take(0)
     cot_gather.begin(0)
+    cot_route.hand_out(1)
+    mlp_fetch[0].share()
     for q in slab_ids:
         x_gather.after_far(q)
-    cot_route.hand_out(1)
+    cot_route.take(1)
+    cot_gather.begin(1)
+    mlp_fetch[1].begin()
+    cot_gather.after_y(0)
+    cot_gather.after_x(0)
+    cot_gather.after_y(1)
+    cot_gather.after_x(1)
     for q in slab_ids:
         x_gather.end(q)
     for copy in norm_copies:
         copy().wait_recv()
-    when(is_mid, norm_stage)
-    cot_route.take(1)
-    cot_gather.begin(1)
-    cot_gather.after_y(0)
-    cot_gather.after_x(0)
-    when(is_edge, norm_stage)
-    cot_gather.after_y(1)
-    mlp_fetch[1].begin()
-    cot_gather.after_x(1)
+    mlp_fetch[1].share()
+    norm_stage()
     for q in slab_ids:
         cot_gather.after_far(q)
+    mlp_fetch[2].begin()
     for q in slab_ids:
         cot_gather.end(q)
     mlp_fetch[0].end()
-    mlp_fetch[2].begin()
     mlp_stage(0)
-    queue(mlp_units[0], near)
-    lead()
+    queue(mlp_units[0])
+    mlp_fetch[2].share()
+    attn_fetch.begin()
     mlp_fetch[1].end()
-    mlp_fetch[3].begin()
     mlp_stage(1)
-    queue(mlp_units[1], near)
+    queue(mlp_units[1])
     serve(1)
     mlp_fetch[2].end()
-    attn_fetch.begin()
     mlp_stage(2)
-    queue(mlp_units[2], near)
+    mlp_fetch[3].begin()
+    queue(mlp_units[2])
     serve(2)
+    attn_fetch.end()
+    attention_slab(0)
+    serve(1)
+    attention_slab(1)
+    serve(1)
+    attention_slab(2)
+    serve(1)
+    attention_slab(3)
+    queue(attn_units)
+    serve(1)
     mlp_fetch[3].end()
     mlp_stage(3)
-    queue(mlp_units[3], near)
-    serve(4)
-    attn_fetch.end()
-    cross(2)
-    attention_slab(0)
+    queue(mlp_units[3])
     serve(1)
-    cross(1)
-    queue(mlp_units[0], far)
-    attention_slab(1)
+    out_stage(0)
+    out_stage(1)
     serve(1)
-    cross(1)
-    queue(mlp_units[1][:1], far)
-    attention_slab(2)
+    out_stage(2)
+    out_stage(3)
+    out_scatter.begin()
     serve(1)
-    cross(1)
-    attention_slab(3)
-    queue(attn_units, near)
-    serve(1)
-    cross(1)
-    for n in range(4):
-        out_stage(n)
-        if n % 2:
-            serve(1)
-            cross(1)
-    out_scatter.begin()
-    queue(mlp_units[1][1:] + mlp_units[2], far)
     dx_stage(0)
     out_scatter.second()
     dx_stage(1)
     serve(1)
-    cross(1)
     dx_stage(2)
+    dx_stage(3)
     serve(1)
-    dx_stage(3)
+    small_begin()
+    out_scatter.third()
     dx_scatter.begin()
-    small_begin()
+    small_second()
     serve(1)
-    cross(1)
-    small_second()
-    queue(mlp_units[3], far)
-    serve(1)
-    out_scatter.third()
-    cross(1)
+    finish_output()
+    out_route.begin(0)
     dx_scatter.second()
-    serve(1)
     small_third()
     serve(1)
-    cross(1)
-    queue(attn_units, far)
-    finish_output()
-    out_route.begin(0)
-    serve(1)
-    cross(1)
-    small_halve()
     out_route.relay(0)
     out_route.begin(1)
+    small_halve()
+    serve(1)
+    out_route.relay(1)
+    out_route.hand_out(0)
+    serve(1)
+    small_close()
     dx_scatter.third()
     serve(1)
-    cross(1)
-    small_close()
-    out_route.relay(1)
-    serve(1)
-    cross(4)
-    out_route.hand_out(0)
+    out_route.hand_out(1)
     serve(1)
     sum_grad()
-    out_route.hand_out(1)
-    serve(1)
+    serve(1, True)
     out_route.take(0)
     finish_grad()
-    serve(1)
+    serve(1, True)
     out_route.take(1)
-    while closed[0] < len(line):
-        serve(1)
-    for at, (unit, which) in enumerate(line):
-        unit.finish(which, at >= len(line) - flight)
-    for unit in crossing[len(crossing) - flight :]:
-        unit.sent_far()
+    while served[0] < len(line) + 3:
+        serve(1, True)
+    for at, unit in enumerate(line):
+        unit.finish(at >= len(line) - flight)
     small_finish()
     cot_route.finish()
     out_route.finish()
@@ -1570,7 +1576,7 @@
         + [low(4, 4, slab, feats)] * 2
         + [low(rows, D)] * 2
         + [first, second, low(rows, second_rows), low(rows, first_cols)]
-        + [first, second] * 5
+        + [first, second]
         + scatter
         + [item]
         + scatter
@@ -1580,6 +1586,7 @@
     vmem = pl.BlockSpec(memory_space=pltpu.VMEM)
     smem = pl.BlockSpec(memory_space=pltpu.SMEM)
     copies = 250
+    first_units, second_units = first_cols // UNIT, second_rows // UNIT
     results = pl.pallas_call(
         layer_kernel,
         in_specs=[smem] * 2 + [any_space] * 2 + [vmem] * 5 + [any_space] * 4,
@@ -1588,7 +1595,12 @@
         scratch_shapes=[
             pltpu.VMEM((4, UNIT + qkv_here, feats), F32),
             pltpu.VMEM((4, 8, feats), F32),
-            pltpu.VMEM((4, D, 128), F32),
+            pltpu.VMEM((first_units, 4, feats, UNIT), BF16),
+            pltpu.VMEM((second_units, 4, UNIT, feats), BF16),
+            pltpu.VMEM((first_units, 4, feats // 2, UNIT), BF16),
+            pltpu.VMEM((second_units, 4, UNIT // 2, feats), BF16),
+            pltpu.VMEM((2, 4, feats, UNIT), BF16),
+            pltpu.VMEM((2, 4, UNIT, feats), BF16),
             pltpu.VMEM((8, qkv_here), F32),
             pltpu.VMEM((8, first_cols), F32),
             pltpu.VMEM((4, 8, feats), F32),
@@ -1603,7 +1615,7 @@
             pltpu.VMEM((4, 2, 8, slab), F32),
             pltpu.SemaphoreType.DMA((copies,)),
             pltpu.SemaphoreType.DMA((copies,)),
-            pltpu.SemaphoreType.DMA((32,)),
+            pltpu.SemaphoreType.DMA((96,)),
         ],
         compiler_params=pltpu.CompilerParams(
             collective_id=0, has_side_effects=True, vmem_limit_bytes=60 * 1024 * 1024

time: 673 us -> 608 us (0.903)
  Pallas kernels: 642 us -> 578 us
    pallas_call x1, Pallas kernels: 632 us -> 568 us  [dealt_layer(): pl.pallas_call(layer_kernel, in_specs=[smem] * 2 + [any_space] * 2 + [vme...]
where the time goes in v4:
time: 608 us; the launch traced here: 597 us
  Pallas kernels  578 us (95%)
  local copies, waits for them, and re-layouts  16.7 us (3%)
    pallas_call x1, Pallas kernels, dealt_layer(): pl.pallas_call(layer_kernel, in_specs=[smem] * 2 + [any_space] * 2 + [vme...  568 us

profile of v4, /device:TPU:0, one launch (start us, length us, event | category | flops | bytes accessed | tf_op | source)
XLA Modules:
  0.0 596.9 jit_solution(3088726445442620222)
XLA Ops:
  0.6 1.3 add.3
  1.9 1.4 copy.31.lengths
  3.3 1.4 stack.23.norm_own
  4.7 1.2 jit_solution_.3.turns
  6.0 567.7 %shard_map.272 = (bf16[4,512,1792]{2,1,0:T(8,128)(2,1)}, bf16[4,1280,512]{2,1,0:T(8,128)(2,1)}, bf16[2,512,512]{2,1,0:T(8,128)(2,1)}, f32[2,512,512]{2,1,0:T(8,1...) custom-call(s32[16,4]{1,0:T(8,128)} %copy.31.lengths, ...), custom_call_target="tpu_custom_call" | custom-call | flops 77309411328 | bytes 209715200 | tf_op jit(solution)/shard_map/pallas_call | solution.py:1590
  573.6 1.5 fusion
  575.1 0.0 copy-start.4
  575.1 0.7 slice.30
  575.9 0.8 slice_bitcast_fusion
  576.6 0.6 copy.34
  577.2 0.6 reshape.62
  577.9 0.0 copy-start
  577.9 2.5 copy-done
  580.3 0.0 copy-start.1
  580.3 3.1 copy-done.1
  583.4 0.0 copy-start.3
  583.4 0.0 copy-start.2
  583.4 10.2 %shard_map.273 = (f32[512,3072]{1,0:T(8,128)}, f32[512,4096]{1,0:T(8,128)}, f32[1024,512]{1,0:T(8,128)}, f32[4096,512]{1,0:T(8,128)}) custom-call(bf16[4,512,1792]{2,1,0:T(8,128)(2,1)S(1)} %copy-done.1, bf16[4,1280,512]{2,1,0:T(8,128)(2,1)S(1)} %copy-done, bf16[4,1280,512]{2,1,0:T(8,128)(2,1)S(1)} %copy-done), custom_call_target="tpu_custom_call" | custom-call | tf_op jit(solution)/shard_map/pallas_call | solution.py:1500
  593.6 0.0 copy-done.4
  593.6 0.6 copy.38
  594.2 0.0 copy-done.3
  594.2 1.0 copy.39
  595.2 0.0 copy-done.2
  595.2 1.3 copy.40
Async XLA Ops:
  575.1 18.5 %copy-start.4 = (f32[1,512]{1,0:T(1,128)}, f32[1,512]{1,0:T(1,128)S(1)}, u32[]{:S(2)}) copy-start(f32[1,512]{1,0:T(1,128)S(1)} %get-tuple-element.34) | copy-start | bytes 6148
  577.9 2.5 copy-start
  580.3 3.1 copy-start.1
  583.4 10.8 %copy-start.3 = (bf16[2,512,512]{2,1,0:T(8,128)(2,1)S(1)}, bf16[2,512,512]{2,1,0:T(8,128)(2,1)}, u32[]{:S(2)}) copy-start(bf16[2,512,512]{2,1,0:T(8,128)(2,1)} %get-tuple-element.23) | copy-start | bytes 3145732
  583.4 11.7 %copy-start.2 = (f32[2,512,512]{2,1,0:T(8,128)S(1)}, f32[2,512,512]{2,1,0:T(8,128)}, u32[]{:S(2)}) copy-start(f32[2,512,512]{2,1,0:T(8,128)} %get-tuple-element.24) | copy-start | bytes 6291460

commit v5 on v4

--- a/solution.py
+++ b/solution.py
@@ -724,6 +724,8 @@
             self.kept = [local(*pair) for pair in self.kept]
 
         def share(self):
+            if not self.paired:
+                return
             for copy, onward in zip(self.over, self.shared):
                 copy().wait_recv()
                 start(onward)
@@ -736,7 +738,7 @@
 
     attn_fetch = Fetch(False, qkv_w, 0, qkv_here, 0, dense_w, 0, attn_here, 0)
     mlp_fetch = [
-        Fetch(at < 3 * UNIT, fc1_w, at, hidden_here, qkv_here + at, fc2_w, at, hidden_here, attn_here + at)
+        Fetch(at < 2 * UNIT, fc1_w, at, hidden_here, qkv_here + at, fc2_w, at, hidden_here, attn_here + at)
         for at in range(0, hidden_here, UNIT)
     ]
 
@@ -1443,10 +1445,10 @@
     serve(1)
     dx_stage(2)
     dx_stage(3)
+    dx_scatter.begin()
     serve(1)
     small_begin()
     out_scatter.third()
-    dx_scatter.begin()
     small_second()
     serve(1)
     finish_output()

time: 608 us -> 595 us (0.979)
  the two profiles are of different devices: /device:TPU:0 before, /device:TPU:3 now
where the time goes in v5:
time: 595 us; the launch traced here: 584 us
  Pallas kernels  565 us (95%)
  local copies, waits for them, and re-layouts  16.7 us (3%)
    pallas_call x1, Pallas kernels, dealt_layer(): pl.pallas_call(layer_kernel, in_specs=[smem] * 2 + [any_space] * 2 + [vme...  555 us

profile of v5, /device:TPU:3, one launch (start us, length us, event | category | flops | bytes accessed | tf_op | source)
XLA Modules:
  0.0 583.9 jit_solution(13777640398133453366)
XLA Ops:
  0.6 1.3 add.3
  1.9 1.4 copy.31.lengths
  3.3 1.4 stack.23.norm_own
  4.7 1.2 jit_solution_.3.turns
  6.0 554.6 %shard_map.272 = (bf16[4,512,1792]{2,1,0:T(8,128)(2,1)}, bf16[4,1280,512]{2,1,0:T(8,128)(2,1)}, bf16[2,512,512]{2,1,0:T(8,128)(2,1)}, f32[2,512,512]{2,1,0:T(8,1...) custom-call(s32[16,4]{1,0:T(8,128)} %copy.31.lengths, ...), custom_call_target="tpu_custom_call" | custom-call | flops 77309411328 | bytes 209715200 | tf_op jit(solution)/shard_map/pallas_call | solution.py:1592
  560.6 1.5 fusion
  562.1 0.0 copy-start.4
  562.1 0.7 slice.30
  562.8 0.8 slice_bitcast_fusion
  563.6 0.6 copy.34
  564.2 0.6 reshape.62
  564.8 0.0 copy-start
  564.8 2.5 copy-done
  567.3 0.0 copy-start.1
  567.3 3.1 copy-done.1
  570.4 0.0 copy-start.3
  570.4 0.0 copy-start.2
  570.4 10.2 %shard_map.273 = (f32[512,3072]{1,0:T(8,128)}, f32[512,4096]{1,0:T(8,128)}, f32[1024,512]{1,0:T(8,128)}, f32[4096,512]{1,0:T(8,128)}) custom-call(bf16[4,512,1792]{2,1,0:T(8,128)(2,1)S(1)} %copy-done.1, bf16[4,1280,512]{2,1,0:T(8,128)(2,1)S(1)} %copy-done, bf16[4,1280,512]{2,1,0:T(8,128)(2,1)S(1)} %copy-done), custom_call_target="tpu_custom_call" | custom-call | tf_op jit(solution)/shard_map/pallas_call | solution.py:1502
  580.6 0.0 copy-done.4
  580.6 0.6 copy.38
  581.1 0.0 copy-done.3
  581.1 1.0 copy.39
  582.1 0.0 copy-done.2
  582.1 1.3 copy.40
Async XLA Ops:
  562.1 18.5 %copy-start.4 = (f32[1,512]{1,0:T(1,128)}, f32[1,512]{1,0:T(1,128)S(1)}, u32[]{:S(2)}) copy-start(f32[1,512]{1,0:T(1,128)S(1)} %get-tuple-element.34) | copy-start | bytes 6148
  564.8 2.5 copy-start
  567.3 3.1 copy-start.1
  570.4 10.8 %copy-start.3 = (bf16[2,512,512]{2,1,0:T(8,128)(2,1)S(1)}, bf16[2,512,512]{2,1,0:T(8,128)(2,1)}, u32[]{:S(2)}) copy-start(bf16[2,512,512]{2,1,0:T(8,128)(2,1)} %get-tuple-element.23) | copy-start | bytes 3145732
  570.4 11.7 %copy-start.2 = (f32[2,512,512]{2,1,0:T(8,128)S(1)}, f32[2,512,512]{2,1,0:T(8,128)}, u32[]{:S(2)}) copy-start(f32[2,512,512]{2,1,0:T(8,128)} %get-tuple-element.24) | copy-start | bytes 6291460

commit v6 on v5

--- a/solution.py
+++ b/solution.py
@@ -1448,6 +1448,7 @@
     dx_scatter.begin()
     serve(1)
     small_begin()
+    serve(1)
     out_scatter.third()
     small_second()
     serve(1)

time: 595 us -> 596 us (level)
  the two profiles are of different devices: /device:TPU:3 before, /device:TPU:0 now
where the time goes in v6:
time: 596 us; the launch traced here: 584 us
  Pallas kernels  565 us (95%)
  local copies, waits for them, and re-layouts  16.7 us (3%)
    pallas_call x1, Pallas kernels, dealt_layer(): pl.pallas_call(layer_kernel, in_specs=[smem] * 2 + [any_space] * 2 + [vme...  555 us

profile of v6, /device:TPU:0, one launch (start us, length us, event | category | flops | bytes accessed | tf_op | source)
XLA Modules:
  0.0 583.8 jit_solution(7171085656136940021)
XLA Ops:
  0.6 1.3 add.3
  1.9 1.4 copy.31.lengths
  3.3 1.4 stack.23.norm_own
  4.7 1.2 jit_solution_.3.turns
  6.0 554.5 %shard_map.272 = (bf16[4,512,1792]{2,1,0:T(8,128)(2,1)}, bf16[4,1280,512]{2,1,0:T(8,128)(2,1)}, bf16[2,512,512]{2,1,0:T(8,128)(2,1)}, f32[2,512,512]{2,1,0:T(8,1...) custom-call(s32[16,4]{1,0:T(8,128)} %copy.31.lengths, ...), custom_call_target="tpu_custom_call" | custom-call | flops 77309411328 | bytes 209715200 | tf_op jit(solution)/shard_map/pallas_call | solution.py:1593
  560.5 1.5 fusion
  562.0 0.0 copy-start.4
  562.0 0.7 slice.30
  562.7 0.8 slice_bitcast_fusion
  563.5 0.6 copy.34
  564.1 0.6 reshape.62
  564.7 0.0 copy-start
  564.7 2.5 copy-done
  567.2 0.0 copy-start.1
  567.2 3.1 copy-done.1
  570.3 0.0 copy-start.3
  570.3 0.0 copy-start.2
  570.3 10.2 %shard_map.273 = (f32[512,3072]{1,0:T(8,128)}, f32[512,4096]{1,0:T(8,128)}, f32[1024,512]{1,0:T(8,128)}, f32[4096,512]{1,0:T(8,128)}) custom-call(bf16[4,512,1792]{2,1,0:T(8,128)(2,1)S(1)} %copy-done.1, bf16[4,1280,512]{2,1,0:T(8,128)(2,1)S(1)} %copy-done, bf16[4,1280,512]{2,1,0:T(8,128)(2,1)S(1)} %copy-done), custom_call_target="tpu_custom_call" | custom-call | tf_op jit(solution)/shard_map/pallas_call | solution.py:1503
  580.4 0.0 copy-done.4
  580.4 0.6 copy.38
  581.0 0.0 copy-done.3
  581.0 1.0 copy.39
  582.0 0.0 copy-done.2
  582.0 1.3 copy.40
Async XLA Ops:
  562.0 18.5 %copy-start.4 = (f32[1,512]{1,0:T(1,128)}, f32[1,512]{1,0:T(1,128)S(1)}, u32[]{:S(2)}) copy-start(f32[1,512]{1,0:T(1,128)S(1)} %get-tuple-element.34) | copy-start | bytes 6148
  564.7 2.5 copy-start
  567.2 3.1 copy-start.1
  570.3 10.8 %copy-start.3 = (bf16[2,512,512]{2,1,0:T(8,128)(2,1)S(1)}, bf16[2,512,512]{2,1,0:T(8,128)(2,1)}, u32[]{:S(2)}) copy-start(bf16[2,512,512]{2,1,0:T(8,128)(2,1)} %get-tuple-element.23) | copy-start | bytes 3145732
  570.3 11.7 %copy-start.2 = (f32[2,512,512]{2,1,0:T(8,128)S(1)}, f32[2,512,512]{2,1,0:T(8,128)}, u32[]{:S(2)}) copy-start(f32[2,512,512]{2,1,0:T(8,128)} %get-tuple-element.24) | copy-start | bytes 6291460
